TPU v7x, 512 devices: a whole 4x8x8 slice. The times are simulated.
512 devices in a mesh: node: 16 (over y, core), local: 8 (over z), section: 4 (over x).
Axes of the slice: x: 4, y: 8, z: 8, core: 2. Of those that a mesh axis runs over, the one named last changes fastest.
Arguments:
- inputs_b: bfloat16 [4, 2048, 4096], P('section', 'node', 'local'), may hold values from -6 to 6
- grads_a: bfloat16 [4, 2048, 4096], P('section', 'node', 'local'), may hold values from -6 to 6
- experts_a: int32 [4, 2048, 4], P('section', 'node'), may hold values from 0 to 15, all different within a row; in each aligned block of 128 rows (0 to 127, 128 to 255, ..., all dimensions but the last counted through in order) at most 40 rows name the same one
- experts_b: int32 [4, 2048, 4], P('section', 'node'), may hold values from 0 to 15, all different within a row; in each aligned block of 128 rows (0 to 127, 128 to 255, ..., all dimensions but the last counted through in order) at most 40 rows name the same one
- gates_a: float32 [4, 2048, 4], P('section', 'node'), may hold values from 0.05 to 0.5
- gates_b: float32 [4, 2048, 4], P('section', 'node'), may hold values from 0.05 to 0.5
- w_gate_up: bfloat16 [4, 16, 4096, 2, 1024], P('section', 'node', 'local'), may hold values from -0.09375 to 0.09375
- w_down: bfloat16 [4, 16, 1024, 4096], P('section', 'node', None, 'local'), may hold values from -0.1875 to 0.1875
- saved_a: bfloat16 [4, 16, 2, 1024, 640], P('section', 'node', None, 'local'), may hold values from -5 to 5
Outputs:
- outputs_b: bfloat16 [4, 2048, 4096], P('section', 'node', 'local')
- grads_prev: bfloat16 [4, 2048, 4096], P('section', 'node', 'local')
Inputs may be any that keep to these rules, and one draw needn't show every extreme that they name: `experts_a`: each row names 4 distinct experts. Among the 128 rows of one source block of a section, no expert is named by more than 40 rows, and in some blocks an expert is named by exactly 40. `experts_b`: each row names 4 distinct experts. Among the 128 rows of one source block of a section, no expert is named by more than 40 rows, and in some blocks an expert is named by exactly 40.
All inputs are finite; a program needn't handle non-finite values.
Results may differ from a plain program's by a relative error of at most 0.029.
Values may be sent and summed in bfloat16 or wider, within the bound.
No kernel may reach another device: no remote copies, remote signals or barrier semaphores. Data moves between devices by JAX's collectives and lax.ppermute only.
A program may use at most 64 MiB of HBM per device.

v0:
```python
import jax
import jax.numpy as jnp
from jax import lax
from jax.sharding import PartitionSpec as P

TOPK = 4


def shifted(value, axis, steps):
    count = lax.axis_size(axis)
    first, last = (max(0, -steps), min(count, count - steps))
    return lax.ppermute(value, axis, [(source, source + steps) for source in range(first, last)])


def slot_layout(ids_block, expert_total, slot_count):
    flat = ids_block.reshape(-1)
    count = flat.shape[0]
    onehot = (flat[:, None] == jnp.arange(expert_total, dtype=jnp.int32)[None, :]).astype(jnp.int32)
    before = jnp.cumsum(onehot, axis=0) - onehot
    position = jnp.sum(before * onehot, axis=1)
    keep = position < slot_count
    table = jnp.full((expert_total, slot_count), -1, jnp.int32)
    table = table.at[flat, position].set(jnp.arange(count, dtype=jnp.int32), mode="drop")
    return (flat, position, keep, table)


def gather_sum(returned, flat, position, weight, slot_count):
    width = returned.shape[-1]
    index_rows = flat * slot_count + jnp.minimum(position, slot_count - 1)
    picked = returned.reshape(-1, width)[index_rows]
    total = (picked.astype(jnp.float32) * weight[:, None]).reshape(-1, TOPK, width)
    return jnp.sum(total, axis=1).astype(jnp.bfloat16)


def body(inputs_b, grads_a, experts_a, experts_b, gates_a, gates_b, w_gate_up, w_down, saved_a):
    node_count = lax.axis_size("node")
    weights_in = w_gate_up[0, 0]
    weights_out = w_down[0, 0]
    saved = saved_a[0, 0]
    feature_cols = weights_out.shape[1]
    slot_total = saved.shape[2]
    slot_count = slot_total // node_count
    flat, position, keep, table = slot_layout(experts_b[0], node_count, slot_count)
    valid = table >= 0
    assign = jnp.maximum(table, 0)
    outgoing = jnp.where(valid[..., None], inputs_b[0][assign // TOPK], jnp.zeros((), jnp.bfloat16))
    weight = jnp.where(keep, gates_b[0].reshape(-1), 0.0)
    prepare_flat, prepare_position, keep, table = slot_layout(experts_a[0], node_count, slot_count)
    valid = table >= 0
    assign = jnp.maximum(table, 0)
    gate_slot = gates_a[0].reshape(-1)[assign]
    scaled = (grads_a[0][assign // TOPK].astype(jnp.float32) * gate_slot[..., None]).astype(
        jnp.bfloat16
    )
    prepare_outgoing = jnp.where(valid[..., None], scaled, jnp.zeros((), jnp.bfloat16))
    prepare_weight = jnp.where(keep, 1.0, 0.0).astype(jnp.float32)
    arrived_b = lax.all_to_all(outgoing, "node", split_axis=0, concat_axis=0, tiled=True)
    rows_b = arrived_b.reshape(-1, feature_cols)
    w_part = weights_in
    shared = lax.psum_scatter(
        jnp.einsum("rd,dgf->fgr", rows_b, w_part, preferred_element_type=jnp.float32).astype(
            jnp.bfloat16
        ),
        "local",
        scatter_dimension=0,
        tiled=True,
    ).astype(jnp.float32)
    hidden = (jax.nn.silu(shared[:, 0]) * shared[:, 1]).astype(jnp.bfloat16)
    w_part = weights_out
    result_b = (
        lax.dot_general(
            lax.all_gather(hidden, "local", axis=0, tiled=True),
            w_part,
            (((0,), (0,)), ((), ())),
            preferred_element_type=jnp.float32,
        )
        .astype(jnp.bfloat16)
        .reshape(arrived_b.shape)
    )
    returned_b = lax.all_to_all(result_b, "node", split_axis=0, concat_axis=0, tiled=True)
    arrived_a = lax.all_to_all(prepare_outgoing, "node", split_axis=0, concat_axis=0, tiled=True)
    rows_a = arrived_a.reshape(-1, feature_cols)
    w_part = weights_out
    grad_hidden = lax.psum_scatter(
        lax.dot_general(
            w_part, rows_a, (((1,), (1,)), ((), ())), preferred_element_type=jnp.float32
        ).astype(jnp.bfloat16),
        "local",
        scatter_dimension=0,
        tiled=True,
    ).astype(jnp.float32)
    gate_pre = saved[0].astype(jnp.float32)
    up_pre = saved[1].astype(jnp.float32)
    sigma = jax.nn.sigmoid(gate_pre)
    slope = sigma * (1.0 + gate_pre * (1.0 - sigma))
    d_pre = jnp.stack(
        [grad_hidden * up_pre * slope, grad_hidden * gate_pre * sigma], axis=0
    ).astype(jnp.bfloat16)
    w_part = weights_in
    result_a = (
        jnp.einsum(
            "gnr,dgn->rd",
            lax.all_gather(d_pre, "local", axis=1, tiled=True),
            w_part,
            preferred_element_type=jnp.float32,
        )
        .astype(jnp.bfloat16)
        .reshape(arrived_a.shape)
    )
    returned_a = lax.all_to_all(result_a, "node", split_axis=0, concat_axis=0, tiled=True)
    outputs = gather_sum(returned_b, flat, position, weight, slot_count)
    input_grad = gather_sum(returned_a, prepare_flat, prepare_position, prepare_weight, slot_count)
    grads_prev = shifted(input_grad[None], "section", -1)
    return (outputs[None], grads_prev)


def solution(mesh):
    return jax.shard_map(
        body,
        mesh=mesh,
        in_specs=(
            P("section", "node", "local"),
            P("section", "node", "local"),
            P("section", "node", None),
            P("section", "node", None),
            P("section", "node", None),
            P("section", "node", None),
            P("section", "node", "local", None, None),
            P("section", "node", None, "local"),
            P("section", "node", None, "local", None),
        ),
        out_specs=(P("section", "node", "local"), P("section", "node", "local")),
        check_vma=False,
    )
```

profile of v0, /device:TPU:1, one launch (start us, length us, event | category | flops | bytes accessed | tf_op | source)
XLA Modules:
  0.0 328.0 jit_solution(5999399579988695973)
XLA Ops:
  7.2 0.9 copy.36
  8.1 0.1 eq.58
  8.2 0.1 eq.62
  8.3 0.1 reshape_squeeze.14
  8.5 1.2 reduce-window.16
  9.6 0.2 slice_reduce_fusion
  9.9 0.1 fusion.29
  10.0 0.6 compare_select_fusion.2
  10.6 25.3 %scatter_fusion.1 = s32[16,40]{1,0:T(8,128)S(1)} fusion(s32[16,40]{1,0:T(8,128)S(1)} %broadcast.216.clone.1, s32[512]{0:T(512)S(1)} %bitcast.121, s32[512]{0:T(512)S(1)} %iota.20), kind=kCustom, calls=%fused_computation.6 | custom fusion | bytes 10240 | tf_op jit(solution)/shard_map/scatter | solution.py:23
  36.0 0.1 copy.40
  36.1 0.1 reshape_squeeze.15
  36.2 0.1 reshape.300
  36.4 4.3 %gather_fusion.3 = f32[640]{0:T(1024)S(1)} fusion(f32[512]{0:T(512)S(1)} %reshape_squeeze.15, s32[1024]{0:T(1024)S(1)} %pad_clamp_fusion.1), kind=kCustom, calls=%fused_computation.3 | custom fusion | bytes 7680 | tf_op jit(solution)/shard_map/gather | solution.py:51
  40.8 2.8 gather_fusion.2
  43.6 1.1 fusion.13
  44.7 10.3 %all-to-all-start.2 = ((bf16[16,40,512]{2,1,0:T(8,128)(2,1)}), bf16[16,40,512]{2,1,0:T(8,128)(2,1)S(1)}, u32[]{:S(2)}, u32[]{:S(2)}) async-start(bf16[16,40,512]{2,1,0:T(8,128)(2,1)} %fusion.13), calls=%async_computation.2 | async-start | bytes 1310720 | tf_op jit(solution)/shard_map/all_to_all | solution.py:81
  55.0 0.1 copy.30
  55.1 0.1 eq.50
  55.2 0.1 eq.54
  55.3 0.1 reshape_squeeze.12
  55.4 1.2 reduce-window.14
  56.6 0.2 slice_reduce_fusion.1
  56.8 0.1 fusion.32
  56.9 18.0 %all-to-all-done.2 = bf16[16,40,512]{2,1,0:T(8,128)(2,1)S(1)} async-done(((bf16[16,40,512]{2,1,0:T(8,128)(2,1)}), bf16[16,40,512]{2,1,0:T(8,128)(2,1)S(1)}, u32[]{:S(2)}, u32[]{:S(2)}) %all-to-all-start.2) | async-done | bytes 655392 | tf_op jit(solution)/shard_map/all_to_all | solution.py:81
  75.0 0.8 copy-done.3
  75.8 2.3 fusion.3
  78.1 1.5 copy.46
  79.6 0.6 compare_select_fusion.5
  80.2 25.3 %scatter_fusion = s32[16,40]{1,0:T(8,128)S(1)} fusion(s32[16,40]{1,0:T(8,128)S(1)} %broadcast.216.clone, s32[512]{0:T(512)S(1)} %bitcast.120, s32[512]{0:T(512)S(1)} %iota.19), kind=kCustom, calls=%fused_computation.5 | custom fusion | bytes 10240 | tf_op jit(solution)/shard_map/scatter | solution.py:23
  105.7 2.8 gather_fusion
  108.5 0.2 broadcast_select_fusion
  108.6 23.1 %all_to_all.20 = bf16[16,40,512]{2,1,0:T(8,128)(2,1)S(1)} all-to-all(bf16[16,40,512]{2,1,0:T(8,128)(2,1)S(1)} %broadcast_select_fusion), channel_id=1, replica_groups=mesh['node'=16,'local'=8,'section'=4] {'node'}, dimensions={0} | all-to-all | bytes 1310720 | tf_op jit(solution)/shard_map/all_to_all | solution.py:57
  131.7 3.1 convolution_convert_fusion
  134.8 4.4 %copy.48 = bf16[1024,1280]{1,0:T(8,128)(2,1)} copy(bf16[1024,1280]{0,1:T(8,128)(2,1)} %bitcast.122) | data formatting | bytes 5242880
  139.3 0.9 copy-done.4
  140.2 0.2 copy.51
  140.4 0.2 copy.50
  140.6 1.1 copy.47
  141.6 0.2 fusion.26
  141.8 0.8 pad_maximum_fusion
  142.7 38.2 %reduce-scatter.7.cloned.1.call-done = bf16[128,1280]{1,0:T(8,128)(2,1)} async-done(((bf16[1024,1280]{1,0:T(8,128)(2,1)}), bf16[128,1280]{1,0:T(8,128)(2,1)}) %reduce-scatter.7.cloned.1.call-update) | async-done | bytes 327696
  180.9 1.2 copy.49
  182.2 0.8 fusion.24
  182.9 53.3 %all-gather.5.cloned.1.call-done = bf16[2,1024,640]{1,2,0:T(8,128)(2,1)} async-done(((bf16[2,128,640]{1,2,0:T(8,128)(2,1)}), bf16[2,1024,640]{1,2,0:T(8,128)(2,1)}) %all-gather.5.cloned.1.call-update) | async-done | bytes 2621456 | tf_op jit(solution)/shard_map/all_gather | solution.py:103
  236.2 4.1 %fusion.7 = bf16[640,512]{1,0:T(8,128)(2,1)} fusion(bf16[2,1024,640]{1,2,0:T(8,128)(2,1)} %all-gather.5.cloned.1.call-done, bf16[512,2,1024]{2,1,0:T(2,128)(2,1)S(1)} %bitcast.115), kind=kOutput, calls=%fused_computation.14 | convolution fusion | flops 1342504960 | bytes 5373952 | tf_op jit(solution)/shard_map/gnr,dgn->rd/dot_general | solution.py:101
  240.3 10.9 %all-to-all-start.3 = ((bf16[16,40,512]{2,1,0:T(8,128)(2,1)}), bf16[16,40,512]{2,1,0:T(8,128)(2,1)S(1)}, u32[]{:S(2)}, u32[]{:S(2)}) async-start(bf16[16,40,512]{2,1,0:T(8,128)(2,1)} %bitcast.30), calls=%async_computation.3 | async-start | bytes 1310720 | tf_op jit(solution)/shard_map/all_to_all | solution.py:110
  251.2 29.9 %all-gather.3.cloned.1.call-done = bf16[1024,640]{0,1:T(8,128)(2,1)} async-done(((bf16[128,640]{0,1:T(8,128)(2,1)}), bf16[1024,640]{0,1:T(8,128)(2,1)}) %all-gather.3.cloned.1.call-update) | async-done | bytes 1310736 | tf_op jit(solution)/shard_map/all_gather | solution.py:72
  281.1 3.3 %convolution_convert_fusion.2 = bf16[640,512]{1,0:T(8,128)(2,1)} fusion(bf16[1024,640]{0,1:T(8,128)(2,1)} %all-gather.3.cloned.1.call-done, bf16[1,1,1024,512]{3,2,1,0:T(8,128)(2,1)} %param.16), kind=kOutput, calls=%fused_computation.15 | convolution fusion | flops 671416320 | bytes 3014656 | tf_op jit(solution)/shard_map/dot_general | solution.py:71
  284.5 11.0 %all-to-all-start.1 = ((bf16[16,40,512]{2,1,0:T(8,128)(2,1)}), bf16[16,40,512]{2,1,0:T(8,128)(2,1)S(1)}, u32[]{:S(2)}, u32[]{:S(2)}) async-start(bf16[16,40,512]{2,1,0:T(8,128)(2,1)} %bitcast.126), calls=%async_computation.1 | async-start | bytes 1310720 | tf_op jit(solution)/shard_map/all_to_all | solution.py:80
  295.5 0.1 lt.90
  295.6 0.1 copy.35
  295.7 0.6 compare_select_fusion.8
  296.3 0.8 select_n.115
  297.1 1.3 pad_clamp_fusion
  298.4 2.8 gather_fusion.4
  301.1 2.4 reshape.273
  303.5 1.9 multiply_reduce_fusion
  305.4 1.3 collective-permute-start
  306.8 5.6 %collective-permute-done = bf16[1,128,512]{2,1,0:T(8,128)(2,1)S(1)} collective-permute-done((bf16[1,128,512]{2,1,0:T(8,128)(2,1)S(1)}, bf16[1,128,512]{2,1,0:T(8,128)(2,1)S(1)}, u32[]{:S(2)}, u32[]{:S(2)}) %collective-permute-start) | collective-permute-done | bytes 131104 | tf_op jit(solution)/shard_map/ppermute | solution.py:12
  312.4 3.1 all-to-all-done.1
  315.5 2.6 gather_fusion.1
  318.1 1.4 reshape.270
  319.5 1.4 multiply_reduce_fusion.1
  320.8 0.7 copy.67
  (51 shorter events, 0.8 us)
Async XLA Ops:
  7.2 124.5 %copy-start = (bf16[1,1,512,2,1024]{4,3,2,1,0:T(2,128)(2,1)S(1)}, bf16[1,1,512,2,1024]{4,3,2,1,0:T(2,128)(2,1)}, u32[]{:S(2)}) copy-start(bf16[1,1,512,2,1024]{4,3,2,1,0:T(2,128)(2,1)} %param.15) | copy-start | bytes 6291460
  10.6 25.4 %copy-start.6 = (f32[1,128,4]{1,2,0:T(4,128)S(1)}, f32[1,128,4]{1,2,0:T(4,128)}, u32[]{:S(2)}) copy-start(f32[1,128,4]{1,2,0:T(4,128)} %param.13) | copy-start | bytes 6148
  36.3 4.4 %copy-start.1 = (bf16[1,128,512]{2,1,0:T(8,128)(2,1)S(1)}, bf16[1,128,512]{2,1,0:T(8,128)(2,1)}, u32[]{:S(2)}) copy-start(bf16[1,128,512]{2,1,0:T(8,128)(2,1)} %param.10) | copy-start | bytes 393220
  43.6 11.4 %copy-start.7 = (s32[1,128,4]{1,2,0:T(4,128)S(1)}, s32[1,128,4]{1,2,0:T(4,128)}, u32[]{:S(2)}) copy-start(s32[1,128,4]{1,2,0:T(4,128)} %param.12) | copy-start | bytes 6148
  44.7 30.3 %all-to-all-start.2 = ((bf16[16,40,512]{2,1,0:T(8,128)(2,1)}), bf16[16,40,512]{2,1,0:T(8,128)(2,1)S(1)}, u32[]{:S(2)}, u32[]{:S(2)}) async-start(bf16[16,40,512]{2,1,0:T(8,128)(2,1)} %fusion.13), calls=%async_computation.2 | async-start | bytes 1310720 | tf_op jit(solution)/shard_map/all_to_all | solution.py:81
  54.9 85.6 %reduce-scatter.9.cloned.1.call-start = ((), (), s32[]{:S(2)}) async-start(), calls=%async_computation.9 | async-start | bytes 1474560
  75.0 0.8 copy-start.3
  79.6 101.3 %reduce-scatter.7.cloned.1.call-start = ((), (), s32[]{:S(2)}) async-start(), calls=%async_computation.8 | async-start | bytes 2949120
  80.2 25.4 %copy-start.2 = (bf16[1,128,512]{2,1,0:T(8,128)(2,1)S(1)}, bf16[1,128,512]{2,1,0:T(8,128)(2,1)}, u32[]{:S(2)}) copy-start(bf16[1,128,512]{2,1,0:T(8,128)(2,1)} %param.9) | copy-start | bytes 393220
  139.2 1.0 copy-start.4
  139.2 97.0 %all-gather.5.cloned.1.call-start = ((), (), s32[]{:S(2)}) async-start(), calls=%async_computation.7 | async-start | bytes 2949120 | tf_op jit(solution)/shard_map/all_gather | solution.py:103
  142.6 138.5 %all-gather.3.cloned.1.call-start = ((), (), s32[]{:S(2)}) async-start(), calls=%async_computation.6 | async-start | bytes 1474560 | tf_op jit(solution)/shard_map/all_gather | solution.py:72
  240.3 44.1 %all-to-all-start.3 = ((bf16[16,40,512]{2,1,0:T(8,128)(2,1)}), bf16[16,40,512]{2,1,0:T(8,128)(2,1)S(1)}, u32[]{:S(2)}, u32[]{:S(2)}) async-start(bf16[16,40,512]{2,1,0:T(8,128)(2,1)} %bitcast.30), calls=%async_computation.3 | async-start | bytes 1310720 | tf_op jit(solution)/shard_map/all_to_all | solution.py:110
  251.2 44.4 %copy-start.8 = (f32[1,128,4]{1,2,0:T(4,128)S(1)}, f32[1,128,4]{1,2,0:T(4,128)}, u32[]{:S(2)}) copy-start(f32[1,128,4]{1,2,0:T(4,128)} %param.14) | copy-start | bytes 6148
  284.5 31.0 %all-to-all-start.1 = ((bf16[16,40,512]{2,1,0:T(8,128)(2,1)}), bf16[16,40,512]{2,1,0:T(8,128)(2,1)S(1)}, u32[]{:S(2)}, u32[]{:S(2)}) async-start(bf16[16,40,512]{2,1,0:T(8,128)(2,1)} %bitcast.126), calls=%async_computation.1 | async-start | bytes 1310720 | tf_op jit(solution)/shard_map/all_to_all | solution.py:80
  301.1 5.7 %copy-start.5 = (s32[512,1]{0,1:T(1,128)S(1)}, s32[512,1]{0,1:T(1,128)}, u32[]{:S(2)}) copy-start(s32[512,1]{0,1:T(1,128)} %get-tuple-element.10) | copy-start | bytes 6148
  305.4 7.0 %collective-permute-start = (bf16[1,128,512]{2,1,0:T(8,128)(2,1)S(1)}, bf16[1,128,512]{2,1,0:T(8,128)(2,1)S(1)}, u32[]{:S(2)}, u32[]{:S(2)}) collective-permute-start(bf16[1,128,512]{2,1,0:T(8,128)(2,1)S(1)} %bitcast.130), channel_id=1, source_target_pairs={{1,0},{2,1},{3,2},{5,4},{6,5},{7,6},{9,8},{10,9},{11,10},{13,12},{... | collective-permute-start | bytes 393224 | tf_op jit(solution)/shard_map/ppermute | solution.py:12
Sparse Core Ops, SparseCore 0:
  79.7 36.8 reduce-scatter.8
  139.3 41.5 reduce-scatter.6
  182.9 53.2 all-gather.4
  238.1 43.0 all-gather.2
where the time goes:
time: 329 us; the launch traced here: 328 us
  waiting for transfers between devices  148 us (45%)
  local copies, waits for them, and re-layouts  84.2 us (26%)
  starting transfers between devices  33.6 us (10%)
  blocking collectives  23.1 us (7%)
  between operations  14.1 us (4%)
  matrix products  12.9 us (4%)
  other arithmetic  12 us (4%)
    all_gather x1, waiting for transfers between devices, body(): lax.all_gather(d_pre, 'local', axis=1, tiled=True)  53.3 us
    scatter x2, local copies, waits for them, and re-layouts, slot_layout(): table.at[flat, position]  50.6 us
    unnamed x6, waiting for transfers between devices  38.3 us
    all_gather x1, waiting for transfers between devices, body(): lax.all_gather(hidden, 'local', axis=0, tiled=True)  29.9 us
    all_to_all x1, blocking collectives, body(): lax.all_to_all(outgoing, 'node', split_axis=0, concat_axis=0, tiled=True)  23.1 us
    all_to_all x1, waiting for transfers between devices, body(): lax.all_to_all(prepare_outgoing, 'node', split_axis=0, concat_axis=0, til...  18 us
    unnamed x29, local copies, waits for them, and re-layouts  12.1 us
    all_to_all x1, starting transfers between devices, body(): lax.all_to_all(result_b, 'node', split_axis=0, concat_axis=0, tiled=True)  11 us
  transfers between devices with their start and end apart: 8, of which 6 were waited for; matrix products, arithmetic and copies ran while one was open for 18% of the time, Pallas kernels for 0%

commit v1 on v0

v1 whole, which is shorter than its diff:
```python
import functools

import jax
import jax.numpy as jnp
from jax import lax
from jax.experimental import pallas as pl
from jax.experimental.pallas import tpu as pltpu
from jax.sharding import PartitionSpec as P

BF = jnp.bfloat16
F32 = jnp.float32
VMEM_LIMIT = 48 * 1024 * 1024


def call(kernel, outs, args, flops=0, grid=None, in_specs=None, out_specs=None, scratch=()):
    moved = sum(a.size * a.dtype.itemsize for a in args)
    moved += sum(o.size * o.dtype.itemsize for o in jax.tree.leaves(outs))
    extra = {}
    if grid is not None:
        extra = dict(grid=grid, in_specs=in_specs, out_specs=out_specs)
    return pl.pallas_call(
        kernel,
        out_shape=outs,
        scratch_shapes=scratch,
        compiler_params=pltpu.CompilerParams(vmem_limit_bytes=VMEM_LIMIT),
        cost_estimate=pl.CostEstimate(flops=flops, bytes_accessed=moved, transcendentals=0),
        **extra,
    )(*args)


def shape(dims, dtype=BF):
    return jax.ShapeDtypeStruct(dims, dtype)


def dot(a, b, ca, cb):
    return lax.dot_general(a, b, (((ca,), (cb,)), ((), ())), preferred_element_type=F32)


def slot_table(ids_ref, gates_ref, experts, cap):
    top, tokens = ids_ref.shape
    expert = lax.broadcasted_iota(jnp.int32, (experts, tokens), 0)
    named = jnp.zeros((experts, tokens), F32)
    gate = jnp.zeros((experts, tokens), F32)
    for k in range(top):
        hit = (ids_ref[k : k + 1, :] == expert).astype(F32)
        named = named + hit
        gate = gate + hit * gates_ref[k : k + 1, :]
    earlier = lax.broadcasted_iota(jnp.int32, (tokens, tokens), 0) < lax.broadcasted_iota(
        jnp.int32, (tokens, tokens), 1
    )
    position = dot(named.astype(BF), earlier.astype(F32).astype(BF), 1, 0)
    position = jnp.where(named > 0, position, -1.0)
    slot = lax.broadcasted_iota(jnp.int32, (cap, tokens), 0).astype(F32)
    rows, gated = [], []
    for e in range(experts):
        fill = (position[e : e + 1, :] == slot).astype(F32)
        rows.append(fill)
        gated.append(fill * gate[e : e + 1, :])
    return jnp.concatenate(rows, axis=0), jnp.concatenate(gated, axis=0)


def dispatch_kernel(experts, cap, gate_rows, ids_ref, gates_ref, x_ref, out_ref):
    rows, gated = slot_table(ids_ref, gates_ref, experts, cap)
    picked = dot(rows.astype(BF), x_ref[...], 1, 0)
    if gate_rows:
        picked = picked * jnp.sum(gated, axis=1, keepdims=True)
    out_ref[...] = picked.astype(BF)


def combine_table_kernel(experts, cap, gate_rows, ids_ref, gates_ref, out_ref):
    rows, gated = slot_table(ids_ref, gates_ref, experts, cap)
    if gate_rows:
        out_ref[0] = rows.T.astype(BF)
    else:
        weight = gated.T
        high = weight.astype(BF)
        out_ref[0] = high
        out_ref[1] = (weight - high.astype(F32)).astype(BF)


def combine_kernel(table_ref, rows_ref, out_ref):
    total = dot(table_ref[0], rows_ref[...], 1, 0)
    for i in range(1, table_ref.shape[0]):
        total = total + dot(table_ref[i], rows_ref[...], 1, 0)
    out_ref[...] = total.astype(BF)


def up_kernel(x_ref, w_ref, out_ref):
    count = out_ref.shape[0]
    for j in range(count):
        w = jnp.concatenate([w_ref[0, :, 128 * j : 128 * j + 128], w_ref[1, :, 128 * j : 128 * j + 128]], axis=1)
        part = dot(x_ref[...], w, 1, 0).astype(BF)
        out_ref[j, 0] = part[:, :128]
        out_ref[j, 1] = part[:, 128:]


def activate_kernel(pre_ref, out_ref):
    gate = pre_ref[0].astype(F32)
    up = pre_ref[1].astype(F32)
    hidden = (gate / (1.0 + jnp.exp(-gate)) * up).astype(BF)
    if len(out_ref.shape) == 2:
        out_ref[...] = hidden
    else:
        for i in range(out_ref.shape[0]):
            out_ref[i] = hidden


def down_kernel(h_ref, w_ref, out_ref):
    blocks = h_ref.shape[0]
    h = jnp.concatenate([h_ref[i] for i in range(blocks)], axis=1)
    out_ref[...] = dot(h, w_ref[...], 1, 0).astype(BF)


def grad_hidden_kernel(x_ref, w_ref, out_ref):
    count = out_ref.shape[0]
    part = dot(x_ref[...], w_ref[...], 1, 1).astype(BF)
    for j in range(count):
        out_ref[j] = part[:, 128 * j : 128 * j + 128]


def slope_kernel(saved_ref, out_ref):
    gate = saved_ref[0].astype(F32)
    up = saved_ref[1].astype(F32)
    sigma = 1.0 / (1.0 + jnp.exp(-gate))
    out_ref[0] = (up * sigma * (1.0 + gate * (1.0 - sigma))).T
    out_ref[1] = (gate * sigma).T


def d_pre_kernel(parts_ref, slope_ref, out_ref):
    total = parts_ref[0].astype(F32)
    for i in range(1, parts_ref.shape[0]):
        total = total + parts_ref[i].astype(F32)
    out_ref[0] = (total * slope_ref[0]).astype(BF)
    out_ref[1] = (total * slope_ref[1]).astype(BF)


def input_grad_kernel(d_ref, w_ref, out_ref):
    blocks = d_ref.shape[0]
    d = jnp.concatenate([d_ref[i, g] for g in range(2) for i in range(blocks)], axis=1)
    w = jnp.concatenate([w_ref[0], w_ref[1]], axis=1)
    out_ref[...] = dot(d, w, 1, 1).astype(BF)


def shifted(value, axis, steps):
    count = lax.axis_size(axis)
    first, last = (max(0, -steps), min(count, count - steps))
    return lax.ppermute(value, axis, [(source, source + steps) for source in range(first, last)])


def exchange(value, axis):
    return lax.all_to_all(value, axis, split_axis=0, concat_axis=0, tiled=True)


def body(inputs_b, grads_a, experts_a, experts_b, gates_a, gates_b, w_gate_up, w_down, saved_a):
    nodes, locals_ = lax.axis_size("node"), lax.axis_size("local")
    tokens, width = inputs_b.shape[1:]
    slots = saved_a.shape[4]
    cap = slots // nodes
    units = saved_a.shape[3]
    ids_a, ids_b = experts_a[0].T, experts_b[0].T
    gate_a, gate_b = gates_a[0].T, gates_b[0].T
    w_out = w_down[0, 0]
    w_in = w_gate_up[0, 0].transpose(1, 0, 2)

    def dispatch(ids, gates, x, gate_rows):
        return call(
            functools.partial(dispatch_kernel, nodes, cap, gate_rows),
            shape((slots, width)),
            (ids, gates, x),
            flops=2 * slots * tokens * width,
        )

    def combine_table(ids, gates, gate_rows):
        return call(
            functools.partial(combine_table_kernel, nodes, cap, gate_rows),
            shape((1 if gate_rows else 2, tokens, slots)),
            (ids, gates),
            flops=10**6,
        )

    def combine(table, rows):
        return call(combine_kernel, shape((tokens, width)), (table, rows), flops=2 * tokens * slots * width)

    rows_a = exchange(dispatch(ids_a, gate_a, grads_a[0], True), "node")
    send_b = dispatch(ids_b, gate_b, inputs_b[0], False)
    slope = call(slope_kernel, shape((2, slots, units), F32), (saved_a[0, 0],), flops=10**6)
    table_a = combine_table(ids_a, gate_a, True)
    table_b = combine_table(ids_b, gate_b, False)
    part_a = call(
        grad_hidden_kernel,
        shape((locals_, slots, units)),
        (rows_a, w_out),
        flops=2 * slots * width * units * locals_,
    )
    send_b, part_a = lax.optimization_barrier((send_b, part_a))
    rows_b = exchange(send_b, "node")
    parts_a = exchange(part_a, "local")
    half = 2
    part_b = call(
        up_kernel,
        shape((locals_, 2, slots, units)),
        (rows_b, w_in),
        flops=4 * slots * width * units * locals_,
        grid=(locals_ // half,),
        in_specs=[
            pl.BlockSpec((slots, width), lambda i: (0, 0)),
            pl.BlockSpec((2, width, half * units), lambda i: (0, 0, i)),
        ],
        out_specs=pl.BlockSpec((half, 2, slots, units), lambda i: (i, 0, 0, 0)),
    )
    pre_b = lax.psum_scatter(
        part_b.reshape(locals_, 2 * slots, units), "local", scatter_dimension=0, tiled=True
    ).reshape(2, slots, units)
    d_pre = call(d_pre_kernel, shape((2, slots, units)), (parts_a, slope), flops=10**6)
    d_all = lax.all_gather(d_pre, "local", axis=0, tiled=True).reshape(locals_, 2, slots, units)
    hidden = call(activate_kernel, shape((locals_, slots, units)), (pre_b,), flops=10**6)
    hidden_all = exchange(hidden, "local")
    result_b = call(
        down_kernel, shape((slots, width)), (hidden_all, w_out), flops=2 * slots * width * units * locals_
    )
    result_a = call(
        input_grad_kernel, shape((slots, width)), (d_all, w_in), flops=4 * slots * width * units * locals_
    )
    returned_a = exchange(result_a, "node")
    input_grad = combine(table_a, returned_a)
    grads_prev = shifted(input_grad[None], "section", -1)
    returned_b = exchange(result_b, "node")
    outputs = combine(table_b, returned_b)
    return (outputs[None], grads_prev)


def solution(mesh):
    return jax.shard_map(
        body,
        mesh=mesh,
        in_specs=(
            P("section", "node", "local"),
            P("section", "node", "local"),
            P("section", "node", None),
            P("section", "node", None),
            P("section", "node", None),
            P("section", "node", None),
            P("section", "node", "local", None, None),
            P("section", "node", None, "local"),
            P("section", "node", None, "local", None),
        ),
        out_specs=(P("section", "node", "local"), P("section", "node", "local")),
        check_vma=False,
    )
```

time: 329 us -> 262 us (0.80)
  local copies, waits for them, and re-layouts: 84.2 us -> 16.1 us
  waiting for transfers between devices: 148 us -> 181 us
  blocking collectives: 23.1 us -> 0 us
  matrix products: 12.9 us -> 0 us
  Pallas kernels: 0 us -> 12.6 us
  other arithmetic: 12 us -> 0 us
  starting transfers between devices: 33.6 us -> 37.2 us
    all_to_all x3 -> x6, waiting for transfers between devices: 21.1 us -> 109 us  [exchange(): return lax.all_to_all(value, axis, split_axis=0, concat_axis=0, tiled=True)]
    scatter x2 -> x0, local copies, waits for them, and re-layouts: 50.6 us -> none  [slot_layout(): table.at[flat, position]]
    unnamed x6 -> x2, waiting for transfers between devices: 38.3 us -> 0.03 us
    all_gather x2 -> x1, waiting for transfers between devices: 83.2 us -> 57.3 us  [body(): lax.all_gather(d_pre, 'local', axis=0, tiled=True)]
    all_to_all x1 -> x0, blocking collectives: 23.1 us -> none  [body(): lax.all_to_all(outgoing, 'node', split_axis=0, concat_axis=0, tiled=True)]
    gather x6 -> x0, local copies, waits for them, and re-layouts: 15.3 us -> none  [the longest x2 5.37 us: gather_sum(): picked = returned.reshape(-1, width)[index_rows]]
    dot_general x4 -> x0, matrix products: 12.9 us -> none  [the longest x1 4.14 us: body(): jnp.einsum('gnr,dgn->rd', lax.all_gather(d_pre, 'local', axis=1, tiled=Tr...]
    pallas_call x0 -> x13, Pallas kernels: none -> 12.6 us  [call(): pl.pallas_call(kernel, out_shape=outs, scratch_shapes=scratch, compiler_p...]
  transfers between devices with their start and end apart: 8 -> 9, of which waited for: 6 -> 8; matrix products, arithmetic and copies ran while one was open for 18% -> 1% of each run, Pallas kernels for 0% -> 2%
where the time goes in v1:
time: 262 us; the launch traced here: 261 us
  waiting for transfers between devices  181 us (69%)
  starting transfers between devices  37.2 us (14%)
  local copies, waits for them, and re-layouts  16.1 us (6%)
  between operations  14.2 us (5%)
  Pallas kernels  12.6 us (5%)
    all_to_all x6, waiting for transfers between devices, exchange(): return lax.all_to_all(value, axis, split_axis=0, concat_axis=0, tiled=True)  109 us
    all_gather x1, waiting for transfers between devices, body(): lax.all_gather(d_pre, 'local', axis=0, tiled=True)  57.3 us
    all_to_all x6, starting transfers between devices, exchange(): return lax.all_to_all(value, axis, split_axis=0, concat_axis=0, tiled=True)  35.8 us
    unnamed x40, local copies, waits for them, and re-layouts  16.1 us
    pallas_call x13, Pallas kernels, call(): pl.pallas_call(kernel, out_shape=outs, scratch_shapes=scratch, compiler_p...  12.6 us
    reduce_scatter x1, waiting for transfers between devices, body(): lax.psum_scatter(part_b.reshape(locals_, 2 * slots, units), 'local', scat...  8.34 us
    ppermute x1, waiting for transfers between devices, shifted(): lax.ppermute(value, axis, [(source, source + steps) for source in range(f...  5.73 us
  transfers between devices with their start and end apart: 9, of which 8 were waited for; matrix products, arithmetic and copies ran while one was open for 1% of the time, Pallas kernels for 2%

profile of v1, /device:TPU:1, one launch (start us, length us, event | category | flops | bytes accessed | tf_op | source)
XLA Modules:
  0.0 260.8 jit_solution(15567125492136116115)
XLA Ops:
  7.2 0.0 copy-start.2
  7.2 0.0 copy-start.11
  7.2 1.0 copy-done.11
  8.2 0.0 copy-start.13
  8.2 0.7 copy-done.13
  8.9 0.0 copy-start.15
  8.9 0.7 copy-done.15
  9.5 0.0 copy-start.12
  9.5 1.3 shard_map.106
  10.9 10.3 %all-to-all-start = ((bf16[16,40,512]{2,1,0:T(8,128)(2,1)}), bf16[16,40,512]{2,1,0:T(8,128)(2,1)S(1)}, u32[]{:S(2)}, u32[]{:S(2)}) async-start(bf16[16,40,512]{2,1,0:T(8,128)(2,1)} %bitcast.12), calls=%async_computation | async-start | bytes 1310720 | tf_op jit(solution)/shard_map/all_to_all | solution.py:151
  21.1 0.0 copy-done.12
  21.1 0.0 copy-done.17
  21.1 0.0 copy-done.18
  21.1 1.3 shard_map.105
  22.4 18.7 %all-to-all-done = bf16[16,40,512]{2,1,0:T(8,128)(2,1)S(1)} async-done(((bf16[16,40,512]{2,1,0:T(8,128)(2,1)}), bf16[16,40,512]{2,1,0:T(8,128)(2,1)S(1)}, u32[]{:S(2)}, u32[]{:S(2)}) %all-to-all-start) | async-done | bytes 655392 | tf_op jit(solution)/shard_map/all_to_all | solution.py:151
  41.2 0.0 copy-done.2
  41.2 2.0 shard_map.107
  43.1 3.5 %all-to-all-start.1 = ((bf16[16,40,512]{2,1,0:T(8,128)(2,1)}), bf16[16,40,512]{2,1,0:T(8,128)(2,1)S(1)}, u32[]{:S(2)}, u32[]{:S(2)}) async-start(bf16[16,40,512]{2,1,0:T(8,128)(2,1)} %bitcast.15), calls=%async_computation.1 | async-start | bytes 1310720 | tf_op jit(solution)/shard_map/all_to_all | solution.py:151
  46.6 0.0 reduce-scatter.2.cloned.1.call-start
  46.7 2.2 copy.14
  48.9 17.3 %all-to-all-done.1 = bf16[16,40,512]{2,1,0:T(8,128)(2,1)S(1)} async-done(((bf16[16,40,512]{2,1,0:T(8,128)(2,1)}), bf16[16,40,512]{2,1,0:T(8,128)(2,1)S(1)}, u32[]{:S(2)}, u32[]{:S(2)}) %all-to-all-start.1) | async-done | bytes 655392 | tf_op jit(solution)/shard_map/all_to_all | solution.py:151
  66.2 2.4 shard_map.108
  68.5 0.0 copy-start
  68.6 1.5 copy-done
  70.0 0.0 reduce-scatter.2.cloned.1.call-update
  70.1 8.4 %all-to-all-start.4 = ((bf16[8,640,128]{2,1,0:T(8,128)(2,1)}), bf16[8,640,128]{2,1,0:T(8,128)(2,1)S(1)}, u32[]{:S(2)}, u32[]{:S(2)}) async-start(bf16[8,640,128]{2,1,0:T(8,128)(2,1)} %shard_map.107), calls=%async_computation.5 | async-start | bytes 2621440 | tf_op jit(solution)/shard_map/all_to_all | solution.py:151
  78.4 0.0 all-gather.2.cloned.1.call-start
  78.5 0.0 copy-start.9
  78.5 1.0 copy-done.9
  79.4 0.3 shard_map.113.slope_ref
  79.7 0.0 copy-start.5
  79.7 0.8 copy-done.5
  80.6 44.5 %all-to-all-done.4.parts_ref = bf16[8,640,128]{2,1,0:T(8,128)(2,1)S(1)} async-done(((bf16[8,640,128]{2,1,0:T(8,128)(2,1)}), bf16[8,640,128]{2,1,0:T(8,128)(2,1)S(1)}, u32[]{:S(2)}, u32[]{:S(2)}) %all-to-all-start.4) | async-done | bytes 1310752 | tf_op jit(solution)/shard_map/all_to_all | solution.py:151
  125.0 1.1 copy-done.6
  126.1 0.2 shard_map.114
  126.3 0.7 copy-done.8
  127.1 0.0 all-gather.2.cloned.1.call-update
  127.1 8.3 %reduce-scatter.2.cloned.1.call-done = bf16[1,1280,128]{2,1,0:T(8,128)(2,1)} async-done(((bf16[8,1280,128]{2,1,0:T(8,128)(2,1)}), bf16[1,1280,128]{2,1,0:T(8,128)(2,1)}) %reduce-scatter.2.cloned.1.call-update) | async-done | bytes 327696 | tf_op jit(solution)/shard_map/reduce_scatter | solution.py:211
  135.4 1.0 copy-done.10
  136.4 0.1 shard_map.109
  136.5 0.0 copy-start.1
  136.5 1.1 copy-done.1
  137.6 4.3 %all-to-all-start.2 = ((bf16[8,640,128]{2,1,0:T(8,128)(2,1)}), bf16[8,640,128]{2,1,0:T(8,128)(2,1)S(1)}, u32[]{:S(2)}, u32[]{:S(2)}) async-start(bf16[8,640,128]{2,1,0:T(8,128)(2,1)} %copy-done.1), calls=%async_computation.3 | async-start | bytes 2621440 | tf_op jit(solution)/shard_map/all_to_all | solution.py:151
  141.8 57.3 %all-gather.2.cloned.1.call-done = bf16[16,640,128]{2,1,0:T(8,128)(2,1)} async-done(((bf16[2,640,128]{2,1,0:T(8,128)(2,1)}), bf16[16,640,128]{2,1,0:T(8,128)(2,1)}) %all-gather.2.cloned.1.call-update) | async-done | bytes 2621456 | tf_op jit(solution)/shard_map/all_gather | solution.py:215
  199.1 1.7 copy-done.4
  200.9 1.5 shard_map.115
  202.4 0.0 copy-start.7
  202.4 0.8 copy-done.7
  203.3 0.0 all-to-all-done.2.h_ref
  203.3 6.0 %all-to-all-start.5 = ((bf16[16,40,512]{2,1,0:T(8,128)(2,1)}), bf16[16,40,512]{2,1,0:T(8,128)(2,1)S(1)}, u32[]{:S(2)}, u32[]{:S(2)}) async-start(bf16[16,40,512]{2,1,0:T(8,128)(2,1)} %bitcast.43), calls=%async_computation.6 | async-start | bytes 1310720 | tf_op jit(solution)/shard_map/all_to_all | solution.py:151
  209.2 1.2 copy-done.3
  210.5 1.7 shard_map.110
  212.1 17.1 %all-to-all-done.5 = bf16[16,40,512]{2,1,0:T(8,128)(2,1)S(1)} async-done(((bf16[16,40,512]{2,1,0:T(8,128)(2,1)}), bf16[16,40,512]{2,1,0:T(8,128)(2,1)S(1)}, u32[]{:S(2)}, u32[]{:S(2)}) %all-to-all-start.5) | async-done | bytes 655392 | tf_op jit(solution)/shard_map/all_to_all | solution.py:151
  229.3 3.5 %all-to-all-start.3 = ((bf16[16,40,512]{2,1,0:T(8,128)(2,1)}), bf16[16,40,512]{2,1,0:T(8,128)(2,1)S(1)}, u32[]{:S(2)}, u32[]{:S(2)}) async-start(bf16[16,40,512]{2,1,0:T(8,128)(2,1)} %bitcast.21), calls=%async_computation.4 | async-start | bytes 1310720 | tf_op jit(solution)/shard_map/all_to_all | solution.py:151
  232.8 0.0 copy-done.14
  232.8 0.0 copy-done.16
  232.8 0.3 shard_map.112.table_ref
  233.1 0.3 shard_map.116
  233.3 1.3 collective-permute-start
  234.6 0.3 shard_map.104.table_ref
  234.9 5.7 %collective-permute-done = bf16[1,128,512]{2,1,0:T(8,128)(2,1)S(1)} collective-permute-done((bf16[1,128,512]{2,1,0:T(8,128)(2,1)S(1)}, bf16[1,128,512]{2,1,0:T(8,128)(2,1)S(1)}, u32[]{:S(2)}, u32[]{:S(2)}) %collective-permute-start) | collective-permute-done | bytes 131104 | tf_op jit(solution)/shard_map/ppermute | solution.py:147
  240.7 11.6 %all-to-all-done.3 = bf16[16,40,512]{2,1,0:T(8,128)(2,1)S(1)} async-done(((bf16[16,40,512]{2,1,0:T(8,128)(2,1)}), bf16[16,40,512]{2,1,0:T(8,128)(2,1)S(1)}, u32[]{:S(2)}, u32[]{:S(2)}) %all-to-all-start.3) | async-done | bytes 655392 | tf_op jit(solution)/shard_map/all_to_all | solution.py:151
  252.3 1.0 shard_map.111
  253.3 0.7 copy.16
  (9 shorter events, 0.0 us)
Async XLA Ops:
  7.2 34.0 %copy-start.2 = (bf16[1,1,1024,512]{3,2,1,0:T(8,128)(2,1)S(1)}, bf16[1,1,1024,512]{3,2,1,0:T(8,128)(2,1)}, u32[]{:S(2)}) copy-start(bf16[1,1,1024,512]{3,2,1,0:T(8,128)(2,1)} %param.16) | copy-start | bytes 3145732
  7.2 1.0 copy-start.11
  8.2 0.7 copy-start.13
  8.9 0.7 copy-start.15
  9.5 11.6 %copy-start.12 = (bf16[1,128,512]{2,1,0:T(8,128)(2,1)S(1)}, bf16[1,128,512]{2,1,0:T(8,128)(2,1)}, u32[]{:S(2)}) copy-start(bf16[1,128,512]{2,1,0:T(8,128)(2,1)} %param.9) | copy-start | bytes 393220
  9.5 11.6 %copy-start.17 = (s32[1,128,4]{1,2,0:T(4,128)S(1)}, s32[1,128,4]{1,2,0:T(4,128)}, u32[]{:S(2)}) copy-start(s32[1,128,4]{1,2,0:T(4,128)} %param.12) | copy-start | bytes 6148
  9.5 11.6 %copy-start.18 = (f32[1,128,4]{1,2,0:T(4,128)S(1)}, f32[1,128,4]{1,2,0:T(4,128)}, u32[]{:S(2)}) copy-start(f32[1,128,4]{1,2,0:T(4,128)} %param.14) | copy-start | bytes 6148
  10.9 30.3 %all-to-all-start = ((bf16[16,40,512]{2,1,0:T(8,128)(2,1)}), bf16[16,40,512]{2,1,0:T(8,128)(2,1)S(1)}, u32[]{:S(2)}, u32[]{:S(2)}) async-start(bf16[16,40,512]{2,1,0:T(8,128)(2,1)} %bitcast.12), calls=%async_computation | async-start | bytes 1310720 | tf_op jit(solution)/shard_map/all_to_all | solution.py:151
  43.1 23.1 %all-to-all-start.1 = ((bf16[16,40,512]{2,1,0:T(8,128)(2,1)}), bf16[16,40,512]{2,1,0:T(8,128)(2,1)S(1)}, u32[]{:S(2)}, u32[]{:S(2)}) async-start(bf16[16,40,512]{2,1,0:T(8,128)(2,1)} %bitcast.15), calls=%async_computation.1 | async-start | bytes 1310720 | tf_op jit(solution)/shard_map/all_to_all | solution.py:151
  46.6 88.8 %reduce-scatter.2.cloned.1.call-start = ((), (), s32[]{:S(2)}) async-start(), calls=%async_computation.7 | async-start | bytes 2949120 | tf_op jit(solution)/shard_map/reduce_scatter | solution.py:211
  68.5 1.5 copy-start
  70.1 55.0 %all-to-all-start.4 = ((bf16[8,640,128]{2,1,0:T(8,128)(2,1)}), bf16[8,640,128]{2,1,0:T(8,128)(2,1)S(1)}, u32[]{:S(2)}, u32[]{:S(2)}) async-start(bf16[8,640,128]{2,1,0:T(8,128)(2,1)} %shard_map.107), calls=%async_computation.5 | async-start | bytes 2621440 | tf_op jit(solution)/shard_map/all_to_all | solution.py:151
  78.4 120.7 %all-gather.2.cloned.1.call-start = ((), (), s32[]{:S(2)}) async-start(), calls=%async_computation.8 | async-start | bytes 2949120 | tf_op jit(solution)/shard_map/all_gather | solution.py:215
  78.5 1.0 copy-start.9
  79.7 0.8 copy-start.5
  125.0 1.1 copy-start.6
  126.3 0.7 copy-start.8
  135.4 1.0 copy-start.10
  136.5 1.1 copy-start.1
  137.6 65.7 %all-to-all-start.2 = ((bf16[8,640,128]{2,1,0:T(8,128)(2,1)}), bf16[8,640,128]{2,1,0:T(8,128)(2,1)S(1)}, u32[]{:S(2)}, u32[]{:S(2)}) async-start(bf16[8,640,128]{2,1,0:T(8,128)(2,1)} %copy-done.1), calls=%async_computation.3 | async-start | bytes 2621440 | tf_op jit(solution)/shard_map/all_to_all | solution.py:151
  199.1 1.7 copy-start.4
  202.4 0.8 copy-start.7
  203.3 26.0 %all-to-all-start.5 = ((bf16[16,40,512]{2,1,0:T(8,128)(2,1)}), bf16[16,40,512]{2,1,0:T(8,128)(2,1)S(1)}, u32[]{:S(2)}, u32[]{:S(2)}) async-start(bf16[16,40,512]{2,1,0:T(8,128)(2,1)} %bitcast.43), calls=%async_computation.6 | async-start | bytes 1310720 | tf_op jit(solution)/shard_map/all_to_all | solution.py:151
  209.2 1.2 copy-start.3
  210.5 22.3 %copy-start.14 = (s32[1,128,4]{1,2,0:T(4,128)S(1)}, s32[1,128,4]{1,2,0:T(4,128)}, u32[]{:S(2)}) copy-start(s32[1,128,4]{1,2,0:T(4,128)} %param.11) | copy-start | bytes 6148
  210.5 22.3 %copy-start.16 = (f32[1,128,4]{1,2,0:T(4,128)S(1)}, f32[1,128,4]{1,2,0:T(4,128)}, u32[]{:S(2)}) copy-start(f32[1,128,4]{1,2,0:T(4,128)} %param.13) | copy-start | bytes 6148
  229.3 23.0 %all-to-all-start.3 = ((bf16[16,40,512]{2,1,0:T(8,128)(2,1)}), bf16[16,40,512]{2,1,0:T(8,128)(2,1)S(1)}, u32[]{:S(2)}, u32[]{:S(2)}) async-start(bf16[16,40,512]{2,1,0:T(8,128)(2,1)} %bitcast.21), calls=%async_computation.4 | async-start | bytes 1310720 | tf_op jit(solution)/shard_map/all_to_all | solution.py:151
  233.3 7.3 %collective-permute-start = (bf16[1,128,512]{2,1,0:T(8,128)(2,1)S(1)}, bf16[1,128,512]{2,1,0:T(8,128)(2,1)S(1)}, u32[]{:S(2)}, u32[]{:S(2)}) collective-permute-start(bf16[1,128,512]{2,1,0:T(8,128)(2,1)S(1)} %bitcast.49), channel_id=1, source_target_pairs={{1,0},{2,1},{3,2},{5,4},{6,5},{7,6},{9,8},{10,9},{11,10},{13,12},{... | collective-permute-start | bytes 393224 | tf_op jit(solution)/shard_map/ppermute | solution.py:147
Sparse Core Ops, SparseCore 0:
  70.2 65.1 reduce-scatter.1
  137.5 61.5 all-gather.1

commit v2 on v1

--- a/solution.py
+++ b/solution.py
@@ -10,14 +10,18 @@
 BF = jnp.bfloat16
 F32 = jnp.float32
 VMEM_LIMIT = 48 * 1024 * 1024
-
-
-def call(kernel, outs, args, flops=0, grid=None, in_specs=None, out_specs=None, scratch=()):
+LOCAL_ORDER = (3, 1, -3, -1, 4, 0, 2, -2)
+
+
+def call(kernel, outs, args, flops=0, grid=None, in_specs=None, out_specs=None, scratch=(), scalars=False):
     moved = sum(a.size * a.dtype.itemsize for a in args)
     moved += sum(o.size * o.dtype.itemsize for o in jax.tree.leaves(outs))
     extra = {}
     if grid is not None:
         extra = dict(grid=grid, in_specs=in_specs, out_specs=out_specs)
+    elif scalars:
+        smem, vmem = pl.BlockSpec(memory_space=pltpu.SMEM), pl.BlockSpec(memory_space=pltpu.VMEM)
+        extra = dict(in_specs=[smem] + [vmem] * (len(args) - 1))
     return pl.pallas_call(
         kernel,
         out_shape=outs,
@@ -85,6 +89,10 @@
     out_ref[...] = total.astype(BF)
 
 
+def spread_refs(ahead_ref, behind_ref, across_ref, own_ref):
+    return [ahead_ref.at[0], ahead_ref.at[1], behind_ref.at[0], behind_ref.at[1], across_ref, *[own_ref.at[i] for i in range(3)]]
+
+
 def up_kernel(x_ref, w_ref, out_ref):
     count = out_ref.shape[0]
     for j in range(count):
@@ -94,15 +102,50 @@
         out_ref[j, 1] = part[:, 128:]
 
 
+def grad_hidden_kernel(place_ref, x_ref, w_ref, *out_refs):
+    outs = spread_refs(*out_refs)
+    unit = outs[0].shape[-1]
+    for i in range(0, len(outs), 2):
+        w = jnp.concatenate(
+            [w_ref[pl.ds(pl.multiple_of(place_ref[i + j] * unit, unit), unit), :] for j in range(2)], axis=0
+        )
+        part = dot(x_ref[...], w, 1, 1).astype(BF)
+        outs[i][...] = part[:, :unit]
+        outs[i + 1][...] = part[:, unit:]
+
+
+def relay_sum_kernel(core_ref, own_ref, ahead_ref, behind_ref, across_ref, plus_ref, minus_ref):
+    plus = own_ref[1].astype(F32) + ahead_ref[0].astype(F32)
+    minus = own_ref[2].astype(F32) + behind_ref[0].astype(F32)
+    across = across_ref[...].astype(F32)
+    first = core_ref[0] == 0
+    zero = jnp.zeros_like(across)
+    plus_ref[...] = (plus + jnp.where(first, zero, across)).astype(BF)
+    minus_ref[...] = (minus + jnp.where(first, across, zero)).astype(BF)
+
+
+def arrived_sum(own_ref, ahead_ref, behind_ref, plus_ref, minus_ref):
+    total = own_ref[0].astype(F32)
+    for part in (ahead_ref[1], behind_ref[1], plus_ref[...], minus_ref[...]):
+        total = total + part.astype(F32)
+    return total
+
+
 def activate_kernel(pre_ref, out_ref):
-    gate = pre_ref[0].astype(F32)
-    up = pre_ref[1].astype(F32)
-    hidden = (gate / (1.0 + jnp.exp(-gate)) * up).astype(BF)
-    if len(out_ref.shape) == 2:
-        out_ref[...] = hidden
-    else:
-        for i in range(out_ref.shape[0]):
-            out_ref[i] = hidden
+    gate, up = pre_ref[0].astype(F32), pre_ref[1].astype(F32)
+    out_ref[...] = (gate / (1.0 + jnp.exp(-gate)) * up).astype(BF)
+
+
+def grad_sum_kernel(*refs):
+    refs[-1][...] = arrived_sum(*refs[:-1]).astype(BF)
+
+
+def pack_kernel(core_ref, own_ref, low_ref, high_ref, ahead_ref, behind_ref, across_ref):
+    ahead_ref[0] = own_ref[...]
+    ahead_ref[1] = low_ref[...]
+    behind_ref[0] = own_ref[...]
+    behind_ref[1] = high_ref[...]
+    across_ref[...] = jnp.where(core_ref[0] == 0, low_ref[...], high_ref[...])
 
 
 def down_kernel(h_ref, w_ref, out_ref):
@@ -111,34 +154,54 @@
     out_ref[...] = dot(h, w_ref[...], 1, 0).astype(BF)
 
 
-def grad_hidden_kernel(x_ref, w_ref, out_ref):
-    count = out_ref.shape[0]
-    part = dot(x_ref[...], w_ref[...], 1, 1).astype(BF)
-    for j in range(count):
-        out_ref[j] = part[:, 128 * j : 128 * j + 128]
+def input_grad_kernel(
+    place_ref, own_ref, low_ref, high_ref, ahead_ref, behind_ref, across_ref, slope_ref, w_ref, out_ref
+):
+    blocks = [ahead_ref.at[1], ahead_ref.at[0], behind_ref.at[1], behind_ref.at[0], across_ref, own_ref, high_ref, low_ref]
+    source = [2, 3, 0, 1, 4, 5, 6, 7]
+    unit = own_ref.shape[-1]
+    total = None
+    for block, i in zip(blocks, source):
+        at = place_ref[i]
+        columns = pl.ds(pl.multiple_of(at * unit, unit), unit)
+        w = jnp.concatenate([w_ref[0, :, columns], w_ref[1, :, columns]], axis=1)
+        h = block[...].astype(F32)
+        d = jnp.concatenate([(h * slope_ref[at, g].astype(F32)).astype(BF) for g in range(2)], axis=1)
+        part = dot(d, w, 1, 1)
+        total = part if total is None else total + part
+    out_ref[...] = total.astype(BF)
+
+
+def rotated(value, steps, mirrored=False):
+    nodes, count = lax.axis_size("node"), lax.axis_size("local")
+    pairs = []
+    for node in range(nodes):
+        way = -steps if mirrored and node % 2 else steps
+        pairs += [(node * count + i, node * count + (i + way) % count) for i in range(count)]
+    return lax.ppermute(value, ("node", "local"), pairs)
 
 
 def slope_kernel(saved_ref, out_ref):
     gate = saved_ref[0].astype(F32)
     up = saved_ref[1].astype(F32)
     sigma = 1.0 / (1.0 + jnp.exp(-gate))
-    out_ref[0] = (up * sigma * (1.0 + gate * (1.0 - sigma))).T
-    out_ref[1] = (gate * sigma).T
-
-
-def d_pre_kernel(parts_ref, slope_ref, out_ref):
-    total = parts_ref[0].astype(F32)
-    for i in range(1, parts_ref.shape[0]):
-        total = total + parts_ref[i].astype(F32)
-    out_ref[0] = (total * slope_ref[0]).astype(BF)
-    out_ref[1] = (total * slope_ref[1]).astype(BF)
-
-
-def input_grad_kernel(d_ref, w_ref, out_ref):
-    blocks = d_ref.shape[0]
-    d = jnp.concatenate([d_ref[i, g] for g in range(2) for i in range(blocks)], axis=1)
-    w = jnp.concatenate([w_ref[0], w_ref[1]], axis=1)
-    out_ref[...] = dot(d, w, 1, 1).astype(BF)
+    out_ref[0] = (up * sigma * (1.0 + gate * (1.0 - sigma))).T.astype(BF)
+    out_ref[1] = (gate * sigma).T.astype(BF)
+
+
+def shifted(value, axis, steps):
+    count = lax.axis_size(axis)
+    first, last = (max(0, -steps), min(count, count - steps))
+    return lax.ppermute(value, axis, [(source, source + steps) for source in range(first, last)])
+
+
+def rotated(value, steps, mirrored=False):
+    nodes, count = lax.axis_size("node"), lax.axis_size("local")
+    pairs = []
+    for node in range(nodes):
+        way = -steps if mirrored and node % 2 else steps
+        pairs += [(node * count + i, node * count + (i + way) % count) for i in range(count)]
+    return lax.ppermute(value, ("node", "local"), pairs)
 
 
 def shifted(value, axis, steps):
@@ -181,20 +244,39 @@
     def combine(table, rows):
         return call(combine_kernel, shape((tokens, width)), (table, rows), flops=2 * tokens * slots * width)
 
-    rows_a = exchange(dispatch(ids_a, gate_a, grads_a[0], True), "node")
+    me = lax.axis_index("local").astype(jnp.int32)
+    core = (lax.axis_index("node") % 2).astype(jnp.int32).reshape(1)
+    place = (me + jnp.array(LOCAL_ORDER, jnp.int32)) % locals_
+
+    def partials(kernel, block, x, w):
+        kinds = [shape(lead + block) for lead in ((2,), (2,), (), (3,))]
+        flops = 2 * width * locals_ * functools.reduce(lambda a, b: a * b, block)
+        return call(kernel, kinds, (place, x, w), flops=flops, scalars=True)
+
+    def relay_sum(own, ahead, behind, across):
+        kind = shape(across.shape)
+        return call(relay_sum_kernel, (kind, kind), (core, own, ahead, behind, across), flops=10**6, scalars=True)
+
+    def gather_local(own):
+        low, high = rotated(own, 2), rotated(own, -2)
+        two, one = shape((2,) + own.shape), shape(own.shape)
+        ahead, behind, across = call(pack_kernel, (two, two, one), (core, own, low, high), scalars=True)
+        across = rotated(across, 2, True)
+        return own, low, high, rotated(ahead, 1), rotated(behind, -1), across
+
+    send_a = dispatch(ids_a, gate_a, grads_a[0], True)
+    rows_a = exchange(send_a, "node")
     send_b = dispatch(ids_b, gate_b, inputs_b[0], False)
-    slope = call(slope_kernel, shape((2, slots, units), F32), (saved_a[0, 0],), flops=10**6)
+    slope = call(slope_kernel, shape((2, slots, units)), (saved_a[0, 0],), flops=10**6)
     table_a = combine_table(ids_a, gate_a, True)
     table_b = combine_table(ids_b, gate_b, False)
-    part_a = call(
-        grad_hidden_kernel,
-        shape((locals_, slots, units)),
-        (rows_a, w_out),
-        flops=2 * slots * width * units * locals_,
-    )
-    send_b, part_a = lax.optimization_barrier((send_b, part_a))
+    slopes = lax.all_gather(slope, "local", axis=0, tiled=True).reshape(locals_, 2, slots, units)
+    rows_a, send_b, w_in, table_a, table_b = lax.optimization_barrier((rows_a, send_b, w_in, table_a, table_b))
     rows_b = exchange(send_b, "node")
-    parts_a = exchange(part_a, "local")
+    ahead, behind, across, own = partials(grad_hidden_kernel, (slots, units), rows_a, w_out)
+    across = rotated(across, -2, True)
+    ahead = rotated(ahead, 1)
+    behind = rotated(behind, -1)
     half = 2
     part_b = call(
         up_kernel,
@@ -208,23 +290,32 @@
         ],
         out_specs=pl.BlockSpec((half, 2, slots, units), lambda i: (i, 0, 0, 0)),
     )
+    ahead, behind, across, part_b, slopes = lax.optimization_barrier((ahead, behind, across, part_b, slopes))
+    plus, minus = relay_sum(own, ahead, behind, across)
     pre_b = lax.psum_scatter(
         part_b.reshape(locals_, 2 * slots, units), "local", scatter_dimension=0, tiled=True
     ).reshape(2, slots, units)
-    d_pre = call(d_pre_kernel, shape((2, slots, units)), (parts_a, slope), flops=10**6)
-    d_all = lax.all_gather(d_pre, "local", axis=0, tiled=True).reshape(locals_, 2, slots, units)
-    hidden = call(activate_kernel, shape((locals_, slots, units)), (pre_b,), flops=10**6)
-    hidden_all = exchange(hidden, "local")
+    sums_a = (own, ahead, behind, rotated(plus, 2), rotated(minus, -2))
+    grad_hidden = call(grad_sum_kernel, shape((slots, units)), sums_a, flops=10**6)
+    grad_hidden = gather_local(grad_hidden)
+    pre_b, _, _, _ = lax.optimization_barrier((pre_b, *grad_hidden[3:]))
+    result_a = call(
+        input_grad_kernel,
+        shape((slots, width)),
+        (place, *grad_hidden, slopes, w_in),
+        flops=4 * slots * width * units * locals_,
+        scalars=True,
+    )
+    hidden = call(activate_kernel, shape((slots, units)), (pre_b,), flops=10**6)
+    hidden_all = lax.all_gather(hidden, "local", axis=0, tiled=True).reshape(locals_, slots, units)
     result_b = call(
         down_kernel, shape((slots, width)), (hidden_all, w_out), flops=2 * slots * width * units * locals_
     )
-    result_a = call(
-        input_grad_kernel, shape((slots, width)), (d_all, w_in), flops=4 * slots * width * units * locals_
-    )
     returned_a = exchange(result_a, "node")
+    returned_a, result_b = lax.optimization_barrier((returned_a, result_b))
+    returned_b = exchange(result_b, "node")
     input_grad = combine(table_a, returned_a)
     grads_prev = shifted(input_grad[None], "section", -1)
-    returned_b = exchange(result_b, "node")
     outputs = combine(table_b, returned_b)
     return (outputs[None], grads_prev)
 

time: 262 us -> 220 us (0.84)
  waiting for transfers between devices: 181 us -> 97.9 us
  starting transfers between devices: 37.2 us -> 70.8 us
  Pallas kernels: 12.6 us -> 19.1 us
    all_to_all x6 -> x4, waiting for transfers between devices: 109 us -> 30.1 us  [exchange(): return lax.all_to_all(value, axis, split_axis=0, concat_axis=0, tiled=True)]
    ppermute x0 -> x10, starting transfers between devices: none -> 38.1 us  [rotated(): return lax.ppermute(value, ('node', 'local'), pairs)]
    ppermute x0 -> x10, waiting for transfers between devices: none -> 36.4 us  [rotated(): return lax.ppermute(value, ('node', 'local'), pairs)]
    all_gather x1 -> x2, waiting for transfers between devices: 57.3 us -> 25.8 us  [the longest x1 25.8 us: body(): lax.all_gather(hidden, 'local', axis=0, tiled=True)]
    reduce_scatter x1, waiting for transfers between devices: 8.34 us -> 0.01 us  [body(): lax.psum_scatter(part_b.reshape(locals_, 2 * slots, units), 'local', scat...]
    pallas_call x13 -> x15, Pallas kernels: 12.6 us -> 19.1 us  [call(): pl.pallas_call(kernel, out_shape=outs, scratch_shapes=scratch, compiler_p...]
    all_to_all x6 -> x4, starting transfers between devices: 35.8 us -> 31.3 us  [exchange(): return lax.all_to_all(value, axis, split_axis=0, concat_axis=0, tiled=True)]
    unnamed x40 -> x44, local copies, waits for them, and re-layouts: 16.1 us -> 16.6 us
  transfers between devices with their start and end apart: 9 -> 18, of which waited for: 8 -> 11; matrix products, arithmetic and copies ran while one was open for 1% -> 1% of each run, Pallas kernels for 2% -> 7%
where the time goes in v2:
time: 220 us; the launch traced here: 218 us
  waiting for transfers between devices  97.9 us (44%)
  starting transfers between devices  70.8 us (32%)
  Pallas kernels  19.1 us (9%)
  local copies, waits for them, and re-layouts  16.6 us (8%)
  between operations  14.1 us (6%)
    ppermute x10, starting transfers between devices, rotated(): return lax.ppermute(value, ('node', 'local'), pairs)  38.1 us
    ppermute x10, waiting for transfers between devices, rotated(): return lax.ppermute(value, ('node', 'local'), pairs)  36.4 us
    all_to_all x4, starting transfers between devices, exchange(): return lax.all_to_all(value, axis, split_axis=0, concat_axis=0, tiled=True)  31.3 us
    all_to_all x4, waiting for transfers between devices, exchange(): return lax.all_to_all(value, axis, split_axis=0, concat_axis=0, tiled=True)  30.1 us
    all_gather x1, waiting for transfers between devices, body(): lax.all_gather(hidden, 'local', axis=0, tiled=True)  25.8 us
    pallas_call x15, Pallas kernels, call(): pl.pallas_call(kernel, out_shape=outs, scratch_shapes=scratch, compiler_p...  19.1 us
    unnamed x44, local copies, waits for them, and re-layouts  16.6 us
    ppermute x1, waiting for transfers between devices, shifted(): lax.ppermute(value, axis, [(source, source + steps) for source in range(f...  5.65 us
  transfers between devices with their start and end apart: 18, of which 11 were waited for; matrix products, arithmetic and copies ran while one was open for 1% of the time, Pallas kernels for 7%

profile of v2, /device:TPU:1, one launch (start us, length us, event | category | flops | bytes accessed | tf_op | source)
XLA Modules:
  0.0 218.5 jit_solution(3730680949058688576)
XLA Ops:
  7.2 0.0 all-gather.3.cloned.1.call-start
  7.2 1.0 copy-done.8
  8.2 1.0 shard_map.119
  9.2 0.0 all-gather.3.cloned.1.call-update
  9.2 0.9 copy-done.12
  10.1 0.7 copy-done.14
  10.8 0.7 copy-done.16
  11.5 1.3 shard_map.113
  12.8 10.3 %all-to-all-start = ((bf16[16,40,512]{2,1,0:T(8,128)(2,1)}), bf16[16,40,512]{2,1,0:T(8,128)(2,1)S(1)}, u32[]{:S(2)}, u32[]{:S(2)}) async-start(bf16[16,40,512]{2,1,0:T(8,128)(2,1)} %bitcast.5), calls=%async_computation | async-start | bytes 1310720 | tf_op jit(solution)/shard_map/all_to_all | solution.py:214
  23.1 2.2 %copy.15 = bf16[1,1,512,2,1024]{4,2,3,1,0:T(8,128)(2,1)S(1)} copy(bf16[1,1,512,2,1024]{4,3,2,1,0:T(2,128)(2,1)} %param.16) | data formatting | bytes 4194304 | tf_op args[6]
  25.3 0.3 shard_map.115.table_ref
  25.6 0.3 shard_map.116.table_ref
  26.0 0.7 copy-done.2
  26.7 1.3 shard_map.114
  28.0 15.1 %all-to-all-done = bf16[16,40,512]{2,1,0:T(8,128)(2,1)S(1)} async-done(((bf16[16,40,512]{2,1,0:T(8,128)(2,1)}), bf16[16,40,512]{2,1,0:T(8,128)(2,1)S(1)}, u32[]{:S(2)}, u32[]{:S(2)}) %all-to-all-start) | async-done | bytes 655392 | tf_op jit(solution)/shard_map/all_to_all | solution.py:214
  43.1 0.8 copy-done.6
  43.9 3.5 %all-to-all-start.1 = ((bf16[16,40,512]{2,1,0:T(8,128)(2,1)}), bf16[16,40,512]{2,1,0:T(8,128)(2,1)S(1)}, u32[]{:S(2)}, u32[]{:S(2)}) async-start(bf16[16,40,512]{2,1,0:T(8,128)(2,1)} %bitcast.19), calls=%async_computation.1 | async-start | bytes 1310720 | tf_op jit(solution)/shard_map/all_to_all | solution.py:214
  47.4 0.0 reduce-scatter.2.cloned.1.call-start
  47.5 1.2 copy-done.4
  48.7 1.1 copy-done.7
  49.8 2.1 shard_map.117
  51.9 2.3 %collective-permute-start = (bf16[2,640,128]{2,1,0:T(8,128)(2,1)}, bf16[2,640,128]{2,1,0:T(8,128)(2,1)}, u32[]{:S(2)}, u32[]{:S(2)}) collective-permute-start(bf16[2,640,128]{2,1,0:T(8,128)(2,1)} %get-tuple-element.27), channel_id=1, source_target_pairs={{0,4},{4,8},{8,12},{12,16},{16,20},{20,24},{24,28},{28,0},{32,36},... | collective-permute-start | bytes 983048 | tf_op jit(solution)/shard_map/ppermute | solution.py:204
  54.2 8.6 %collective-permute-start.1 = (bf16[2,640,128]{2,1,0:T(8,128)(2,1)}, bf16[2,640,128]{2,1,0:T(8,128)(2,1)}, u32[]{:S(2)}, u32[]{:S(2)}) collective-permute-start(bf16[2,640,128]{2,1,0:T(8,128)(2,1)} %get-tuple-element.28), channel_id=1, source_target_pairs={{0,28},{4,0},{8,4},{12,8},{16,12},{20,16},{24,20},{28,24},{32,60},... | collective-permute-start | bytes 983048 | tf_op jit(solution)/shard_map/ppermute | solution.py:204
  62.8 1.9 collective-permute-start.2
  64.8 2.2 %all-to-all-done.1 = bf16[16,40,512]{2,1,0:T(8,128)(2,1)S(1)} async-done(((bf16[16,40,512]{2,1,0:T(8,128)(2,1)}), bf16[16,40,512]{2,1,0:T(8,128)(2,1)S(1)}, u32[]{:S(2)}, u32[]{:S(2)}) %all-to-all-start.1) | async-done | bytes 655392 | tf_op jit(solution)/shard_map/all_to_all | solution.py:214
  66.9 2.4 %shard_map.118 = bf16[8,2,640,128]{3,2,1,0:T(8,128)(2,1)S(1)} custom-call(bf16[640,512]{1,0:T(8,128)(2,1)S(1)} %bitcast.41, bf16[2,512,1024]{2,1,0:T(8,128)(2,1)S(1)} %bitcast.36), custom_call_target="tpu_custom_call" | custom-call | flops 1342177280 | bytes 5373952 | tf_op jit(solution)/shard_map/pallas_call | solution.py:25
  69.3 1.5 copy-done
  70.8 1.8 collective-permute-done.2.across_ref
  72.7 0.0 all-gather.3.cloned.1.call-done
  72.7 0.0 reduce-scatter.2.cloned.1.call-update
  72.7 0.0 all-gather.5.cloned.1.call-start
  72.8 1.3 shard_map.120
  74.0 2.3 %collective-permute-start.3 = (bf16[640,128]{1,0:T(8,128)(2,1)S(1)}, bf16[640,128]{1,0:T(8,128)(2,1)S(1)}, u32[]{:S(2)}, u32[]{:S(2)}) collective-permute-start(bf16[640,128]{1,0:T(8,128)(2,1)S(1)} %get-tuple-element.35), channel_id=1, source_target_pairs={{0,8},{4,12},{8,16},{12,20},{16,24},{20,28},{24,0},{28,4},{32,40},... | collective-permute-start | bytes 491528 | tf_op jit(solution)/shard_map/ppermute | solution.py:204
  76.3 6.8 %collective-permute-start.4 = (bf16[640,128]{1,0:T(8,128)(2,1)S(1)}, bf16[640,128]{1,0:T(8,128)(2,1)S(1)}, u32[]{:S(2)}, u32[]{:S(2)}) collective-permute-start(bf16[640,128]{1,0:T(8,128)(2,1)S(1)} %get-tuple-element.36), channel_id=1, source_target_pairs={{0,24},{4,28},{8,0},{12,4},{16,8},{20,12},{24,16},{28,20},{32,56},... | collective-permute-start | bytes 491528 | tf_op jit(solution)/shard_map/ppermute | solution.py:204
  83.1 5.3 %collective-permute-done.3.refs_3_ = bf16[640,128]{1,0:T(8,128)(2,1)S(1)} collective-permute-done((bf16[640,128]{1,0:T(8,128)(2,1)S(1)}, bf16[640,128]{1,0:T(8,128)(2,1)S(1)}, u32[]{:S(2)}, u32[]{:S(2)}) %collective-permute-start.3) | collective-permute-done | bytes 163872 | tf_op jit(solution)/shard_map/ppermute | solution.py:204
  88.4 2.0 collective-permute-done.4.refs_4_
  90.4 1.2 shard_map.121.own_ref
  91.6 5.4 %collective-permute-start.5 = (bf16[640,128]{1,0:T(8,128)(2,1)S(1)}, bf16[640,128]{1,0:T(8,128)(2,1)S(1)}, u32[]{:S(2)}, u32[]{:S(2)}) collective-permute-start(bf16[640,128]{1,0:T(8,128)(2,1)S(1)} %shard_map.121.own_ref), channel_id=1, source_target_pairs={{0,8},{4,12},{8,16},{12,20},{16,24},{20,28},{24,0},{28,4},{32,40},... | collective-permute-start | bytes 491528 | tf_op jit(solution)/shard_map/ppermute | solution.py:204
  97.0 2.4 %collective-permute-start.6 = (bf16[640,128]{1,0:T(8,128)(2,1)S(1)}, bf16[640,128]{1,0:T(8,128)(2,1)S(1)}, u32[]{:S(2)}, u32[]{:S(2)}) collective-permute-start(bf16[640,128]{1,0:T(8,128)(2,1)S(1)} %shard_map.121.own_ref), channel_id=1, source_target_pairs={{0,24},{4,28},{8,0},{12,4},{16,8},{20,12},{24,16},{28,20},{32,56},... | collective-permute-start | bytes 491528 | tf_op jit(solution)/shard_map/ppermute | solution.py:204
  99.4 6.8 %collective-permute-done.5.low_ref = bf16[640,128]{1,0:T(8,128)(2,1)S(1)} collective-permute-done((bf16[640,128]{1,0:T(8,128)(2,1)S(1)}, bf16[640,128]{1,0:T(8,128)(2,1)S(1)}, u32[]{:S(2)}, u32[]{:S(2)}) %collective-permute-start.5) | collective-permute-done | bytes 163872 | tf_op jit(solution)/shard_map/ppermute | solution.py:204
  106.2 5.9 %collective-permute-done.6.high_ref = bf16[640,128]{1,0:T(8,128)(2,1)S(1)} collective-permute-done((bf16[640,128]{1,0:T(8,128)(2,1)S(1)}, bf16[640,128]{1,0:T(8,128)(2,1)S(1)}, u32[]{:S(2)}, u32[]{:S(2)}) %collective-permute-start.6) | collective-permute-done | bytes 163872 | tf_op jit(solution)/shard_map/ppermute | solution.py:204
  112.1 0.1 shard_map.122
  112.3 1.9 collective-permute-start.7
  114.2 4.6 %collective-permute-start.8 = (bf16[2,640,128]{2,1,0:T(8,128)(2,1)S(1)}, bf16[2,640,128]{2,1,0:T(8,128)(2,1)S(1)}, u32[]{:S(2)}, u32[]{:S(2)}) collective-permute-start(bf16[2,640,128]{2,1,0:T(8,128)(2,1)S(1)} %get-tuple-element.38), channel_id=1, source_target_pairs={{0,28},{4,0},{8,4},{12,8},{16,12},{20,16},{24,20},{28,24},{32,60},... | collective-permute-start | bytes 983048 | tf_op jit(solution)/shard_map/ppermute | solution.py:204
  118.8 1.9 collective-permute-start.9
  120.7 14.5 %collective-permute-done.9.across_ref = bf16[640,128]{1,0:T(8,128)(2,1)S(1)} collective-permute-done((bf16[640,128]{1,0:T(8,128)(2,1)S(1)}, bf16[640,128]{1,0:T(8,128)(2,1)S(1)}, u32[]{:S(2)}, u32[]{:S(2)}) %collective-permute-start.9) | collective-permute-done | bytes 163872 | tf_op jit(solution)/shard_map/ppermute | solution.py:204
  135.2 0.7 copy-done.10
  135.8 1.0 copy-done.9
  136.8 0.8 shard_map.124
  137.6 0.0 all-gather.5.cloned.1.call-update
  137.6 0.9 copy-done.11
  138.5 4.2 %shard_map.123 = bf16[640,512]{1,0:T(8,128)(2,1)} custom-call(s32[8]{0:T(128)S(1)} %and_select_fusion.place_ref, bf16[640,128]{1,0:T(8,128)(2,1)S(1)} %shard_map.121.own_ref, bf16[640,128]{1,0:T(8,128)(2,1)S(1)} %collective-permute-done.5.low_ref, bf16[640,128]{1,0:T(8,128)(2,1)S(1)} %collective-permute-done.6.high_ref, ...), custom_call_target="tpu_custom_call" | custom-call | flops 1342177280 | bytes 6684704 | tf_op jit(solution)/shard_map/pallas_call | solution.py:25
  142.7 6.3 %all-to-all-start.2 = ((bf16[16,40,512]{2,1,0:T(8,128)(2,1)}), bf16[16,40,512]{2,1,0:T(8,128)(2,1)S(1)}, u32[]{:S(2)}, u32[]{:S(2)}) async-start(bf16[16,40,512]{2,1,0:T(8,128)(2,1)} %bitcast.24), calls=%async_computation.2 | async-start | bytes 1310720 | tf_op jit(solution)/shard_map/all_to_all | solution.py:214
  149.0 25.8 %all-gather.5.cloned.1.call-done = bf16[5120,128]{1,0:T(8,128)(2,1)} async-done(((bf16[640,128]{1,0:T(8,128)(2,1)}), bf16[5120,128]{1,0:T(8,128)(2,1)}) %all-gather.5.cloned.1.call-update) | async-done | bytes 1310736 | tf_op jit(solution)/shard_map/all_gather | solution.py:310
  174.8 1.3 copy-done.1
  176.1 1.2 copy-done.5
  177.3 1.7 shard_map.125
  179.0 11.2 %all-to-all-start.3 = ((bf16[16,40,512]{2,1,0:T(8,128)(2,1)}), bf16[16,40,512]{2,1,0:T(8,128)(2,1)S(1)}, u32[]{:S(2)}, u32[]{:S(2)}) async-start(bf16[16,40,512]{2,1,0:T(8,128)(2,1)} %bitcast.29), calls=%async_computation.4 | async-start | bytes 1310720 | tf_op jit(solution)/shard_map/all_to_all | solution.py:214
  190.2 0.3 shard_map.127
  190.5 1.3 collective-permute-start.10
  191.8 5.7 %collective-permute-done.10 = bf16[1,128,512]{2,1,0:T(8,128)(2,1)S(1)} collective-permute-done((bf16[1,128,512]{2,1,0:T(8,128)(2,1)S(1)}, bf16[1,128,512]{2,1,0:T(8,128)(2,1)S(1)}, u32[]{:S(2)}, u32[]{:S(2)}) %collective-permute-start.10) | collective-permute-done | bytes 131104 | tf_op jit(solution)/shard_map/ppermute | solution.py:210
  197.5 12.8 %all-to-all-done.3 = bf16[16,40,512]{2,1,0:T(8,128)(2,1)S(1)} async-done(((bf16[16,40,512]{2,1,0:T(8,128)(2,1)}), bf16[16,40,512]{2,1,0:T(8,128)(2,1)S(1)}, u32[]{:S(2)}, u32[]{:S(2)}) %all-to-all-start.3) | async-done | bytes 655392 | tf_op jit(solution)/shard_map/all_to_all | solution.py:214
  210.3 1.0 shard_map.126
  211.3 0.7 copy.17
  (35 shorter events, 0.1 us)
Async XLA Ops:
  7.2 65.5 %all-gather.3.cloned.1.call-start = ((), (), s32[]{:S(2)}) async-start(), calls=%async_computation.5 | async-start | bytes 2949120 | tf_op jit(solution)/shard_map/all_gather | solution.py:273
  7.2 1.0 copy-start.8
  9.2 0.9 copy-start.12
  10.1 0.7 copy-start.14
  10.8 0.7 copy-start.16
  12.8 30.3 %all-to-all-start = ((bf16[16,40,512]{2,1,0:T(8,128)(2,1)}), bf16[16,40,512]{2,1,0:T(8,128)(2,1)S(1)}, u32[]{:S(2)}, u32[]{:S(2)}) async-start(bf16[16,40,512]{2,1,0:T(8,128)(2,1)} %bitcast.5), calls=%async_computation | async-start | bytes 1310720 | tf_op jit(solution)/shard_map/all_to_all | solution.py:214
  23.0 2.3 %copy-start.15 = (s32[1,128,4]{1,2,0:T(4,128)S(1)}, s32[1,128,4]{1,2,0:T(4,128)}, u32[]{:S(2)}) copy-start(s32[1,128,4]{1,2,0:T(4,128)} %param.12) | copy-start | bytes 6148
  23.0 2.3 %copy-start.17 = (f32[1,128,4]{1,2,0:T(4,128)S(1)}, f32[1,128,4]{1,2,0:T(4,128)}, u32[]{:S(2)}) copy-start(f32[1,128,4]{1,2,0:T(4,128)} %param.14) | copy-start | bytes 6148
  23.0 2.6 %copy-start.18 = (s32[1,128,4]{1,2,0:T(4,128)S(1)}, s32[1,128,4]{1,2,0:T(4,128)}, u32[]{:S(2)}) copy-start(s32[1,128,4]{1,2,0:T(4,128)} %param.13) | copy-start | bytes 6148
  23.0 2.6 %copy-start.19 = (f32[1,128,4]{1,2,0:T(4,128)S(1)}, f32[1,128,4]{1,2,0:T(4,128)}, u32[]{:S(2)}) copy-start(f32[1,128,4]{1,2,0:T(4,128)} %param.15) | copy-start | bytes 6148
  23.1 3.6 %copy-start.13 = (bf16[1,128,512]{2,1,0:T(8,128)(2,1)S(1)}, bf16[1,128,512]{2,1,0:T(8,128)(2,1)}, u32[]{:S(2)}) copy-start(bf16[1,128,512]{2,1,0:T(8,128)(2,1)} %param.10) | copy-start | bytes 393220
  25.3 22.1 %copy-start.20 = (s32[8]{0:T(128)S(1)}, s32[8]{0:T(128)}, u32[]{:S(2)}) copy-start(s32[8]{0:T(128)} %constant.41.clone) | copy-start | bytes 100
  26.0 0.7 copy-start.2
  43.1 0.8 copy-start.6
  43.9 23.1 %all-to-all-start.1 = ((bf16[16,40,512]{2,1,0:T(8,128)(2,1)}), bf16[16,40,512]{2,1,0:T(8,128)(2,1)S(1)}, u32[]{:S(2)}, u32[]{:S(2)}) async-start(bf16[16,40,512]{2,1,0:T(8,128)(2,1)} %bitcast.19), calls=%async_computation.1 | async-start | bytes 1310720 | tf_op jit(solution)/shard_map/all_to_all | solution.py:214
  47.4 88.4 %reduce-scatter.2.cloned.1.call-start = ((), (), s32[]{:S(2)}) async-start(), calls=%async_computation.6 | async-start | bytes 2949120 | tf_op jit(solution)/shard_map/reduce_scatter | solution.py:295
  47.5 1.2 copy-start.4
  48.7 1.1 copy-start.7
  51.9 20.8 %collective-permute-start = (bf16[2,640,128]{2,1,0:T(8,128)(2,1)}, bf16[2,640,128]{2,1,0:T(8,128)(2,1)}, u32[]{:S(2)}, u32[]{:S(2)}) collective-permute-start(bf16[2,640,128]{2,1,0:T(8,128)(2,1)} %get-tuple-element.27), channel_id=1, source_target_pairs={{0,4},{4,8},{8,12},{12,16},{16,20},{20,24},{24,28},{28,0},{32,36},... | collective-permute-start | bytes 983048 | tf_op jit(solution)/shard_map/ppermute | solution.py:204
  54.2 18.5 %collective-permute-start.1 = (bf16[2,640,128]{2,1,0:T(8,128)(2,1)}, bf16[2,640,128]{2,1,0:T(8,128)(2,1)}, u32[]{:S(2)}, u32[]{:S(2)}) collective-permute-start(bf16[2,640,128]{2,1,0:T(8,128)(2,1)} %get-tuple-element.28), channel_id=1, source_target_pairs={{0,28},{4,0},{8,4},{12,8},{16,12},{20,16},{24,20},{28,24},{32,60},... | collective-permute-start | bytes 983048 | tf_op jit(solution)/shard_map/ppermute | solution.py:204
  62.8 9.9 %collective-permute-start.2 = (bf16[640,128]{1,0:T(8,128)(2,1)}, bf16[640,128]{1,0:T(8,128)(2,1)}, u32[]{:S(2)}, u32[]{:S(2)}) collective-permute-start(bf16[640,128]{1,0:T(8,128)(2,1)} %get-tuple-element.29), channel_id=1, source_target_pairs={{0,24},{4,28},{8,0},{12,4},{16,8},{20,12},{24,16},{28,20},{32,40},... | collective-permute-start | bytes 491528 | tf_op jit(solution)/shard_map/ppermute | solution.py:204
  69.3 1.5 copy-start
  72.7 102.0 %all-gather.5.cloned.1.call-start = ((), (), s32[]{:S(2)}) async-start(), calls=%async_computation.7 | async-start | bytes 1474560 | tf_op jit(solution)/shard_map/all_gather | solution.py:310
  74.0 14.3 %collective-permute-start.3 = (bf16[640,128]{1,0:T(8,128)(2,1)S(1)}, bf16[640,128]{1,0:T(8,128)(2,1)S(1)}, u32[]{:S(2)}, u32[]{:S(2)}) collective-permute-start(bf16[640,128]{1,0:T(8,128)(2,1)S(1)} %get-tuple-element.35), channel_id=1, source_target_pairs={{0,8},{4,12},{8,16},{12,20},{16,24},{20,28},{24,0},{28,4},{32,40},... | collective-permute-start | bytes 491528 | tf_op jit(solution)/shard_map/ppermute | solution.py:204
  76.3 14.1 %collective-permute-start.4 = (bf16[640,128]{1,0:T(8,128)(2,1)S(1)}, bf16[640,128]{1,0:T(8,128)(2,1)S(1)}, u32[]{:S(2)}, u32[]{:S(2)}) collective-permute-start(bf16[640,128]{1,0:T(8,128)(2,1)S(1)} %get-tuple-element.36), channel_id=1, source_target_pairs={{0,24},{4,28},{8,0},{12,4},{16,8},{20,12},{24,16},{28,20},{32,56},... | collective-permute-start | bytes 491528 | tf_op jit(solution)/shard_map/ppermute | solution.py:204
  91.6 14.6 %collective-permute-start.5 = (bf16[640,128]{1,0:T(8,128)(2,1)S(1)}, bf16[640,128]{1,0:T(8,128)(2,1)S(1)}, u32[]{:S(2)}, u32[]{:S(2)}) collective-permute-start(bf16[640,128]{1,0:T(8,128)(2,1)S(1)} %shard_map.121.own_ref), channel_id=1, source_target_pairs={{0,8},{4,12},{8,16},{12,20},{16,24},{20,28},{24,0},{28,4},{32,40},... | collective-permute-start | bytes 491528 | tf_op jit(solution)/shard_map/ppermute | solution.py:204
  97.0 15.1 %collective-permute-start.6 = (bf16[640,128]{1,0:T(8,128)(2,1)S(1)}, bf16[640,128]{1,0:T(8,128)(2,1)S(1)}, u32[]{:S(2)}, u32[]{:S(2)}) collective-permute-start(bf16[640,128]{1,0:T(8,128)(2,1)S(1)} %shard_map.121.own_ref), channel_id=1, source_target_pairs={{0,24},{4,28},{8,0},{12,4},{16,8},{20,12},{24,16},{28,20},{32,56},... | collective-permute-start | bytes 491528 | tf_op jit(solution)/shard_map/ppermute | solution.py:204
  112.3 23.6 %collective-permute-start.7 = (bf16[2,640,128]{2,1,0:T(8,128)(2,1)S(1)}, bf16[2,640,128]{2,1,0:T(8,128)(2,1)S(1)}, u32[]{:S(2)}, u32[]{:S(2)}) collective-permute-start(bf16[2,640,128]{2,1,0:T(8,128)(2,1)S(1)} %get-tuple-element.37), channel_id=1, source_target_pairs={{0,4},{4,8},{8,12},{12,16},{16,20},{20,24},{24,28},{28,0},{32,36},... | collective-permute-start | bytes 983048 | tf_op jit(solution)/shard_map/ppermute | solution.py:204
  114.2 21.6 %collective-permute-start.8 = (bf16[2,640,128]{2,1,0:T(8,128)(2,1)S(1)}, bf16[2,640,128]{2,1,0:T(8,128)(2,1)S(1)}, u32[]{:S(2)}, u32[]{:S(2)}) collective-permute-start(bf16[2,640,128]{2,1,0:T(8,128)(2,1)S(1)} %get-tuple-element.38), channel_id=1, source_target_pairs={{0,28},{4,0},{8,4},{12,8},{16,12},{20,16},{24,20},{28,24},{32,60},... | collective-permute-start | bytes 983048 | tf_op jit(solution)/shard_map/ppermute | solution.py:204
  118.8 16.4 %collective-permute-start.9 = (bf16[640,128]{1,0:T(8,128)(2,1)S(1)}, bf16[640,128]{1,0:T(8,128)(2,1)S(1)}, u32[]{:S(2)}, u32[]{:S(2)}) collective-permute-start(bf16[640,128]{1,0:T(8,128)(2,1)S(1)} %get-tuple-element.39), channel_id=1, source_target_pairs={{0,8},{4,12},{8,16},{12,20},{16,24},{20,28},{24,0},{28,4},{32,56},... | collective-permute-start | bytes 491528 | tf_op jit(solution)/shard_map/ppermute | solution.py:204
  135.2 0.7 copy-start.10
  135.8 1.0 copy-start.9
  137.6 0.9 copy-start.11
  142.7 36.3 %all-to-all-start.2 = ((bf16[16,40,512]{2,1,0:T(8,128)(2,1)}), bf16[16,40,512]{2,1,0:T(8,128)(2,1)S(1)}, u32[]{:S(2)}, u32[]{:S(2)}) async-start(bf16[16,40,512]{2,1,0:T(8,128)(2,1)} %bitcast.24), calls=%async_computation.2 | async-start | bytes 1310720 | tf_op jit(solution)/shard_map/all_to_all | solution.py:214
  174.8 1.3 copy-start.1
  176.1 1.2 copy-start.5
  177.3 33.0 %copy-start.3 = (bf16[2,128,640]{2,1,0:T(8,128)(2,1)S(1)}, bf16[2,128,640]{2,1,0:T(8,128)(2,1)}, u32[]{:S(2)}) copy-start(bf16[2,128,640]{2,1,0:T(8,128)(2,1)} %copy-done.2) | copy-start | bytes 983044
  179.0 31.3 %all-to-all-start.3 = ((bf16[16,40,512]{2,1,0:T(8,128)(2,1)}), bf16[16,40,512]{2,1,0:T(8,128)(2,1)S(1)}, u32[]{:S(2)}, u32[]{:S(2)}) async-start(bf16[16,40,512]{2,1,0:T(8,128)(2,1)} %bitcast.29), calls=%async_computation.4 | async-start | bytes 1310720 | tf_op jit(solution)/shard_map/all_to_all | solution.py:214
  190.5 7.0 %collective-permute-start.10 = (bf16[1,128,512]{2,1,0:T(8,128)(2,1)S(1)}, bf16[1,128,512]{2,1,0:T(8,128)(2,1)S(1)}, u32[]{:S(2)}, u32[]{:S(2)}) collective-permute-start(bf16[1,128,512]{2,1,0:T(8,128)(2,1)S(1)} %bitcast.50), channel_id=1, source_target_pairs={{1,0},{2,1},{3,2},{5,4},{6,5},{7,6},{9,8},{10,9},{11,10},{13,12},{... | collective-permute-start | bytes 393224 | tf_op jit(solution)/shard_map/ppermute | solution.py:210
Sparse Core Ops, SparseCore 0:
  10.1 47.9 all-gather.2
  72.8 57.4 reduce-scatter.1
  137.7 36.9 all-gather.4

commit v3 on v2

--- a/solution.py
+++ b/solution.py
@@ -13,12 +13,12 @@
 LOCAL_ORDER = (3, 1, -3, -1, 4, 0, 2, -2)
 
 
-def call(kernel, outs, args, flops=0, grid=None, in_specs=None, out_specs=None, scratch=(), scalars=False):
+def call(kernel, outs, args, flops=0, in_specs=None, out_specs=None, scratch=(), scalars=False):
     moved = sum(a.size * a.dtype.itemsize for a in args)
     moved += sum(o.size * o.dtype.itemsize for o in jax.tree.leaves(outs))
     extra = {}
-    if grid is not None:
-        extra = dict(grid=grid, in_specs=in_specs, out_specs=out_specs)
+    if in_specs is not None:
+        extra = dict(in_specs=in_specs, out_specs=out_specs)
     elif scalars:
         smem, vmem = pl.BlockSpec(memory_space=pltpu.SMEM), pl.BlockSpec(memory_space=pltpu.VMEM)
         extra = dict(in_specs=[smem] + [vmem] * (len(args) - 1))
@@ -63,7 +63,15 @@
     return jnp.concatenate(rows, axis=0), jnp.concatenate(gated, axis=0)
 
 
-def dispatch_kernel(experts, cap, gate_rows, ids_ref, gates_ref, x_ref, out_ref):
+def dispatch_kernel(experts, cap, gate_rows, ids_from, gates_from, x_from, out_ref, ids_ref, gates_ref, x_ref, sems):
+    copies = [
+        pltpu.make_async_copy(source, target, sems.at[i])
+        for i, (source, target) in enumerate([(ids_from, ids_ref), (gates_from, gates_ref), (x_from, x_ref)])
+    ]
+    for copy in copies:
+        copy.start()
+    for copy in copies:
+        copy.wait()
     rows, gated = slot_table(ids_ref, gates_ref, experts, cap)
     picked = dot(rows.astype(BF), x_ref[...], 1, 0)
     if gate_rows:
@@ -93,13 +101,19 @@
     return [ahead_ref.at[0], ahead_ref.at[1], behind_ref.at[0], behind_ref.at[1], across_ref, *[own_ref.at[i] for i in range(3)]]
 
 
-def up_kernel(x_ref, w_ref, out_ref):
-    count = out_ref.shape[0]
+def up_kernel(x_ref, w_ref, out_ref, held, sems):
+    count, unit = held.shape[0], held.shape[-1]
+    copies = []
     for j in range(count):
-        w = jnp.concatenate([w_ref[0, :, 128 * j : 128 * j + 128], w_ref[1, :, 128 * j : 128 * j + 128]], axis=1)
+        w = jnp.concatenate([w_ref[g, :, unit * j : unit * (j + 1)] for g in range(2)], axis=1)
         part = dot(x_ref[...], w, 1, 0).astype(BF)
-        out_ref[j, 0] = part[:, :128]
-        out_ref[j, 1] = part[:, 128:]
+        held[j, 0] = part[:, :unit]
+        held[j, 1] = part[:, unit:]
+        copy = pltpu.make_async_copy(held.at[j], out_ref.at[j], sems.at[j])
+        copy.start()
+        copies.append(copy)
+    for copy in copies:
+        copy.wait()
 
 
 def grad_hidden_kernel(place_ref, x_ref, w_ref, *out_refs):
@@ -231,6 +245,9 @@
             shape((slots, width)),
             (ids, gates, x),
             flops=2 * slots * tokens * width,
+            in_specs=[pl.BlockSpec(memory_space=pl.ANY)] * 3,
+            out_specs=pl.BlockSpec(memory_space=pltpu.VMEM),
+            scratch=[pltpu.VMEM(a.shape, a.dtype) for a in (ids, gates, x)] + [pltpu.SemaphoreType.DMA((3,))],
         )
 
     def combine_table(ids, gates, gate_rows):
@@ -267,7 +284,8 @@
     send_a = dispatch(ids_a, gate_a, grads_a[0], True)
     rows_a = exchange(send_a, "node")
     send_b = dispatch(ids_b, gate_b, inputs_b[0], False)
-    slope = call(slope_kernel, shape((2, slots, units)), (saved_a[0, 0],), flops=10**6)
+    send_a, saved = lax.optimization_barrier((send_a, saved_a))
+    slope = call(slope_kernel, shape((2, slots, units)), (saved[0, 0],), flops=10**6)
     table_a = combine_table(ids_a, gate_a, True)
     table_b = combine_table(ids_b, gate_b, False)
     slopes = lax.all_gather(slope, "local", axis=0, tiled=True).reshape(locals_, 2, slots, units)
@@ -277,18 +295,15 @@
     across = rotated(across, -2, True)
     ahead = rotated(ahead, 1)
     behind = rotated(behind, -1)
-    half = 2
+    spec = pl.BlockSpec(memory_space=pltpu.VMEM)
     part_b = call(
         up_kernel,
         shape((locals_, 2, slots, units)),
         (rows_b, w_in),
         flops=4 * slots * width * units * locals_,
-        grid=(locals_ // half,),
-        in_specs=[
-            pl.BlockSpec((slots, width), lambda i: (0, 0)),
-            pl.BlockSpec((2, width, half * units), lambda i: (0, 0, i)),
-        ],
-        out_specs=pl.BlockSpec((half, 2, slots, units), lambda i: (i, 0, 0, 0)),
+        in_specs=[spec, spec],
+        out_specs=pl.BlockSpec(memory_space=pltpu.HBM),
+        scratch=[pltpu.VMEM((locals_, 2, slots, units), BF), pltpu.SemaphoreType.DMA((locals_,))],
     )
     ahead, behind, across, part_b, slopes = lax.optimization_barrier((ahead, behind, across, part_b, slopes))
     plus, minus = relay_sum(own, ahead, behind, across)

time: 220 us -> 220 us (level)
  Pallas kernels: 19.1 us -> 21.9 us
    pallas_call x15, Pallas kernels: 19.1 us -> 21.9 us  [call(): pl.pallas_call(kernel, out_shape=outs, scratch_shapes=scratch, compiler_p...]
    all_to_all x4, starting transfers between devices: 31.3 us -> 28.8 us  [exchange(): return lax.all_to_all(value, axis, split_axis=0, concat_axis=0, tiled=True)]
  transfers between devices with their start and end apart: 18 -> 18, of which waited for: 11 -> 10; matrix products, arithmetic and copies ran while one was open for 1% -> 1% of each run, Pallas kernels for 7% -> 8%
where the time goes in v3:
time: 220 us; the launch traced here: 219 us
  waiting for transfers between devices  96.4 us (44%)
  starting transfers between devices  70 us (32%)
  Pallas kernels  21.9 us (10%)
  local copies, waits for them, and re-layouts  16.6 us (8%)
  between operations  14.1 us (6%)
    ppermute x10, starting transfers between devices, rotated(): return lax.ppermute(value, ('node', 'local'), pairs)  39.7 us
    ppermute x10, waiting for transfers between devices, rotated(): return lax.ppermute(value, ('node', 'local'), pairs)  35.4 us
    all_to_all x4, waiting for transfers between devices, exchange(): return lax.all_to_all(value, axis, split_axis=0, concat_axis=0, tiled=True)  29.9 us
    all_to_all x4, starting transfers between devices, exchange(): return lax.all_to_all(value, axis, split_axis=0, concat_axis=0, tiled=True)  28.8 us
    all_gather x1, waiting for transfers between devices, body(): lax.all_gather(hidden, 'local', axis=0, tiled=True)  25.4 us
    pallas_call x15, Pallas kernels, call(): pl.pallas_call(kernel, out_shape=outs, scratch_shapes=scratch, compiler_p...  21.9 us
    unnamed x44, local copies, waits for them, and re-layouts  16.6 us
    ppermute x1, waiting for transfers between devices, shifted(): lax.ppermute(value, axis, [(source, source + steps) for source in range(f...  5.65 us
  transfers between devices with their start and end apart: 18, of which 10 were waited for; matrix products, arithmetic and copies ran while one was open for 1% of the time, Pallas kernels for 8%

profile of v3, /device:TPU:1, one launch (start us, length us, event | category | flops | bytes accessed | tf_op | source)
XLA Modules:
  0.0 219.0 jit_solution(9766995080039345812)
XLA Ops:
  7.2 0.0 all-gather.3.cloned.1.call-start
  7.2 0.9 copy-done.12
  8.1 0.7 copy-done.14
  8.8 0.7 copy-done.16
  9.5 1.5 shard_map.113
  11.0 1.0 copy-done.8
  11.9 1.0 shard_map.119
  12.9 0.0 all-gather.3.cloned.1.call-update
  12.9 10.3 %all-to-all-start = ((bf16[16,40,512]{2,1,0:T(8,128)(2,1)}), bf16[16,40,512]{2,1,0:T(8,128)(2,1)S(1)}, u32[]{:S(2)}, u32[]{:S(2)}) async-start(bf16[16,40,512]{2,1,0:T(8,128)(2,1)} %bitcast.5), calls=%async_computation | async-start | bytes 1310720 | tf_op jit(solution)/shard_map/all_to_all | solution.py:228
  23.3 2.2 %copy.15 = bf16[1,1,512,2,1024]{4,2,3,1,0:T(8,128)(2,1)S(1)} copy(bf16[1,1,512,2,1024]{4,3,2,1,0:T(2,128)(2,1)} %param.16) | data formatting | bytes 4194304 | tf_op args[6]
  25.5 0.0 copy-start.20
  25.6 0.3 shard_map.115.table_ref
  25.9 0.3 shard_map.116.table_ref
  26.2 0.7 copy-done.2
  26.9 1.5 shard_map.114
  28.4 14.9 %all-to-all-done = bf16[16,40,512]{2,1,0:T(8,128)(2,1)S(1)} async-done(((bf16[16,40,512]{2,1,0:T(8,128)(2,1)}), bf16[16,40,512]{2,1,0:T(8,128)(2,1)S(1)}, u32[]{:S(2)}, u32[]{:S(2)}) %all-to-all-start) | async-done | bytes 655392 | tf_op jit(solution)/shard_map/all_to_all | solution.py:228
  43.3 0.8 copy-done.6
  44.1 3.5 %all-to-all-start.1 = ((bf16[16,40,512]{2,1,0:T(8,128)(2,1)}), bf16[16,40,512]{2,1,0:T(8,128)(2,1)S(1)}, u32[]{:S(2)}, u32[]{:S(2)}) async-start(bf16[16,40,512]{2,1,0:T(8,128)(2,1)} %bitcast.19), calls=%async_computation.1 | async-start | bytes 1310720 | tf_op jit(solution)/shard_map/all_to_all | solution.py:228
  47.6 0.0 reduce-scatter.2.cloned.1.call-start
  47.7 1.2 copy-done.4
  48.9 1.1 copy-done.7
  50.0 2.1 shard_map.117
  52.1 2.3 %collective-permute-start = (bf16[2,640,128]{2,1,0:T(8,128)(2,1)}, bf16[2,640,128]{2,1,0:T(8,128)(2,1)}, u32[]{:S(2)}, u32[]{:S(2)}) collective-permute-start(bf16[2,640,128]{2,1,0:T(8,128)(2,1)} %get-tuple-element.28), channel_id=1, source_target_pairs={{0,4},{4,8},{8,12},{12,16},{16,20},{20,24},{24,28},{28,0},{32,36},... | collective-permute-start | bytes 983048 | tf_op jit(solution)/shard_map/ppermute | solution.py:218
  54.4 8.6 %collective-permute-start.1 = (bf16[2,640,128]{2,1,0:T(8,128)(2,1)}, bf16[2,640,128]{2,1,0:T(8,128)(2,1)}, u32[]{:S(2)}, u32[]{:S(2)}) collective-permute-start(bf16[2,640,128]{2,1,0:T(8,128)(2,1)} %get-tuple-element.29), channel_id=1, source_target_pairs={{0,28},{4,0},{8,4},{12,8},{16,12},{20,16},{24,20},{28,24},{32,60},... | collective-permute-start | bytes 983048 | tf_op jit(solution)/shard_map/ppermute | solution.py:218
  63.0 1.9 collective-permute-start.2
  65.0 2.2 %all-to-all-done.1 = bf16[16,40,512]{2,1,0:T(8,128)(2,1)S(1)} async-done(((bf16[16,40,512]{2,1,0:T(8,128)(2,1)}), bf16[16,40,512]{2,1,0:T(8,128)(2,1)S(1)}, u32[]{:S(2)}, u32[]{:S(2)}) %all-to-all-start.1) | async-done | bytes 655392 | tf_op jit(solution)/shard_map/all_to_all | solution.py:228
  67.2 4.8 %shard_map.118 = bf16[8,2,640,128]{3,2,1,0:T(8,128)(2,1)S(1)} custom-call(bf16[640,512]{1,0:T(8,128)(2,1)S(1)} %bitcast.41, bf16[2,512,1024]{2,1,0:T(8,128)(2,1)S(1)} %bitcast.36), custom_call_target="tpu_custom_call" | custom-call | flops 1342177280 | bytes 5373952 | tf_op jit(solution)/shard_map/pallas_call | solution.py:25
  72.0 1.5 copy-done
  73.5 0.0 all-gather.3.cloned.1.call-done
  73.5 0.0 reduce-scatter.2.cloned.1.call-update
  73.6 0.0 all-gather.5.cloned.1.call-start
  73.6 1.3 shard_map.120
  74.9 4.1 %collective-permute-start.3 = (bf16[640,128]{1,0:T(8,128)(2,1)S(1)}, bf16[640,128]{1,0:T(8,128)(2,1)S(1)}, u32[]{:S(2)}, u32[]{:S(2)}) collective-permute-start(bf16[640,128]{1,0:T(8,128)(2,1)S(1)} %get-tuple-element.37), channel_id=1, source_target_pairs={{0,8},{4,12},{8,16},{12,20},{16,24},{20,28},{24,0},{28,4},{32,40},... | collective-permute-start | bytes 491528 | tf_op jit(solution)/shard_map/ppermute | solution.py:218
  79.0 6.8 %collective-permute-start.4 = (bf16[640,128]{1,0:T(8,128)(2,1)S(1)}, bf16[640,128]{1,0:T(8,128)(2,1)S(1)}, u32[]{:S(2)}, u32[]{:S(2)}) collective-permute-start(bf16[640,128]{1,0:T(8,128)(2,1)S(1)} %get-tuple-element.38), channel_id=1, source_target_pairs={{0,24},{4,28},{8,0},{12,4},{16,8},{20,12},{24,16},{28,20},{32,56},... | collective-permute-start | bytes 491528 | tf_op jit(solution)/shard_map/ppermute | solution.py:218
  85.8 1.4 collective-permute-done.3.refs_3_
  87.2 9.2 %collective-permute-done.4.refs_4_ = bf16[640,128]{1,0:T(8,128)(2,1)S(1)} collective-permute-done((bf16[640,128]{1,0:T(8,128)(2,1)S(1)}, bf16[640,128]{1,0:T(8,128)(2,1)S(1)}, u32[]{:S(2)}, u32[]{:S(2)}) %collective-permute-start.4) | collective-permute-done | bytes 163872 | tf_op jit(solution)/shard_map/ppermute | solution.py:218
  96.4 1.2 shard_map.121.own_ref
  97.5 3.9 %collective-permute-start.5 = (bf16[640,128]{1,0:T(8,128)(2,1)S(1)}, bf16[640,128]{1,0:T(8,128)(2,1)S(1)}, u32[]{:S(2)}, u32[]{:S(2)}) collective-permute-start(bf16[640,128]{1,0:T(8,128)(2,1)S(1)} %shard_map.121.own_ref), channel_id=1, source_target_pairs={{0,8},{4,12},{8,16},{12,20},{16,24},{20,28},{24,0},{28,4},{32,40},... | collective-permute-start | bytes 491528 | tf_op jit(solution)/shard_map/ppermute | solution.py:218
  101.5 3.4 %collective-permute-start.6 = (bf16[640,128]{1,0:T(8,128)(2,1)S(1)}, bf16[640,128]{1,0:T(8,128)(2,1)S(1)}, u32[]{:S(2)}, u32[]{:S(2)}) collective-permute-start(bf16[640,128]{1,0:T(8,128)(2,1)S(1)} %shard_map.121.own_ref), channel_id=1, source_target_pairs={{0,24},{4,28},{8,0},{12,4},{16,8},{20,12},{24,16},{28,20},{32,56},... | collective-permute-start | bytes 491528 | tf_op jit(solution)/shard_map/ppermute | solution.py:218
  105.0 8.7 %collective-permute-done.5.low_ref = bf16[640,128]{1,0:T(8,128)(2,1)S(1)} collective-permute-done((bf16[640,128]{1,0:T(8,128)(2,1)S(1)}, bf16[640,128]{1,0:T(8,128)(2,1)S(1)}, u32[]{:S(2)}, u32[]{:S(2)}) %collective-permute-start.5) | collective-permute-done | bytes 163872 | tf_op jit(solution)/shard_map/ppermute | solution.py:218
  113.6 3.5 %collective-permute-done.6.high_ref = bf16[640,128]{1,0:T(8,128)(2,1)S(1)} collective-permute-done((bf16[640,128]{1,0:T(8,128)(2,1)S(1)}, bf16[640,128]{1,0:T(8,128)(2,1)S(1)}, u32[]{:S(2)}, u32[]{:S(2)}) %collective-permute-start.6) | collective-permute-done | bytes 163872 | tf_op jit(solution)/shard_map/ppermute | solution.py:218
  117.1 0.1 shard_map.122
  117.2 1.9 collective-permute-start.7
  119.2 4.6 %collective-permute-start.8 = (bf16[2,640,128]{2,1,0:T(8,128)(2,1)S(1)}, bf16[2,640,128]{2,1,0:T(8,128)(2,1)S(1)}, u32[]{:S(2)}, u32[]{:S(2)}) collective-permute-start(bf16[2,640,128]{2,1,0:T(8,128)(2,1)S(1)} %get-tuple-element.40), channel_id=1, source_target_pairs={{0,28},{4,0},{8,4},{12,8},{16,12},{20,16},{24,20},{28,24},{32,60},... | collective-permute-start | bytes 983048 | tf_op jit(solution)/shard_map/ppermute | solution.py:218
  123.7 2.1 collective-permute-start.9
  125.9 12.7 %collective-permute-done.9.across_ref = bf16[640,128]{1,0:T(8,128)(2,1)S(1)} collective-permute-done((bf16[640,128]{1,0:T(8,128)(2,1)S(1)}, bf16[640,128]{1,0:T(8,128)(2,1)S(1)}, u32[]{:S(2)}, u32[]{:S(2)}) %collective-permute-start.9) | collective-permute-done | bytes 163872 | tf_op jit(solution)/shard_map/ppermute | solution.py:218
  138.5 0.7 copy-done.10
  139.2 1.0 copy-done.9
  140.2 0.8 shard_map.124
  141.0 0.0 all-gather.5.cloned.1.call-update
  141.0 0.9 copy-done.11
  141.9 4.2 %shard_map.123 = bf16[640,512]{1,0:T(8,128)(2,1)} custom-call(s32[8]{0:T(128)S(1)} %and_select_fusion.place_ref, bf16[640,128]{1,0:T(8,128)(2,1)S(1)} %shard_map.121.own_ref, bf16[640,128]{1,0:T(8,128)(2,1)S(1)} %collective-permute-done.5.low_ref, bf16[640,128]{1,0:T(8,128)(2,1)S(1)} %collective-permute-done.6.high_ref, ...), custom_call_target="tpu_custom_call" | custom-call | flops 1342177280 | bytes 6684704 | tf_op jit(solution)/shard_map/pallas_call | solution.py:25
  146.1 3.7 %all-to-all-start.2 = ((bf16[16,40,512]{2,1,0:T(8,128)(2,1)}), bf16[16,40,512]{2,1,0:T(8,128)(2,1)S(1)}, u32[]{:S(2)}, u32[]{:S(2)}) async-start(bf16[16,40,512]{2,1,0:T(8,128)(2,1)} %bitcast.24), calls=%async_computation.2 | async-start | bytes 1310720 | tf_op jit(solution)/shard_map/all_to_all | solution.py:228
  149.8 25.4 %all-gather.5.cloned.1.call-done = bf16[5120,128]{1,0:T(8,128)(2,1)} async-done(((bf16[640,128]{1,0:T(8,128)(2,1)}), bf16[5120,128]{1,0:T(8,128)(2,1)}) %all-gather.5.cloned.1.call-update) | async-done | bytes 1310736 | tf_op jit(solution)/shard_map/all_gather | solution.py:325
  175.2 1.3 copy-done.1
  176.5 1.2 copy-done.5
  177.8 1.7 shard_map.125
  179.4 11.4 %all-to-all-start.3 = ((bf16[16,40,512]{2,1,0:T(8,128)(2,1)}), bf16[16,40,512]{2,1,0:T(8,128)(2,1)S(1)}, u32[]{:S(2)}, u32[]{:S(2)}) async-start(bf16[16,40,512]{2,1,0:T(8,128)(2,1)} %bitcast.29), calls=%async_computation.4 | async-start | bytes 1310720 | tf_op jit(solution)/shard_map/all_to_all | solution.py:228
  190.8 0.3 shard_map.127
  191.1 1.3 collective-permute-start.10
  192.4 5.7 %collective-permute-done.10 = bf16[1,128,512]{2,1,0:T(8,128)(2,1)S(1)} collective-permute-done((bf16[1,128,512]{2,1,0:T(8,128)(2,1)S(1)}, bf16[1,128,512]{2,1,0:T(8,128)(2,1)S(1)}, u32[]{:S(2)}, u32[]{:S(2)}) %collective-permute-start.10) | collective-permute-done | bytes 131104 | tf_op jit(solution)/shard_map/ppermute | solution.py:224
  198.0 12.8 %all-to-all-done.3 = bf16[16,40,512]{2,1,0:T(8,128)(2,1)S(1)} async-done(((bf16[16,40,512]{2,1,0:T(8,128)(2,1)}), bf16[16,40,512]{2,1,0:T(8,128)(2,1)S(1)}, u32[]{:S(2)}, u32[]{:S(2)}) %all-to-all-start.3) | async-done | bytes 655392 | tf_op jit(solution)/shard_map/all_to_all | solution.py:228
  210.8 1.0 shard_map.126
  211.9 0.7 copy.17
  (35 shorter events, 0.1 us)
Async XLA Ops:
  7.2 66.4 %all-gather.3.cloned.1.call-start = ((), (), s32[]{:S(2)}) async-start(), calls=%async_computation.5 | async-start | bytes 2949120 | tf_op jit(solution)/shard_map/all_gather | solution.py:291
  7.2 0.9 copy-start.12
  8.1 0.7 copy-start.14
  8.8 0.7 copy-start.16
  11.0 1.0 copy-start.8
  12.9 30.3 %all-to-all-start = ((bf16[16,40,512]{2,1,0:T(8,128)(2,1)}), bf16[16,40,512]{2,1,0:T(8,128)(2,1)S(1)}, u32[]{:S(2)}, u32[]{:S(2)}) async-start(bf16[16,40,512]{2,1,0:T(8,128)(2,1)} %bitcast.5), calls=%async_computation | async-start | bytes 1310720 | tf_op jit(solution)/shard_map/all_to_all | solution.py:228
  23.2 2.3 %copy-start.15 = (s32[1,128,4]{1,2,0:T(4,128)S(1)}, s32[1,128,4]{1,2,0:T(4,128)}, u32[]{:S(2)}) copy-start(s32[1,128,4]{1,2,0:T(4,128)} %param.12) | copy-start | bytes 6148
  23.2 2.3 %copy-start.17 = (f32[1,128,4]{1,2,0:T(4,128)S(1)}, f32[1,128,4]{1,2,0:T(4,128)}, u32[]{:S(2)}) copy-start(f32[1,128,4]{1,2,0:T(4,128)} %param.14) | copy-start | bytes 6148
  23.2 2.6 %copy-start.18 = (s32[1,128,4]{1,2,0:T(4,128)S(1)}, s32[1,128,4]{1,2,0:T(4,128)}, u32[]{:S(2)}) copy-start(s32[1,128,4]{1,2,0:T(4,128)} %param.13) | copy-start | bytes 6148
  23.3 2.6 %copy-start.19 = (f32[1,128,4]{1,2,0:T(4,128)S(1)}, f32[1,128,4]{1,2,0:T(4,128)}, u32[]{:S(2)}) copy-start(f32[1,128,4]{1,2,0:T(4,128)} %param.15) | copy-start | bytes 6148
  23.3 3.6 %copy-start.13 = (bf16[1,128,512]{2,1,0:T(8,128)(2,1)S(1)}, bf16[1,128,512]{2,1,0:T(8,128)(2,1)}, u32[]{:S(2)}) copy-start(bf16[1,128,512]{2,1,0:T(8,128)(2,1)} %param.10) | copy-start | bytes 393220
  25.5 22.1 %copy-start.20 = (s32[8]{0:T(128)S(1)}, s32[8]{0:T(128)}, u32[]{:S(2)}) copy-start(s32[8]{0:T(128)} %constant.41.clone) | copy-start | bytes 100
  26.2 0.7 copy-start.2
  43.3 0.8 copy-start.6
  44.1 23.1 %all-to-all-start.1 = ((bf16[16,40,512]{2,1,0:T(8,128)(2,1)}), bf16[16,40,512]{2,1,0:T(8,128)(2,1)S(1)}, u32[]{:S(2)}, u32[]{:S(2)}) async-start(bf16[16,40,512]{2,1,0:T(8,128)(2,1)} %bitcast.19), calls=%async_computation.1 | async-start | bytes 1310720 | tf_op jit(solution)/shard_map/all_to_all | solution.py:228
  47.6 91.6 %reduce-scatter.2.cloned.1.call-start = ((), (), s32[]{:S(2)}) async-start(), calls=%async_computation.6 | async-start | bytes 2949120 | tf_op jit(solution)/shard_map/reduce_scatter | solution.py:310
  47.7 1.2 copy-start.4
  48.9 1.1 copy-start.7
  52.1 21.4 %collective-permute-start = (bf16[2,640,128]{2,1,0:T(8,128)(2,1)}, bf16[2,640,128]{2,1,0:T(8,128)(2,1)}, u32[]{:S(2)}, u32[]{:S(2)}) collective-permute-start(bf16[2,640,128]{2,1,0:T(8,128)(2,1)} %get-tuple-element.28), channel_id=1, source_target_pairs={{0,4},{4,8},{8,12},{12,16},{16,20},{20,24},{24,28},{28,0},{32,36},... | collective-permute-start | bytes 983048 | tf_op jit(solution)/shard_map/ppermute | solution.py:218
  54.4 19.1 %collective-permute-start.1 = (bf16[2,640,128]{2,1,0:T(8,128)(2,1)}, bf16[2,640,128]{2,1,0:T(8,128)(2,1)}, u32[]{:S(2)}, u32[]{:S(2)}) collective-permute-start(bf16[2,640,128]{2,1,0:T(8,128)(2,1)} %get-tuple-element.29), channel_id=1, source_target_pairs={{0,28},{4,0},{8,4},{12,8},{16,12},{20,16},{24,20},{28,24},{32,60},... | collective-permute-start | bytes 983048 | tf_op jit(solution)/shard_map/ppermute | solution.py:218
  63.0 10.5 %collective-permute-start.2 = (bf16[640,128]{1,0:T(8,128)(2,1)}, bf16[640,128]{1,0:T(8,128)(2,1)}, u32[]{:S(2)}, u32[]{:S(2)}) collective-permute-start(bf16[640,128]{1,0:T(8,128)(2,1)} %get-tuple-element.30), channel_id=1, source_target_pairs={{0,24},{4,28},{8,0},{12,4},{16,8},{20,12},{24,16},{28,20},{32,40},... | collective-permute-start | bytes 491528 | tf_op jit(solution)/shard_map/ppermute | solution.py:218
  72.0 1.5 copy-start
  73.6 101.7 %all-gather.5.cloned.1.call-start = ((), (), s32[]{:S(2)}) async-start(), calls=%async_computation.7 | async-start | bytes 1474560 | tf_op jit(solution)/shard_map/all_gather | solution.py:325
  74.9 12.3 %collective-permute-start.3 = (bf16[640,128]{1,0:T(8,128)(2,1)S(1)}, bf16[640,128]{1,0:T(8,128)(2,1)S(1)}, u32[]{:S(2)}, u32[]{:S(2)}) collective-permute-start(bf16[640,128]{1,0:T(8,128)(2,1)S(1)} %get-tuple-element.37), channel_id=1, source_target_pairs={{0,8},{4,12},{8,16},{12,20},{16,24},{20,28},{24,0},{28,4},{32,40},... | collective-permute-start | bytes 491528 | tf_op jit(solution)/shard_map/ppermute | solution.py:218
  79.0 17.4 %collective-permute-start.4 = (bf16[640,128]{1,0:T(8,128)(2,1)S(1)}, bf16[640,128]{1,0:T(8,128)(2,1)S(1)}, u32[]{:S(2)}, u32[]{:S(2)}) collective-permute-start(bf16[640,128]{1,0:T(8,128)(2,1)S(1)} %get-tuple-element.38), channel_id=1, source_target_pairs={{0,24},{4,28},{8,0},{12,4},{16,8},{20,12},{24,16},{28,20},{32,56},... | collective-permute-start | bytes 491528 | tf_op jit(solution)/shard_map/ppermute | solution.py:218
  97.5 16.1 %collective-permute-start.5 = (bf16[640,128]{1,0:T(8,128)(2,1)S(1)}, bf16[640,128]{1,0:T(8,128)(2,1)S(1)}, u32[]{:S(2)}, u32[]{:S(2)}) collective-permute-start(bf16[640,128]{1,0:T(8,128)(2,1)S(1)} %shard_map.121.own_ref), channel_id=1, source_target_pairs={{0,8},{4,12},{8,16},{12,20},{16,24},{20,28},{24,0},{28,4},{32,40},... | collective-permute-start | bytes 491528 | tf_op jit(solution)/shard_map/ppermute | solution.py:218
  101.5 15.6 %collective-permute-start.6 = (bf16[640,128]{1,0:T(8,128)(2,1)S(1)}, bf16[640,128]{1,0:T(8,128)(2,1)S(1)}, u32[]{:S(2)}, u32[]{:S(2)}) collective-permute-start(bf16[640,128]{1,0:T(8,128)(2,1)S(1)} %shard_map.121.own_ref), channel_id=1, source_target_pairs={{0,24},{4,28},{8,0},{12,4},{16,8},{20,12},{24,16},{28,20},{32,56},... | collective-permute-start | bytes 491528 | tf_op jit(solution)/shard_map/ppermute | solution.py:218
  117.2 22.0 %collective-permute-start.7 = (bf16[2,640,128]{2,1,0:T(8,128)(2,1)S(1)}, bf16[2,640,128]{2,1,0:T(8,128)(2,1)S(1)}, u32[]{:S(2)}, u32[]{:S(2)}) collective-permute-start(bf16[2,640,128]{2,1,0:T(8,128)(2,1)S(1)} %get-tuple-element.39), channel_id=1, source_target_pairs={{0,4},{4,8},{8,12},{12,16},{16,20},{20,24},{24,28},{28,0},{32,36},... | collective-permute-start | bytes 983048 | tf_op jit(solution)/shard_map/ppermute | solution.py:218
  119.2 20.0 %collective-permute-start.8 = (bf16[2,640,128]{2,1,0:T(8,128)(2,1)S(1)}, bf16[2,640,128]{2,1,0:T(8,128)(2,1)S(1)}, u32[]{:S(2)}, u32[]{:S(2)}) collective-permute-start(bf16[2,640,128]{2,1,0:T(8,128)(2,1)S(1)} %get-tuple-element.40), channel_id=1, source_target_pairs={{0,28},{4,0},{8,4},{12,8},{16,12},{20,16},{24,20},{28,24},{32,60},... | collective-permute-start | bytes 983048 | tf_op jit(solution)/shard_map/ppermute | solution.py:218
  123.7 14.8 %collective-permute-start.9 = (bf16[640,128]{1,0:T(8,128)(2,1)S(1)}, bf16[640,128]{1,0:T(8,128)(2,1)S(1)}, u32[]{:S(2)}, u32[]{:S(2)}) collective-permute-start(bf16[640,128]{1,0:T(8,128)(2,1)S(1)} %get-tuple-element.41), channel_id=1, source_target_pairs={{0,8},{4,12},{8,16},{12,20},{16,24},{20,28},{24,0},{28,4},{32,56},... | collective-permute-start | bytes 491528 | tf_op jit(solution)/shard_map/ppermute | solution.py:218
  138.5 0.7 copy-start.10
  139.2 1.0 copy-start.9
  141.0 0.9 copy-start.11
  146.1 33.4 %all-to-all-start.2 = ((bf16[16,40,512]{2,1,0:T(8,128)(2,1)}), bf16[16,40,512]{2,1,0:T(8,128)(2,1)S(1)}, u32[]{:S(2)}, u32[]{:S(2)}) async-start(bf16[16,40,512]{2,1,0:T(8,128)(2,1)} %bitcast.24), calls=%async_computation.2 | async-start | bytes 1310720 | tf_op jit(solution)/shard_map/all_to_all | solution.py:228
  175.2 1.3 copy-start.1
  176.5 1.2 copy-start.5
  177.8 33.1 %copy-start.3 = (bf16[2,128,640]{2,1,0:T(8,128)(2,1)S(1)}, bf16[2,128,640]{2,1,0:T(8,128)(2,1)}, u32[]{:S(2)}) copy-start(bf16[2,128,640]{2,1,0:T(8,128)(2,1)} %copy-done.2) | copy-start | bytes 983044
  179.4 31.4 %all-to-all-start.3 = ((bf16[16,40,512]{2,1,0:T(8,128)(2,1)}), bf16[16,40,512]{2,1,0:T(8,128)(2,1)S(1)}, u32[]{:S(2)}, u32[]{:S(2)}) async-start(bf16[16,40,512]{2,1,0:T(8,128)(2,1)} %bitcast.29), calls=%async_computation.4 | async-start | bytes 1310720 | tf_op jit(solution)/shard_map/all_to_all | solution.py:228
  191.1 7.0 %collective-permute-start.10 = (bf16[1,128,512]{2,1,0:T(8,128)(2,1)S(1)}, bf16[1,128,512]{2,1,0:T(8,128)(2,1)S(1)}, u32[]{:S(2)}, u32[]{:S(2)}) collective-permute-start(bf16[1,128,512]{2,1,0:T(8,128)(2,1)S(1)} %bitcast.50), channel_id=1, source_target_pairs={{1,0},{2,1},{3,2},{5,4},{6,5},{7,6},{9,8},{10,9},{11,10},{13,12},{... | collective-permute-start | bytes 393224 | tf_op jit(solution)/shard_map/ppermute | solution.py:224
Sparse Core Ops, SparseCore 0:
  13.1 50.8 all-gather.2
  73.7 58.1 reduce-scatter.1
  141.1 34.0 all-gather.4

commit v4 on v2

--- a/solution.py
+++ b/solution.py
@@ -10,10 +10,11 @@
 BF = jnp.bfloat16
 F32 = jnp.float32
 VMEM_LIMIT = 48 * 1024 * 1024
+VMEM_WHOLE = 60 * 1024 * 1024
 LOCAL_ORDER = (3, 1, -3, -1, 4, 0, 2, -2)
 
 
-def call(kernel, outs, args, flops=0, grid=None, in_specs=None, out_specs=None, scratch=(), scalars=False):
+def call(kernel, outs, args, flops=0, grid=None, in_specs=None, out_specs=None, scratch=(), scalars=False, limit=VMEM_LIMIT):
     moved = sum(a.size * a.dtype.itemsize for a in args)
     moved += sum(o.size * o.dtype.itemsize for o in jax.tree.leaves(outs))
     extra = {}
@@ -26,7 +27,7 @@
         kernel,
         out_shape=outs,
         scratch_shapes=scratch,
-        compiler_params=pltpu.CompilerParams(vmem_limit_bytes=VMEM_LIMIT),
+        compiler_params=pltpu.CompilerParams(vmem_limit_bytes=limit),
         cost_estimate=pl.CostEstimate(flops=flops, bytes_accessed=moved, transcendentals=0),
         **extra,
     )(*args)
@@ -257,12 +258,13 @@
         kind = shape(across.shape)
         return call(relay_sum_kernel, (kind, kind), (core, own, ahead, behind, across), flops=10**6, scalars=True)
 
-    def gather_local(own):
+    def gather_local(own, other):
         low, high = rotated(own, 2), rotated(own, -2)
         two, one = shape((2,) + own.shape), shape(own.shape)
         ahead, behind, across = call(pack_kernel, (two, two, one), (core, own, low, high), scalars=True)
+        ahead, behind, across, other = lax.optimization_barrier((ahead, behind, across, other))
         across = rotated(across, 2, True)
-        return own, low, high, rotated(ahead, 1), rotated(behind, -1), across
+        return (own, low, high, rotated(ahead, 1), rotated(behind, -1), across), other
 
     send_a = dispatch(ids_a, gate_a, grads_a[0], True)
     rows_a = exchange(send_a, "node")
@@ -271,7 +273,7 @@
     table_a = combine_table(ids_a, gate_a, True)
     table_b = combine_table(ids_b, gate_b, False)
     slopes = lax.all_gather(slope, "local", axis=0, tiled=True).reshape(locals_, 2, slots, units)
-    rows_a, send_b, w_in, table_a, table_b = lax.optimization_barrier((rows_a, send_b, w_in, table_a, table_b))
+    send_b, w_in, table_a, table_b = lax.optimization_barrier((send_b, w_in, table_a, table_b))
     rows_b = exchange(send_b, "node")
     ahead, behind, across, own = partials(grad_hidden_kernel, (slots, units), rows_a, w_out)
     across = rotated(across, -2, True)
@@ -297,8 +299,7 @@
     ).reshape(2, slots, units)
     sums_a = (own, ahead, behind, rotated(plus, 2), rotated(minus, -2))
     grad_hidden = call(grad_sum_kernel, shape((slots, units)), sums_a, flops=10**6)
-    grad_hidden = gather_local(grad_hidden)
-    pre_b, _, _, _ = lax.optimization_barrier((pre_b, *grad_hidden[3:]))
+    grad_hidden, pre_b = gather_local(grad_hidden, pre_b)
     result_a = call(
         input_grad_kernel,
         shape((slots, width)),
@@ -306,10 +307,14 @@
         flops=4 * slots * width * units * locals_,
         scalars=True,
     )
-    hidden = call(activate_kernel, shape((slots, units)), (pre_b,), flops=10**6)
+    hidden = call(activate_kernel, shape((slots, units)), (pre_b,), flops=10**6, limit=VMEM_WHOLE)
     hidden_all = lax.all_gather(hidden, "local", axis=0, tiled=True).reshape(locals_, slots, units)
     result_b = call(
-        down_kernel, shape((slots, width)), (hidden_all, w_out), flops=2 * slots * width * units * locals_
+        down_kernel,
+        shape((slots, width)),
+        (hidden_all, w_out),
+        flops=2 * slots * width * units * locals_,
+        limit=VMEM_WHOLE,
     )
     returned_a = exchange(result_a, "node")
     returned_a, result_b = lax.optimization_barrier((returned_a, result_b))

time: 220 us -> 210 us (0.955)
  local copies, waits for them, and re-layouts: 16.6 us -> 11.4 us
  waiting for transfers between devices: 97.9 us -> 93.1 us
  Pallas kernels: 19.1 us -> 21.7 us
  starting transfers between devices: 70.8 us -> 68.5 us
    all_gather x1, waiting for transfers between devices: 25.8 us -> 8.84 us  [body(): lax.all_gather(hidden, 'local', axis=0, tiled=True)]
    reduce_scatter x1, waiting for transfers between devices: 0.01 us -> 12.2 us  [body(): lax.psum_scatter(part_b.reshape(locals_, 2 * slots, units), 'local', scat...]
    ppermute x10, waiting for transfers between devices: 36.4 us -> 29.1 us  [rotated(): return lax.ppermute(value, ('node', 'local'), pairs)]
    all_to_all x4, waiting for transfers between devices: 30.1 us -> 37.1 us  [exchange(): return lax.all_to_all(value, axis, split_axis=0, concat_axis=0, tiled=True)]
    unnamed x44 -> x38, local copies, waits for them, and re-layouts: 16.6 us -> 11.4 us
    all_to_all x4, starting transfers between devices: 31.3 us -> 28 us  [exchange(): return lax.all_to_all(value, axis, split_axis=0, concat_axis=0, tiled=True)]
    pallas_call x15, Pallas kernels: 19.1 us -> 21.7 us  [call(): pl.pallas_call(kernel, out_shape=outs, scratch_shapes=scratch, compiler_p...]
  transfers between devices with their start and end apart: 18 -> 18, of which waited for: 11 -> 13; matrix products, arithmetic and copies ran while one was open for 1% -> 1% of each run, Pallas kernels for 7% -> 9%
where the time goes in v4:
time: 210 us; the launch traced here: 209 us
  waiting for transfers between devices  93.1 us (44%)
  starting transfers between devices  68.5 us (33%)
  Pallas kernels  21.7 us (10%)
  between operations  14.1 us (7%)
  local copies, waits for them, and re-layouts  11.4 us (5%)
    ppermute x10, starting transfers between devices, rotated(): return lax.ppermute(value, ('node', 'local'), pairs)  39.1 us
    all_to_all x4, waiting for transfers between devices, exchange(): return lax.all_to_all(value, axis, split_axis=0, concat_axis=0, tiled=True)  37.1 us
    ppermute x10, waiting for transfers between devices, rotated(): return lax.ppermute(value, ('node', 'local'), pairs)  29.1 us
    all_to_all x4, starting transfers between devices, exchange(): return lax.all_to_all(value, axis, split_axis=0, concat_axis=0, tiled=True)  28 us
    pallas_call x15, Pallas kernels, call(): pl.pallas_call(kernel, out_shape=outs, scratch_shapes=scratch, compiler_p...  21.7 us
    reduce_scatter x1, waiting for transfers between devices, body(): lax.psum_scatter(part_b.reshape(locals_, 2 * slots, units), 'local', scat...  12.2 us
    unnamed x38, local copies, waits for them, and re-layouts  11.4 us
    all_gather x1, waiting for transfers between devices, body(): lax.all_gather(hidden, 'local', axis=0, tiled=True)  8.84 us
  transfers between devices with their start and end apart: 18, of which 13 were waited for; matrix products, arithmetic and copies ran while one was open for 1% of the time, Pallas kernels for 9%

profile of v4, /device:TPU:1, one launch (start us, length us, event | category | flops | bytes accessed | tf_op | source)
XLA Modules:
  0.0 208.7 jit_solution(7249201026913796649)
XLA Ops:
  7.2 0.0 all-gather.3.cloned.1.call-start
  7.2 1.0 copy-done.8
  8.2 1.0 shard_map.119
  9.2 0.0 all-gather.3.cloned.1.call-update
  9.2 0.0 copy-start.9
  9.2 0.9 copy-done.9
  10.1 0.7 copy-done.11
  10.8 0.7 copy-done.13
  11.5 1.3 shard_map.116
  12.8 10.3 %all-to-all-start = ((bf16[16,40,512]{2,1,0:T(8,128)(2,1)}), bf16[16,40,512]{2,1,0:T(8,128)(2,1)S(1)}, u32[]{:S(2)}, u32[]{:S(2)}) async-start(bf16[16,40,512]{2,1,0:T(8,128)(2,1)} %bitcast.16), calls=%async_computation | async-start | bytes 1310720 | tf_op jit(solution)/shard_map/all_to_all | solution.py:215
  23.0 0.0 copy-start.14
  23.1 2.2 %copy.15 = bf16[1,1,512,2,1024]{4,2,3,1,0:T(8,128)(2,1)S(1)} copy(bf16[1,1,512,2,1024]{4,3,2,1,0:T(2,128)(2,1)} %param.16) | data formatting | bytes 4194304 | tf_op args[6]
  25.3 0.0 copy-start.17
  25.4 0.3 shard_map.114.table_ref
  25.6 0.7 copy-done.6
  26.3 0.3 shard_map.115.table_ref
  26.6 0.7 copy-done.1
  27.4 1.3 shard_map.113
  28.6 14.4 %all-to-all-done = bf16[16,40,512]{2,1,0:T(8,128)(2,1)S(1)} async-done(((bf16[16,40,512]{2,1,0:T(8,128)(2,1)}), bf16[16,40,512]{2,1,0:T(8,128)(2,1)S(1)}, u32[]{:S(2)}, u32[]{:S(2)}) %all-to-all-start) | async-done | bytes 655392 | tf_op jit(solution)/shard_map/all_to_all | solution.py:215
  43.1 3.5 %all-to-all-start.1 = ((bf16[16,40,512]{2,1,0:T(8,128)(2,1)}), bf16[16,40,512]{2,1,0:T(8,128)(2,1)S(1)}, u32[]{:S(2)}, u32[]{:S(2)}) async-start(bf16[16,40,512]{2,1,0:T(8,128)(2,1)} %bitcast.19), calls=%async_computation.1 | async-start | bytes 1310720 | tf_op jit(solution)/shard_map/all_to_all | solution.py:215
  46.6 0.0 reduce-scatter.2.cloned.1.call-start
  46.7 1.2 copy-done.3
  47.9 1.1 copy-done.5
  49.0 2.1 %shard_map.117 = (bf16[2,640,128]{2,1,0:T(8,128)(2,1)}, bf16[2,640,128]{2,1,0:T(8,128)(2,1)}, bf16[640,128]{1,0:T(8,128)(2,1)}, bf16[3,640,128]{2,1,0:T(8,128)(2,1)S(1)}) custom-call(s32[8]{0:T(128)S(1)} %and_select_fusion.place_ref, bf16[640,512]{1,0:T(8,128)(2,1)S(1)} %bitcast.44, bf16[1024,512]{1,0:T(8,128)(2,1)S(1)} %bitcast.43), custom_call_target="tpu_custom_call" | custom-call | flops 671088640 | bytes 3014688 | tf_op jit(solution)/shard_map/pallas_call | solution.py:26
  51.1 2.3 %collective-permute-start = (bf16[2,640,128]{2,1,0:T(8,128)(2,1)}, bf16[2,640,128]{2,1,0:T(8,128)(2,1)}, u32[]{:S(2)}, u32[]{:S(2)}) collective-permute-start(bf16[2,640,128]{2,1,0:T(8,128)(2,1)} %get-tuple-element.28), channel_id=1, source_target_pairs={{0,4},{4,8},{8,12},{12,16},{16,20},{20,24},{24,28},{28,0},{32,36},... | collective-permute-start | bytes 983048 | tf_op jit(solution)/shard_map/ppermute | solution.py:205
  53.4 8.6 %collective-permute-start.1 = (bf16[2,640,128]{2,1,0:T(8,128)(2,1)}, bf16[2,640,128]{2,1,0:T(8,128)(2,1)}, u32[]{:S(2)}, u32[]{:S(2)}) collective-permute-start(bf16[2,640,128]{2,1,0:T(8,128)(2,1)} %get-tuple-element.29), channel_id=1, source_target_pairs={{0,28},{4,0},{8,4},{12,8},{16,12},{20,16},{24,20},{28,24},{32,60},... | collective-permute-start | bytes 983048 | tf_op jit(solution)/shard_map/ppermute | solution.py:205
  62.0 1.9 collective-permute-start.2
  64.0 2.2 %all-to-all-done.1 = bf16[16,40,512]{2,1,0:T(8,128)(2,1)S(1)} async-done(((bf16[16,40,512]{2,1,0:T(8,128)(2,1)}), bf16[16,40,512]{2,1,0:T(8,128)(2,1)S(1)}, u32[]{:S(2)}, u32[]{:S(2)}) %all-to-all-start.1) | async-done | bytes 655392 | tf_op jit(solution)/shard_map/all_to_all | solution.py:215
  66.1 2.4 %shard_map.118 = bf16[8,2,640,128]{3,2,1,0:T(8,128)(2,1)S(1)} custom-call(bf16[640,512]{1,0:T(8,128)(2,1)S(1)} %bitcast.41, bf16[2,512,1024]{2,1,0:T(8,128)(2,1)S(1)} %bitcast.36), custom_call_target="tpu_custom_call" | custom-call | flops 1342177280 | bytes 5373952 | tf_op jit(solution)/shard_map/pallas_call | solution.py:26
  68.5 1.5 copy-done
  70.0 2.0 collective-permute-done.2.across_ref
  72.0 0.0 all-gather.3.cloned.1.call-done
  72.0 0.0 reduce-scatter.2.cloned.1.call-update
  72.0 0.0 all-gather.5.cloned.1.call-start
  72.1 1.2 shard_map.120
  73.3 2.1 %collective-permute-start.3 = (bf16[640,128]{1,0:T(8,128)(2,1)S(1)}, bf16[640,128]{1,0:T(8,128)(2,1)S(1)}, u32[]{:S(2)}, u32[]{:S(2)}) collective-permute-start(bf16[640,128]{1,0:T(8,128)(2,1)S(1)} %get-tuple-element.36), channel_id=1, source_target_pairs={{0,8},{4,12},{8,16},{12,20},{16,24},{20,28},{24,0},{28,4},{32,40},... | collective-permute-start | bytes 491528 | tf_op jit(solution)/shard_map/ppermute | solution.py:205
  75.5 6.8 %collective-permute-start.4 = (bf16[640,128]{1,0:T(8,128)(2,1)S(1)}, bf16[640,128]{1,0:T(8,128)(2,1)S(1)}, u32[]{:S(2)}, u32[]{:S(2)}) collective-permute-start(bf16[640,128]{1,0:T(8,128)(2,1)S(1)} %get-tuple-element.37), channel_id=1, source_target_pairs={{0,24},{4,28},{8,0},{12,4},{16,8},{20,12},{24,16},{28,20},{32,56},... | collective-permute-start | bytes 491528 | tf_op jit(solution)/shard_map/ppermute | solution.py:205
  82.3 5.4 %collective-permute-done.3.refs_3_ = bf16[640,128]{1,0:T(8,128)(2,1)S(1)} collective-permute-done((bf16[640,128]{1,0:T(8,128)(2,1)S(1)}, bf16[640,128]{1,0:T(8,128)(2,1)S(1)}, u32[]{:S(2)}, u32[]{:S(2)}) %collective-permute-start.3) | collective-permute-done | bytes 163872 | tf_op jit(solution)/shard_map/ppermute | solution.py:205
  87.6 1.8 collective-permute-done.4.refs_4_
  89.4 1.2 shard_map.121.own_ref
  90.6 5.7 %collective-permute-start.5 = (bf16[640,128]{1,0:T(8,128)(2,1)S(1)}, bf16[640,128]{1,0:T(8,128)(2,1)S(1)}, u32[]{:S(2)}, u32[]{:S(2)}) collective-permute-start(bf16[640,128]{1,0:T(8,128)(2,1)S(1)} %shard_map.121.own_ref), channel_id=1, source_target_pairs={{0,8},{4,12},{8,16},{12,20},{16,24},{20,28},{24,0},{28,4},{32,40},... | collective-permute-start | bytes 491528 | tf_op jit(solution)/shard_map/ppermute | solution.py:205
  96.3 2.2 %collective-permute-start.6 = (bf16[640,128]{1,0:T(8,128)(2,1)S(1)}, bf16[640,128]{1,0:T(8,128)(2,1)S(1)}, u32[]{:S(2)}, u32[]{:S(2)}) collective-permute-start(bf16[640,128]{1,0:T(8,128)(2,1)S(1)} %shard_map.121.own_ref), channel_id=1, source_target_pairs={{0,24},{4,28},{8,0},{12,4},{16,8},{20,12},{24,16},{28,20},{32,56},... | collective-permute-start | bytes 491528 | tf_op jit(solution)/shard_map/ppermute | solution.py:205
  98.6 7.3 %collective-permute-done.5.low_ref = bf16[640,128]{1,0:T(8,128)(2,1)S(1)} collective-permute-done((bf16[640,128]{1,0:T(8,128)(2,1)S(1)}, bf16[640,128]{1,0:T(8,128)(2,1)S(1)}, u32[]{:S(2)}, u32[]{:S(2)}) %collective-permute-start.5) | collective-permute-done | bytes 163872 | tf_op jit(solution)/shard_map/ppermute | solution.py:205
  105.8 5.7 %collective-permute-done.6.high_ref = bf16[640,128]{1,0:T(8,128)(2,1)S(1)} collective-permute-done((bf16[640,128]{1,0:T(8,128)(2,1)S(1)}, bf16[640,128]{1,0:T(8,128)(2,1)S(1)}, u32[]{:S(2)}, u32[]{:S(2)}) %collective-permute-start.6) | collective-permute-done | bytes 163872 | tf_op jit(solution)/shard_map/ppermute | solution.py:205
  111.5 0.1 shard_map.122
  111.7 12.2 %reduce-scatter.2.cloned.1.call-done = bf16[1,1280,128]{2,1,0:T(8,128)(2,1)} async-done(((bf16[8,1280,128]{2,1,0:T(8,128)(2,1)}), bf16[1,1280,128]{2,1,0:T(8,128)(2,1)}) %reduce-scatter.2.cloned.1.call-update) | async-done | bytes 327696 | tf_op jit(solution)/shard_map/reduce_scatter | solution.py:297
  123.9 1.8 shard_map.124
  125.7 0.0 all-gather.5.cloned.1.call-update
  125.7 3.2 %collective-permute-start.7 = (bf16[2,640,128]{2,1,0:T(8,128)(2,1)S(1)}, bf16[2,640,128]{2,1,0:T(8,128)(2,1)S(1)}, u32[]{:S(2)}, u32[]{:S(2)}) collective-permute-start(bf16[2,640,128]{2,1,0:T(8,128)(2,1)S(1)} %get-tuple-element.42), channel_id=1, source_target_pairs={{0,4},{4,8},{8,12},{12,16},{16,20},{20,24},{24,28},{28,0},{32,36},... | collective-permute-start | bytes 983048 | tf_op jit(solution)/shard_map/ppermute | solution.py:205
  128.8 3.3 %collective-permute-start.8 = (bf16[2,640,128]{2,1,0:T(8,128)(2,1)S(1)}, bf16[2,640,128]{2,1,0:T(8,128)(2,1)S(1)}, u32[]{:S(2)}, u32[]{:S(2)}) collective-permute-start(bf16[2,640,128]{2,1,0:T(8,128)(2,1)S(1)} %get-tuple-element.43), channel_id=1, source_target_pairs={{0,28},{4,0},{8,4},{12,8},{16,12},{20,16},{24,20},{28,24},{32,60},... | collective-permute-start | bytes 983048 | tf_op jit(solution)/shard_map/ppermute | solution.py:205
  132.2 2.9 %collective-permute-start.9 = (bf16[640,128]{1,0:T(8,128)(2,1)S(1)}, bf16[640,128]{1,0:T(8,128)(2,1)S(1)}, u32[]{:S(2)}, u32[]{:S(2)}) collective-permute-start(bf16[640,128]{1,0:T(8,128)(2,1)S(1)} %get-tuple-element.44), channel_id=1, source_target_pairs={{0,8},{4,12},{8,16},{12,20},{16,24},{20,28},{24,0},{28,4},{32,56},... | collective-permute-start | bytes 491528 | tf_op jit(solution)/shard_map/ppermute | solution.py:205
  135.1 7.0 %collective-permute-done.9.across_ref = bf16[640,128]{1,0:T(8,128)(2,1)S(1)} collective-permute-done((bf16[640,128]{1,0:T(8,128)(2,1)S(1)}, bf16[640,128]{1,0:T(8,128)(2,1)S(1)}, u32[]{:S(2)}, u32[]{:S(2)}) %collective-permute-start.9) | collective-permute-done | bytes 163872 | tf_op jit(solution)/shard_map/ppermute | solution.py:205
  142.1 4.2 %shard_map.123 = bf16[640,512]{1,0:T(8,128)(2,1)} custom-call(s32[8]{0:T(128)S(1)} %and_select_fusion.place_ref, bf16[640,128]{1,0:T(8,128)(2,1)S(1)} %shard_map.121.own_ref, bf16[640,128]{1,0:T(8,128)(2,1)S(1)} %collective-permute-done.5.low_ref, bf16[640,128]{1,0:T(8,128)(2,1)S(1)} %collective-permute-done.6.high_ref, ...), custom_call_target="tpu_custom_call" | custom-call | flops 1342177280 | bytes 6684704 | tf_op jit(solution)/shard_map/pallas_call | solution.py:26
  146.3 10.7 %all-to-all-start.2 = ((bf16[16,40,512]{2,1,0:T(8,128)(2,1)}), bf16[16,40,512]{2,1,0:T(8,128)(2,1)S(1)}, u32[]{:S(2)}, u32[]{:S(2)}) async-start(bf16[16,40,512]{2,1,0:T(8,128)(2,1)} %bitcast.26), calls=%async_computation.3 | async-start | bytes 1310720 | tf_op jit(solution)/shard_map/all_to_all | solution.py:215
  157.0 8.8 %all-gather.5.cloned.1.call-done = bf16[5120,128]{1,0:T(8,128)(2,1)} async-done(((bf16[640,128]{1,0:T(8,128)(2,1)}), bf16[5120,128]{1,0:T(8,128)(2,1)}) %all-gather.5.cloned.1.call-update) | async-done | bytes 1310736 | tf_op jit(solution)/shard_map/all_gather | solution.py:311
  165.9 3.4 %shard_map.125 = bf16[640,512]{1,0:T(8,128)(2,1)} custom-call(bf16[8,640,128]{2,1,0:T(8,128)(2,1)} %bitcast.59, bf16[1024,512]{1,0:T(8,128)(2,1)} %bitcast.42), custom_call_target="tpu_custom_call" | custom-call | flops 671088640 | bytes 3014656 | tf_op jit(solution)/shard_map/pallas_call | solution.py:26
  169.3 7.8 %all-to-all-done.2 = bf16[16,40,512]{2,1,0:T(8,128)(2,1)S(1)} async-done(((bf16[16,40,512]{2,1,0:T(8,128)(2,1)}), bf16[16,40,512]{2,1,0:T(8,128)(2,1)S(1)}, u32[]{:S(2)}, u32[]{:S(2)}) %all-to-all-start.2) | async-done | bytes 655392 | tf_op jit(solution)/shard_map/all_to_all | solution.py:215
  177.1 3.5 %all-to-all-start.3 = ((bf16[16,40,512]{2,1,0:T(8,128)(2,1)}), bf16[16,40,512]{2,1,0:T(8,128)(2,1)S(1)}, u32[]{:S(2)}, u32[]{:S(2)}) async-start(bf16[16,40,512]{2,1,0:T(8,128)(2,1)} %bitcast.58), calls=%async_computation.4 | async-start | bytes 1310720 | tf_op jit(solution)/shard_map/all_to_all | solution.py:215
  180.6 0.3 shard_map.127
  180.9 1.3 collective-permute-start.10
  182.2 5.7 %collective-permute-done.10 = bf16[1,128,512]{2,1,0:T(8,128)(2,1)S(1)} collective-permute-done((bf16[1,128,512]{2,1,0:T(8,128)(2,1)S(1)}, bf16[1,128,512]{2,1,0:T(8,128)(2,1)S(1)}, u32[]{:S(2)}, u32[]{:S(2)}) %collective-permute-start.10) | collective-permute-done | bytes 131104 | tf_op jit(solution)/shard_map/ppermute | solution.py:211
  187.8 12.7 %all-to-all-done.3 = bf16[16,40,512]{2,1,0:T(8,128)(2,1)S(1)} async-done(((bf16[16,40,512]{2,1,0:T(8,128)(2,1)}), bf16[16,40,512]{2,1,0:T(8,128)(2,1)S(1)}, u32[]{:S(2)}, u32[]{:S(2)}) %all-to-all-start.3) | async-done | bytes 655392 | tf_op jit(solution)/shard_map/all_to_all | solution.py:215
  200.5 1.0 shard_map.126
  201.6 0.7 copy.17
  (29 shorter events, 0.1 us)
Async XLA Ops:
  7.2 64.9 %all-gather.3.cloned.1.call-start = ((), (), s32[]{:S(2)}) async-start(), calls=%async_computation.5 | async-start | bytes 2949120 | tf_op jit(solution)/shard_map/all_gather | solution.py:275
  7.2 1.0 copy-start.8
  9.2 0.9 copy-start.9
  10.1 0.7 copy-start.11
  10.8 0.7 copy-start.13
  12.8 30.3 %all-to-all-start = ((bf16[16,40,512]{2,1,0:T(8,128)(2,1)}), bf16[16,40,512]{2,1,0:T(8,128)(2,1)S(1)}, u32[]{:S(2)}, u32[]{:S(2)}) async-start(bf16[16,40,512]{2,1,0:T(8,128)(2,1)} %bitcast.16), calls=%async_computation | async-start | bytes 1310720 | tf_op jit(solution)/shard_map/all_to_all | solution.py:215
  23.0 2.3 %copy-start.12 = (s32[1,128,4]{1,2,0:T(4,128)S(1)}, s32[1,128,4]{1,2,0:T(4,128)}, u32[]{:S(2)}) copy-start(s32[1,128,4]{1,2,0:T(4,128)} %param.12) | copy-start | bytes 6148
  23.0 2.3 %copy-start.14 = (f32[1,128,4]{1,2,0:T(4,128)S(1)}, f32[1,128,4]{1,2,0:T(4,128)}, u32[]{:S(2)}) copy-start(f32[1,128,4]{1,2,0:T(4,128)} %param.14) | copy-start | bytes 6148
  23.0 3.3 %copy-start.15 = (s32[1,128,4]{1,2,0:T(4,128)S(1)}, s32[1,128,4]{1,2,0:T(4,128)}, u32[]{:S(2)}) copy-start(s32[1,128,4]{1,2,0:T(4,128)} %param.13) | copy-start | bytes 6148
  23.1 3.2 %copy-start.16 = (f32[1,128,4]{1,2,0:T(4,128)S(1)}, f32[1,128,4]{1,2,0:T(4,128)}, u32[]{:S(2)}) copy-start(f32[1,128,4]{1,2,0:T(4,128)} %param.15) | copy-start | bytes 6148
  23.1 4.3 %copy-start.10 = (bf16[1,128,512]{2,1,0:T(8,128)(2,1)S(1)}, bf16[1,128,512]{2,1,0:T(8,128)(2,1)}, u32[]{:S(2)}) copy-start(bf16[1,128,512]{2,1,0:T(8,128)(2,1)} %param.10) | copy-start | bytes 393220
  25.3 21.3 %copy-start.17 = (s32[8]{0:T(128)S(1)}, s32[8]{0:T(128)}, u32[]{:S(2)}) copy-start(s32[8]{0:T(128)} %constant.41.clone) | copy-start | bytes 100
  25.6 0.7 copy-start.6
  26.6 0.7 copy-start.1
  43.1 3.6 %copy-start.4 = (bf16[16,40,512]{2,1,0:T(8,128)(2,1)}, bf16[16,40,512]{2,1,0:T(8,128)(2,1)S(1)}, u32[]{:S(2)}) copy-start(bf16[16,40,512]{2,1,0:T(8,128)(2,1)S(1)} %all-to-all-done) | copy-start | bytes 1966084
  43.1 23.1 %all-to-all-start.1 = ((bf16[16,40,512]{2,1,0:T(8,128)(2,1)}), bf16[16,40,512]{2,1,0:T(8,128)(2,1)S(1)}, u32[]{:S(2)}, u32[]{:S(2)}) async-start(bf16[16,40,512]{2,1,0:T(8,128)(2,1)} %bitcast.19), calls=%async_computation.1 | async-start | bytes 1310720 | tf_op jit(solution)/shard_map/all_to_all | solution.py:215
  46.6 77.3 %reduce-scatter.2.cloned.1.call-start = ((), (), s32[]{:S(2)}) async-start(), calls=%async_computation.6 | async-start | bytes 2949120 | tf_op jit(solution)/shard_map/reduce_scatter | solution.py:297
  46.7 1.2 copy-start.3
  47.9 1.1 copy-start.5
  51.1 20.9 %collective-permute-start = (bf16[2,640,128]{2,1,0:T(8,128)(2,1)}, bf16[2,640,128]{2,1,0:T(8,128)(2,1)}, u32[]{:S(2)}, u32[]{:S(2)}) collective-permute-start(bf16[2,640,128]{2,1,0:T(8,128)(2,1)} %get-tuple-element.28), channel_id=1, source_target_pairs={{0,4},{4,8},{8,12},{12,16},{16,20},{20,24},{24,28},{28,0},{32,36},... | collective-permute-start | bytes 983048 | tf_op jit(solution)/shard_map/ppermute | solution.py:205
  53.4 18.6 %collective-permute-start.1 = (bf16[2,640,128]{2,1,0:T(8,128)(2,1)}, bf16[2,640,128]{2,1,0:T(8,128)(2,1)}, u32[]{:S(2)}, u32[]{:S(2)}) collective-permute-start(bf16[2,640,128]{2,1,0:T(8,128)(2,1)} %get-tuple-element.29), channel_id=1, source_target_pairs={{0,28},{4,0},{8,4},{12,8},{16,12},{20,16},{24,20},{28,24},{32,60},... | collective-permute-start | bytes 983048 | tf_op jit(solution)/shard_map/ppermute | solution.py:205
  62.0 10.0 %collective-permute-start.2 = (bf16[640,128]{1,0:T(8,128)(2,1)}, bf16[640,128]{1,0:T(8,128)(2,1)S(1)}, u32[]{:S(2)}, u32[]{:S(2)}) collective-permute-start(bf16[640,128]{1,0:T(8,128)(2,1)} %get-tuple-element.30), channel_id=1, source_target_pairs={{0,24},{4,28},{8,0},{12,4},{16,8},{20,12},{24,16},{28,20},{32,40},... | collective-permute-start | bytes 491528 | tf_op jit(solution)/shard_map/ppermute | solution.py:205
  68.5 1.5 copy-start
  72.0 93.8 %all-gather.5.cloned.1.call-start = ((), (), s32[]{:S(2)}) async-start(), calls=%async_computation.7 | async-start | bytes 1474560 | tf_op jit(solution)/shard_map/all_gather | solution.py:311
  73.3 14.3 %collective-permute-start.3 = (bf16[640,128]{1,0:T(8,128)(2,1)S(1)}, bf16[640,128]{1,0:T(8,128)(2,1)S(1)}, u32[]{:S(2)}, u32[]{:S(2)}) collective-permute-start(bf16[640,128]{1,0:T(8,128)(2,1)S(1)} %get-tuple-element.36), channel_id=1, source_target_pairs={{0,8},{4,12},{8,16},{12,20},{16,24},{20,28},{24,0},{28,4},{32,40},... | collective-permute-start | bytes 491528 | tf_op jit(solution)/shard_map/ppermute | solution.py:205
  75.5 13.9 %collective-permute-start.4 = (bf16[640,128]{1,0:T(8,128)(2,1)S(1)}, bf16[640,128]{1,0:T(8,128)(2,1)S(1)}, u32[]{:S(2)}, u32[]{:S(2)}) collective-permute-start(bf16[640,128]{1,0:T(8,128)(2,1)S(1)} %get-tuple-element.37), channel_id=1, source_target_pairs={{0,24},{4,28},{8,0},{12,4},{16,8},{20,12},{24,16},{28,20},{32,56},... | collective-permute-start | bytes 491528 | tf_op jit(solution)/shard_map/ppermute | solution.py:205
  90.6 15.2 %collective-permute-start.5 = (bf16[640,128]{1,0:T(8,128)(2,1)S(1)}, bf16[640,128]{1,0:T(8,128)(2,1)S(1)}, u32[]{:S(2)}, u32[]{:S(2)}) collective-permute-start(bf16[640,128]{1,0:T(8,128)(2,1)S(1)} %shard_map.121.own_ref), channel_id=1, source_target_pairs={{0,8},{4,12},{8,16},{12,20},{16,24},{20,28},{24,0},{28,4},{32,40},... | collective-permute-start | bytes 491528 | tf_op jit(solution)/shard_map/ppermute | solution.py:205
  96.3 15.2 %collective-permute-start.6 = (bf16[640,128]{1,0:T(8,128)(2,1)S(1)}, bf16[640,128]{1,0:T(8,128)(2,1)S(1)}, u32[]{:S(2)}, u32[]{:S(2)}) collective-permute-start(bf16[640,128]{1,0:T(8,128)(2,1)S(1)} %shard_map.121.own_ref), channel_id=1, source_target_pairs={{0,24},{4,28},{8,0},{12,4},{16,8},{20,12},{24,16},{28,20},{32,56},... | collective-permute-start | bytes 491528 | tf_op jit(solution)/shard_map/ppermute | solution.py:205
  125.7 16.4 %collective-permute-start.7 = (bf16[2,640,128]{2,1,0:T(8,128)(2,1)S(1)}, bf16[2,640,128]{2,1,0:T(8,128)(2,1)S(1)}, u32[]{:S(2)}, u32[]{:S(2)}) collective-permute-start(bf16[2,640,128]{2,1,0:T(8,128)(2,1)S(1)} %get-tuple-element.42), channel_id=1, source_target_pairs={{0,4},{4,8},{8,12},{12,16},{16,20},{20,24},{24,28},{28,0},{32,36},... | collective-permute-start | bytes 983048 | tf_op jit(solution)/shard_map/ppermute | solution.py:205
  128.8 13.3 %collective-permute-start.8 = (bf16[2,640,128]{2,1,0:T(8,128)(2,1)S(1)}, bf16[2,640,128]{2,1,0:T(8,128)(2,1)S(1)}, u32[]{:S(2)}, u32[]{:S(2)}) collective-permute-start(bf16[2,640,128]{2,1,0:T(8,128)(2,1)S(1)} %get-tuple-element.43), channel_id=1, source_target_pairs={{0,28},{4,0},{8,4},{12,8},{16,12},{20,16},{24,20},{28,24},{32,60},... | collective-permute-start | bytes 983048 | tf_op jit(solution)/shard_map/ppermute | solution.py:205
  132.2 9.9 %collective-permute-start.9 = (bf16[640,128]{1,0:T(8,128)(2,1)S(1)}, bf16[640,128]{1,0:T(8,128)(2,1)S(1)}, u32[]{:S(2)}, u32[]{:S(2)}) collective-permute-start(bf16[640,128]{1,0:T(8,128)(2,1)S(1)} %get-tuple-element.44), channel_id=1, source_target_pairs={{0,8},{4,12},{8,16},{12,20},{16,24},{20,28},{24,0},{28,4},{32,56},... | collective-permute-start | bytes 491528 | tf_op jit(solution)/shard_map/ppermute | solution.py:205
  146.3 30.8 %all-to-all-start.2 = ((bf16[16,40,512]{2,1,0:T(8,128)(2,1)}), bf16[16,40,512]{2,1,0:T(8,128)(2,1)S(1)}, u32[]{:S(2)}, u32[]{:S(2)}) async-start(bf16[16,40,512]{2,1,0:T(8,128)(2,1)} %bitcast.26), calls=%async_computation.3 | async-start | bytes 1310720 | tf_op jit(solution)/shard_map/all_to_all | solution.py:215
  165.9 14.7 %copy-start.7 = (bf16[1,128,640]{2,1,0:T(8,128)(2,1)S(1)}, bf16[1,128,640]{2,1,0:T(8,128)(2,1)}, u32[]{:S(2)}) copy-start(bf16[1,128,640]{2,1,0:T(8,128)(2,1)} %copy-done.6) | copy-start | bytes 491524
  165.9 34.6 %copy-start.2 = (bf16[2,128,640]{2,1,0:T(8,128)(2,1)S(1)}, bf16[2,128,640]{2,1,0:T(8,128)(2,1)}, u32[]{:S(2)}) copy-start(bf16[2,128,640]{2,1,0:T(8,128)(2,1)} %copy-done.1) | copy-start | bytes 983044
  177.1 23.5 %all-to-all-start.3 = ((bf16[16,40,512]{2,1,0:T(8,128)(2,1)}), bf16[16,40,512]{2,1,0:T(8,128)(2,1)S(1)}, u32[]{:S(2)}, u32[]{:S(2)}) async-start(bf16[16,40,512]{2,1,0:T(8,128)(2,1)} %bitcast.58), calls=%async_computation.4 | async-start | bytes 1310720 | tf_op jit(solution)/shard_map/all_to_all | solution.py:215
  180.9 7.0 %collective-permute-start.10 = (bf16[1,128,512]{2,1,0:T(8,128)(2,1)S(1)}, bf16[1,128,512]{2,1,0:T(8,128)(2,1)S(1)}, u32[]{:S(2)}, u32[]{:S(2)}) collective-permute-start(bf16[1,128,512]{2,1,0:T(8,128)(2,1)S(1)} %bitcast.48), channel_id=1, source_target_pairs={{1,0},{2,1},{3,2},{5,4},{6,5},{7,6},{9,8},{10,9},{11,10},{13,12},{... | collective-permute-start | bytes 393224 | tf_op jit(solution)/shard_map/ppermute | solution.py:211
Sparse Core Ops, SparseCore 0:
  10.1 48.2 all-gather.2
  72.2 51.6 reduce-scatter.1
  126.0 39.8 all-gather.4

commit v5 on v4

--- a/solution.py
+++ b/solution.py
@@ -83,6 +83,11 @@
         out_ref[1] = (weight - high.astype(F32)).astype(BF)
 
 
+def first_kernel(experts, cap, ids_ref, gates_ref, x_ref, saved_ref, out_ref, slope_ref):
+    dispatch_kernel(experts, cap, True, ids_ref, gates_ref, x_ref, out_ref)
+    slope_kernel(saved_ref, slope_ref)
+
+
 def combine_kernel(table_ref, rows_ref, out_ref):
     total = dot(table_ref[0], rows_ref[...], 1, 0)
     for i in range(1, table_ref.shape[0]):
@@ -266,10 +271,15 @@
         across = rotated(across, 2, True)
         return (own, low, high, rotated(ahead, 1), rotated(behind, -1), across), other
 
-    send_a = dispatch(ids_a, gate_a, grads_a[0], True)
+    send_a, slope = call(
+        functools.partial(first_kernel, nodes, cap),
+        (shape((slots, width)), shape((2, slots, units))),
+        (ids_a, gate_a, grads_a[0], saved_a[0, 0]),
+        flops=2 * slots * tokens * width,
+        limit=VMEM_WHOLE,
+    )
     rows_a = exchange(send_a, "node")
     send_b = dispatch(ids_b, gate_b, inputs_b[0], False)
-    slope = call(slope_kernel, shape((2, slots, units)), (saved_a[0, 0],), flops=10**6)
     table_a = combine_table(ids_a, gate_a, True)
     table_b = combine_table(ids_b, gate_b, False)
     slopes = lax.all_gather(slope, "local", axis=0, tiled=True).reshape(locals_, 2, slots, units)

time: 210 us -> 209 us (level)
  local copies, waits for them, and re-layouts: 11.4 us -> 8.15 us
    unnamed x38 -> x30, local copies, waits for them, and re-layouts: 11.4 us -> 8.15 us
    all_to_all x4, starting transfers between devices: 28 us -> 30.8 us  [exchange(): return lax.all_to_all(value, axis, split_axis=0, concat_axis=0, tiled=True)]
    all_gather x1, waiting for transfers between devices: 8.84 us -> 6.49 us  [body(): lax.all_gather(hidden, 'local', axis=0, tiled=True)]
    pallas_call x15 -> x14, Pallas kernels: 21.7 us -> 21.9 us  [call(): pl.pallas_call(kernel, out_shape=outs, scratch_shapes=scratch, compiler_p...]
  transfers between devices with their start and end apart: 18 -> 18, of which waited for: 13 -> 13; matrix products, arithmetic and copies ran while one was open for 1% -> 1% of each run, Pallas kernels for 9% -> 8%
where the time goes in v5:
time: 209 us; the launch traced here: 207 us
  waiting for transfers between devices  92.8 us (44%)
  starting transfers between devices  70.6 us (34%)
  Pallas kernels  21.9 us (10%)
  between operations  14 us (7%)
  local copies, waits for them, and re-layouts  8.15 us (4%)
    all_to_all x4, waiting for transfers between devices, exchange(): return lax.all_to_all(value, axis, split_axis=0, concat_axis=0, tiled=True)  38.7 us
    ppermute x10, starting transfers between devices, rotated(): return lax.ppermute(value, ('node', 'local'), pairs)  38.3 us
    all_to_all x4, starting transfers between devices, exchange(): return lax.all_to_all(value, axis, split_axis=0, concat_axis=0, tiled=True)  30.8 us
    ppermute x10, waiting for transfers between devices, rotated(): return lax.ppermute(value, ('node', 'local'), pairs)  28 us
    pallas_call x14, Pallas kernels, call(): pl.pallas_call(kernel, out_shape=outs, scratch_shapes=scratch, compiler_p...  21.9 us
    reduce_scatter x1, waiting for transfers between devices, body(): lax.psum_scatter(part_b.reshape(locals_, 2 * slots, units), 'local', scat...  13.5 us
    unnamed x30, local copies, waits for them, and re-layouts  8.15 us
    all_gather x1, waiting for transfers between devices, body(): lax.all_gather(hidden, 'local', axis=0, tiled=True)  6.49 us
  transfers between devices with their start and end apart: 18, of which 13 were waited for; matrix products, arithmetic and copies ran while one was open for 1% of the time, Pallas kernels for 8%

profile of v5, /device:TPU:1, one launch (start us, length us, event | category | flops | bytes accessed | tf_op | source)
XLA Modules:
  0.0 207.4 jit_solution(4123309270308276204)
XLA Ops:
  7.2 0.0 all-gather.3.cloned.1.call-start
  7.2 2.5 %shard_map.116 = (bf16[640,512]{1,0:T(8,128)(2,1)}, bf16[2,640,128]{2,1,0:T(8,128)(2,1)}) custom-call(s32[4,128]{1,0:T(4,128)} %bitcast.47, f32[4,128]{1,0:T(4,128)} %bitcast.49, bf16[128,512]{1,0:T(8,128)(2,1)} %bitcast.61, bf16[2,128,640]{2,1,0:T(8,128)(2,1)} %bitcast.59), custom_call_target="tpu_custom_call" | custom-call | flops 83886080 | bytes 1445888 | tf_op jit(solution)/shard_map/pallas_call | solution.py:26
  9.7 0.0 all-gather.3.cloned.1.call-update
  9.7 10.3 %all-to-all-start = ((bf16[16,40,512]{2,1,0:T(8,128)(2,1)}), bf16[16,40,512]{2,1,0:T(8,128)(2,1)S(1)}, u32[]{:S(2)}, u32[]{:S(2)}) async-start(bf16[16,40,512]{2,1,0:T(8,128)(2,1)} %bitcast.58), calls=%async_computation | async-start | bytes 1310720 | tf_op jit(solution)/shard_map/all_to_all | solution.py:220
  20.0 0.0 copy-start.10
  20.0 0.0 copy-start.11
  20.0 0.0 copy-start.12
  20.1 0.0 copy-start.8
  20.1 2.2 %copy.15 = bf16[1,1,512,2,1024]{4,2,3,1,0:T(8,128)(2,1)S(1)} copy(bf16[1,1,512,2,1024]{4,3,2,1,0:T(2,128)(2,1)} %param.16) | data formatting | bytes 4194304 | tf_op args[6]
  22.3 0.0 copy-start.13
  22.4 0.3 shard_map.114.table_ref
  22.6 0.7 copy-done.6
  23.3 0.3 shard_map.115.table_ref
  23.6 0.7 copy-done.1
  24.3 1.3 shard_map.113
  25.6 14.4 %all-to-all-done = bf16[16,40,512]{2,1,0:T(8,128)(2,1)S(1)} async-done(((bf16[16,40,512]{2,1,0:T(8,128)(2,1)}), bf16[16,40,512]{2,1,0:T(8,128)(2,1)S(1)}, u32[]{:S(2)}, u32[]{:S(2)}) %all-to-all-start) | async-done | bytes 655392 | tf_op jit(solution)/shard_map/all_to_all | solution.py:220
  40.1 3.5 %all-to-all-start.1 = ((bf16[16,40,512]{2,1,0:T(8,128)(2,1)}), bf16[16,40,512]{2,1,0:T(8,128)(2,1)S(1)}, u32[]{:S(2)}, u32[]{:S(2)}) async-start(bf16[16,40,512]{2,1,0:T(8,128)(2,1)} %bitcast.20), calls=%async_computation.1 | async-start | bytes 1310720 | tf_op jit(solution)/shard_map/all_to_all | solution.py:220
  43.6 0.0 reduce-scatter.2.cloned.1.call-start
  43.6 0.0 copy-start.3
  43.7 1.2 copy-done.3
  44.9 1.1 copy-done.5
  46.0 2.1 %shard_map.117 = (bf16[2,640,128]{2,1,0:T(8,128)(2,1)}, bf16[2,640,128]{2,1,0:T(8,128)(2,1)}, bf16[640,128]{1,0:T(8,128)(2,1)}, bf16[3,640,128]{2,1,0:T(8,128)(2,1)S(1)}) custom-call(s32[8]{0:T(128)S(1)} %and_select_fusion.place_ref, bf16[640,512]{1,0:T(8,128)(2,1)S(1)} %bitcast.44, bf16[1024,512]{1,0:T(8,128)(2,1)S(1)} %bitcast.43), custom_call_target="tpu_custom_call" | custom-call | flops 671088640 | bytes 3014688 | tf_op jit(solution)/shard_map/pallas_call | solution.py:26
  48.1 2.3 %collective-permute-start = (bf16[2,640,128]{2,1,0:T(8,128)(2,1)}, bf16[2,640,128]{2,1,0:T(8,128)(2,1)}, u32[]{:S(2)}, u32[]{:S(2)}) collective-permute-start(bf16[2,640,128]{2,1,0:T(8,128)(2,1)} %get-tuple-element.31), channel_id=1, source_target_pairs={{0,4},{4,8},{8,12},{12,16},{16,20},{20,24},{24,28},{28,0},{32,36},... | collective-permute-start | bytes 983048 | tf_op jit(solution)/shard_map/ppermute | solution.py:210
  50.4 8.6 %collective-permute-start.1 = (bf16[2,640,128]{2,1,0:T(8,128)(2,1)}, bf16[2,640,128]{2,1,0:T(8,128)(2,1)}, u32[]{:S(2)}, u32[]{:S(2)}) collective-permute-start(bf16[2,640,128]{2,1,0:T(8,128)(2,1)} %get-tuple-element.32), channel_id=1, source_target_pairs={{0,28},{4,0},{8,4},{12,8},{16,12},{20,16},{24,20},{28,24},{32,60},... | collective-permute-start | bytes 983048 | tf_op jit(solution)/shard_map/ppermute | solution.py:210
  59.0 1.9 collective-permute-start.2
  60.9 2.2 %all-to-all-done.1 = bf16[16,40,512]{2,1,0:T(8,128)(2,1)S(1)} async-done(((bf16[16,40,512]{2,1,0:T(8,128)(2,1)}), bf16[16,40,512]{2,1,0:T(8,128)(2,1)S(1)}, u32[]{:S(2)}, u32[]{:S(2)}) %all-to-all-start.1) | async-done | bytes 655392 | tf_op jit(solution)/shard_map/all_to_all | solution.py:220
  63.1 2.4 %shard_map.118 = bf16[8,2,640,128]{3,2,1,0:T(8,128)(2,1)S(1)} custom-call(bf16[640,512]{1,0:T(8,128)(2,1)S(1)} %bitcast.41, bf16[2,512,1024]{2,1,0:T(8,128)(2,1)S(1)} %bitcast.36), custom_call_target="tpu_custom_call" | custom-call | flops 1342177280 | bytes 5373952 | tf_op jit(solution)/shard_map/pallas_call | solution.py:26
  65.5 1.5 copy-done
  67.0 2.4 %collective-permute-done.2.across_ref = bf16[640,128]{1,0:T(8,128)(2,1)S(1)} collective-permute-done((bf16[640,128]{1,0:T(8,128)(2,1)}, bf16[640,128]{1,0:T(8,128)(2,1)S(1)}, u32[]{:S(2)}, u32[]{:S(2)}) %collective-permute-start.2) | collective-permute-done | bytes 163872 | tf_op jit(solution)/shard_map/ppermute | solution.py:210
  69.4 0.0 collective-permute-done.ahead_ref.refs_1_
  69.4 0.0 all-gather.3.cloned.1.call-done
  69.4 0.0 reduce-scatter.2.cloned.1.call-update
  69.4 0.0 all-gather.5.cloned.1.call-start
  69.5 1.2 shard_map.119
  70.7 3.2 %collective-permute-start.3 = (bf16[640,128]{1,0:T(8,128)(2,1)S(1)}, bf16[640,128]{1,0:T(8,128)(2,1)S(1)}, u32[]{:S(2)}, u32[]{:S(2)}) collective-permute-start(bf16[640,128]{1,0:T(8,128)(2,1)S(1)} %get-tuple-element.40), channel_id=1, source_target_pairs={{0,8},{4,12},{8,16},{12,20},{16,24},{20,28},{24,0},{28,4},{32,40},... | collective-permute-start | bytes 491528 | tf_op jit(solution)/shard_map/ppermute | solution.py:210
  74.0 5.3 %collective-permute-start.4 = (bf16[640,128]{1,0:T(8,128)(2,1)S(1)}, bf16[640,128]{1,0:T(8,128)(2,1)S(1)}, u32[]{:S(2)}, u32[]{:S(2)}) collective-permute-start(bf16[640,128]{1,0:T(8,128)(2,1)S(1)} %get-tuple-element.41), channel_id=1, source_target_pairs={{0,24},{4,28},{8,0},{12,4},{16,8},{20,12},{24,16},{28,20},{32,56},... | collective-permute-start | bytes 491528 | tf_op jit(solution)/shard_map/ppermute | solution.py:210
  79.3 2.3 %collective-permute-done.3.refs_3_ = bf16[640,128]{1,0:T(8,128)(2,1)S(1)} collective-permute-done((bf16[640,128]{1,0:T(8,128)(2,1)S(1)}, bf16[640,128]{1,0:T(8,128)(2,1)S(1)}, u32[]{:S(2)}, u32[]{:S(2)}) %collective-permute-start.3) | collective-permute-done | bytes 163872 | tf_op jit(solution)/shard_map/ppermute | solution.py:210
  81.6 4.8 %collective-permute-done.4.refs_4_ = bf16[640,128]{1,0:T(8,128)(2,1)S(1)} collective-permute-done((bf16[640,128]{1,0:T(8,128)(2,1)S(1)}, bf16[640,128]{1,0:T(8,128)(2,1)S(1)}, u32[]{:S(2)}, u32[]{:S(2)}) %collective-permute-start.4) | collective-permute-done | bytes 163872 | tf_op jit(solution)/shard_map/ppermute | solution.py:210
  86.4 1.2 shard_map.120.own_ref
  87.6 5.3 %collective-permute-start.5 = (bf16[640,128]{1,0:T(8,128)(2,1)S(1)}, bf16[640,128]{1,0:T(8,128)(2,1)S(1)}, u32[]{:S(2)}, u32[]{:S(2)}) collective-permute-start(bf16[640,128]{1,0:T(8,128)(2,1)S(1)} %shard_map.120.own_ref), channel_id=1, source_target_pairs={{0,8},{4,12},{8,16},{12,20},{16,24},{20,28},{24,0},{28,4},{32,40},... | collective-permute-start | bytes 491528 | tf_op jit(solution)/shard_map/ppermute | solution.py:210
  92.9 2.1 %collective-permute-start.6 = (bf16[640,128]{1,0:T(8,128)(2,1)S(1)}, bf16[640,128]{1,0:T(8,128)(2,1)S(1)}, u32[]{:S(2)}, u32[]{:S(2)}) collective-permute-start(bf16[640,128]{1,0:T(8,128)(2,1)S(1)} %shard_map.120.own_ref), channel_id=1, source_target_pairs={{0,24},{4,28},{8,0},{12,4},{16,8},{20,12},{24,16},{28,20},{32,56},... | collective-permute-start | bytes 491528 | tf_op jit(solution)/shard_map/ppermute | solution.py:210
  95.0 7.0 %collective-permute-done.5.low_ref = bf16[640,128]{1,0:T(8,128)(2,1)S(1)} collective-permute-done((bf16[640,128]{1,0:T(8,128)(2,1)S(1)}, bf16[640,128]{1,0:T(8,128)(2,1)S(1)}, u32[]{:S(2)}, u32[]{:S(2)}) %collective-permute-start.5) | collective-permute-done | bytes 163872 | tf_op jit(solution)/shard_map/ppermute | solution.py:210
  102.0 4.9 %collective-permute-done.6.high_ref = bf16[640,128]{1,0:T(8,128)(2,1)S(1)} collective-permute-done((bf16[640,128]{1,0:T(8,128)(2,1)S(1)}, bf16[640,128]{1,0:T(8,128)(2,1)S(1)}, u32[]{:S(2)}, u32[]{:S(2)}) %collective-permute-start.6) | collective-permute-done | bytes 163872 | tf_op jit(solution)/shard_map/ppermute | solution.py:210
  106.9 0.1 shard_map.121
  107.0 13.5 %reduce-scatter.2.cloned.1.call-done = bf16[1,1280,128]{2,1,0:T(8,128)(2,1)} async-done(((bf16[8,1280,128]{2,1,0:T(8,128)(2,1)}), bf16[1,1280,128]{2,1,0:T(8,128)(2,1)}) %reduce-scatter.2.cloned.1.call-update) | async-done | bytes 327696 | tf_op jit(solution)/shard_map/reduce_scatter | solution.py:307
  120.4 1.7 shard_map.123
  122.2 0.0 all-gather.5.cloned.1.call-update
  122.2 3.4 %collective-permute-start.7 = (bf16[2,640,128]{2,1,0:T(8,128)(2,1)S(1)}, bf16[2,640,128]{2,1,0:T(8,128)(2,1)S(1)}, u32[]{:S(2)}, u32[]{:S(2)}) collective-permute-start(bf16[2,640,128]{2,1,0:T(8,128)(2,1)S(1)} %get-tuple-element.46), channel_id=1, source_target_pairs={{0,4},{4,8},{8,12},{12,16},{16,20},{20,24},{24,28},{28,0},{32,36},... | collective-permute-start | bytes 983048 | tf_op jit(solution)/shard_map/ppermute | solution.py:210
  125.6 3.1 %collective-permute-start.8 = (bf16[2,640,128]{2,1,0:T(8,128)(2,1)S(1)}, bf16[2,640,128]{2,1,0:T(8,128)(2,1)S(1)}, u32[]{:S(2)}, u32[]{:S(2)}) collective-permute-start(bf16[2,640,128]{2,1,0:T(8,128)(2,1)S(1)} %get-tuple-element.47), channel_id=1, source_target_pairs={{0,28},{4,0},{8,4},{12,8},{16,12},{20,16},{24,20},{28,24},{32,60},... | collective-permute-start | bytes 983048 | tf_op jit(solution)/shard_map/ppermute | solution.py:210
  128.7 3.1 %collective-permute-start.9 = (bf16[640,128]{1,0:T(8,128)(2,1)S(1)}, bf16[640,128]{1,0:T(8,128)(2,1)S(1)}, u32[]{:S(2)}, u32[]{:S(2)}) collective-permute-start(bf16[640,128]{1,0:T(8,128)(2,1)S(1)} %get-tuple-element.48), channel_id=1, source_target_pairs={{0,8},{4,12},{8,16},{12,20},{16,24},{20,28},{24,0},{28,4},{32,56},... | collective-permute-start | bytes 491528 | tf_op jit(solution)/shard_map/ppermute | solution.py:210
  131.8 6.6 %collective-permute-done.9.across_ref = bf16[640,128]{1,0:T(8,128)(2,1)S(1)} collective-permute-done((bf16[640,128]{1,0:T(8,128)(2,1)S(1)}, bf16[640,128]{1,0:T(8,128)(2,1)S(1)}, u32[]{:S(2)}, u32[]{:S(2)}) %collective-permute-start.9) | collective-permute-done | bytes 163872 | tf_op jit(solution)/shard_map/ppermute | solution.py:210
  138.4 0.0 collective-permute-done.7.ahead_ref
  138.4 4.2 %shard_map.122 = bf16[640,512]{1,0:T(8,128)(2,1)} custom-call(s32[8]{0:T(128)S(1)} %and_select_fusion.place_ref, bf16[640,128]{1,0:T(8,128)(2,1)S(1)} %shard_map.120.own_ref, bf16[640,128]{1,0:T(8,128)(2,1)S(1)} %collective-permute-done.5.low_ref, bf16[640,128]{1,0:T(8,128)(2,1)S(1)} %collective-permute-done.6.high_ref, ...), custom_call_target="tpu_custom_call" | custom-call | flops 1342177280 | bytes 6684704 | tf_op jit(solution)/shard_map/pallas_call | solution.py:26
  142.6 13.6 %all-to-all-start.2 = ((bf16[16,40,512]{2,1,0:T(8,128)(2,1)}), bf16[16,40,512]{2,1,0:T(8,128)(2,1)S(1)}, u32[]{:S(2)}, u32[]{:S(2)}) async-start(bf16[16,40,512]{2,1,0:T(8,128)(2,1)} %bitcast.26), calls=%async_computation.3 | async-start | bytes 1310720 | tf_op jit(solution)/shard_map/all_to_all | solution.py:220
  156.2 6.5 %all-gather.5.cloned.1.call-done = bf16[5120,128]{1,0:T(8,128)(2,1)} async-done(((bf16[640,128]{1,0:T(8,128)(2,1)}), bf16[5120,128]{1,0:T(8,128)(2,1)}) %all-gather.5.cloned.1.call-update) | async-done | bytes 1310736 | tf_op jit(solution)/shard_map/all_gather | solution.py:321
  162.7 3.4 %shard_map.124 = bf16[640,512]{1,0:T(8,128)(2,1)} custom-call(bf16[8,640,128]{2,1,0:T(8,128)(2,1)} %bitcast.57, bf16[1024,512]{1,0:T(8,128)(2,1)} %bitcast.42), custom_call_target="tpu_custom_call" | custom-call | flops 671088640 | bytes 3014656 | tf_op jit(solution)/shard_map/pallas_call | solution.py:26
  166.0 10.2 %all-to-all-done.2 = bf16[16,40,512]{2,1,0:T(8,128)(2,1)S(1)} async-done(((bf16[16,40,512]{2,1,0:T(8,128)(2,1)}), bf16[16,40,512]{2,1,0:T(8,128)(2,1)S(1)}, u32[]{:S(2)}, u32[]{:S(2)}) %all-to-all-start.2) | async-done | bytes 655392 | tf_op jit(solution)/shard_map/all_to_all | solution.py:220
  176.2 3.5 %all-to-all-start.3 = ((bf16[16,40,512]{2,1,0:T(8,128)(2,1)}), bf16[16,40,512]{2,1,0:T(8,128)(2,1)S(1)}, u32[]{:S(2)}, u32[]{:S(2)}) async-start(bf16[16,40,512]{2,1,0:T(8,128)(2,1)} %bitcast.56), calls=%async_computation.4 | async-start | bytes 1310720 | tf_op jit(solution)/shard_map/all_to_all | solution.py:220
  179.7 0.3 shard_map.126
  180.0 1.3 collective-permute-start.10
  181.3 6.0 %collective-permute-done.10 = bf16[1,128,512]{2,1,0:T(8,128)(2,1)S(1)} collective-permute-done((bf16[1,128,512]{2,1,0:T(8,128)(2,1)S(1)}, bf16[1,128,512]{2,1,0:T(8,128)(2,1)S(1)}, u32[]{:S(2)}, u32[]{:S(2)}) %collective-permute-start.10) | collective-permute-done | bytes 131104 | tf_op jit(solution)/shard_map/ppermute | solution.py:216
  187.3 11.9 %all-to-all-done.3 = bf16[16,40,512]{2,1,0:T(8,128)(2,1)S(1)} async-done(((bf16[16,40,512]{2,1,0:T(8,128)(2,1)}), bf16[16,40,512]{2,1,0:T(8,128)(2,1)S(1)}, u32[]{:S(2)}, u32[]{:S(2)}) %all-to-all-start.3) | async-done | bytes 655392 | tf_op jit(solution)/shard_map/all_to_all | solution.py:220
  199.2 1.0 shard_map.125
  200.3 0.7 copy.17
  (20 shorter events, 0.0 us)
Async XLA Ops:
  7.2 62.3 %all-gather.3.cloned.1.call-start = ((), (), s32[]{:S(2)}) async-start(), calls=%async_computation.5 | async-start | bytes 2949120 | tf_op jit(solution)/shard_map/all_gather | solution.py:285
  9.7 30.3 %all-to-all-start = ((bf16[16,40,512]{2,1,0:T(8,128)(2,1)}), bf16[16,40,512]{2,1,0:T(8,128)(2,1)S(1)}, u32[]{:S(2)}, u32[]{:S(2)}) async-start(bf16[16,40,512]{2,1,0:T(8,128)(2,1)} %bitcast.58), calls=%async_computation | async-start | bytes 1310720 | tf_op jit(solution)/shard_map/all_to_all | solution.py:220
  20.0 2.3 %copy-start.9 = (s32[1,128,4]{1,2,0:T(4,128)S(1)}, s32[1,128,4]{1,2,0:T(4,128)}, u32[]{:S(2)}) copy-start(s32[1,128,4]{1,2,0:T(4,128)} %param.12) | copy-start | bytes 6148
  20.0 2.3 %copy-start.10 = (f32[1,128,4]{1,2,0:T(4,128)S(1)}, f32[1,128,4]{1,2,0:T(4,128)}, u32[]{:S(2)}) copy-start(f32[1,128,4]{1,2,0:T(4,128)} %param.14) | copy-start | bytes 6148
  20.0 3.3 %copy-start.11 = (s32[1,128,4]{1,2,0:T(4,128)S(1)}, s32[1,128,4]{1,2,0:T(4,128)}, u32[]{:S(2)}) copy-start(s32[1,128,4]{1,2,0:T(4,128)} %param.13) | copy-start | bytes 6148
  20.0 3.3 %copy-start.12 = (f32[1,128,4]{1,2,0:T(4,128)S(1)}, f32[1,128,4]{1,2,0:T(4,128)}, u32[]{:S(2)}) copy-start(f32[1,128,4]{1,2,0:T(4,128)} %param.15) | copy-start | bytes 6148
  20.1 4.3 %copy-start.8 = (bf16[1,128,512]{2,1,0:T(8,128)(2,1)S(1)}, bf16[1,128,512]{2,1,0:T(8,128)(2,1)}, u32[]{:S(2)}) copy-start(bf16[1,128,512]{2,1,0:T(8,128)(2,1)} %param.10) | copy-start | bytes 393220
  22.3 21.3 %copy-start.13 = (s32[8]{0:T(128)S(1)}, s32[8]{0:T(128)}, u32[]{:S(2)}) copy-start(s32[8]{0:T(128)} %constant.41.clone) | copy-start | bytes 100
  22.6 0.7 copy-start.6
  23.6 0.7 copy-start.1
  40.1 3.6 %copy-start.4 = (bf16[16,40,512]{2,1,0:T(8,128)(2,1)}, bf16[16,40,512]{2,1,0:T(8,128)(2,1)S(1)}, u32[]{:S(2)}) copy-start(bf16[16,40,512]{2,1,0:T(8,128)(2,1)S(1)} %all-to-all-done) | copy-start | bytes 1966084
  40.1 23.1 %all-to-all-start.1 = ((bf16[16,40,512]{2,1,0:T(8,128)(2,1)}), bf16[16,40,512]{2,1,0:T(8,128)(2,1)S(1)}, u32[]{:S(2)}, u32[]{:S(2)}) async-start(bf16[16,40,512]{2,1,0:T(8,128)(2,1)} %bitcast.20), calls=%async_computation.1 | async-start | bytes 1310720 | tf_op jit(solution)/shard_map/all_to_all | solution.py:220
  43.6 76.9 %reduce-scatter.2.cloned.1.call-start = ((), (), s32[]{:S(2)}) async-start(), calls=%async_computation.6 | async-start | bytes 2949120 | tf_op jit(solution)/shard_map/reduce_scatter | solution.py:307
  43.6 1.2 copy-start.3
  44.9 1.1 copy-start.5
  48.1 21.3 %collective-permute-start = (bf16[2,640,128]{2,1,0:T(8,128)(2,1)}, bf16[2,640,128]{2,1,0:T(8,128)(2,1)}, u32[]{:S(2)}, u32[]{:S(2)}) collective-permute-start(bf16[2,640,128]{2,1,0:T(8,128)(2,1)} %get-tuple-element.31), channel_id=1, source_target_pairs={{0,4},{4,8},{8,12},{12,16},{16,20},{20,24},{24,28},{28,0},{32,36},... | collective-permute-start | bytes 983048 | tf_op jit(solution)/shard_map/ppermute | solution.py:210
  50.4 19.0 %collective-permute-start.1 = (bf16[2,640,128]{2,1,0:T(8,128)(2,1)}, bf16[2,640,128]{2,1,0:T(8,128)(2,1)}, u32[]{:S(2)}, u32[]{:S(2)}) collective-permute-start(bf16[2,640,128]{2,1,0:T(8,128)(2,1)} %get-tuple-element.32), channel_id=1, source_target_pairs={{0,28},{4,0},{8,4},{12,8},{16,12},{20,16},{24,20},{28,24},{32,60},... | collective-permute-start | bytes 983048 | tf_op jit(solution)/shard_map/ppermute | solution.py:210
  59.0 10.4 %collective-permute-start.2 = (bf16[640,128]{1,0:T(8,128)(2,1)}, bf16[640,128]{1,0:T(8,128)(2,1)S(1)}, u32[]{:S(2)}, u32[]{:S(2)}) collective-permute-start(bf16[640,128]{1,0:T(8,128)(2,1)} %get-tuple-element.33), channel_id=1, source_target_pairs={{0,24},{4,28},{8,0},{12,4},{16,8},{20,12},{24,16},{28,20},{32,40},... | collective-permute-start | bytes 491528 | tf_op jit(solution)/shard_map/ppermute | solution.py:210
  65.5 1.5 copy-start
  69.4 93.2 %all-gather.5.cloned.1.call-start = ((), (), s32[]{:S(2)}) async-start(), calls=%async_computation.7 | async-start | bytes 1474560 | tf_op jit(solution)/shard_map/all_gather | solution.py:321
  70.7 10.9 %collective-permute-start.3 = (bf16[640,128]{1,0:T(8,128)(2,1)S(1)}, bf16[640,128]{1,0:T(8,128)(2,1)S(1)}, u32[]{:S(2)}, u32[]{:S(2)}) collective-permute-start(bf16[640,128]{1,0:T(8,128)(2,1)S(1)} %get-tuple-element.40), channel_id=1, source_target_pairs={{0,8},{4,12},{8,16},{12,20},{16,24},{20,28},{24,0},{28,4},{32,40},... | collective-permute-start | bytes 491528 | tf_op jit(solution)/shard_map/ppermute | solution.py:210
  74.0 12.4 %collective-permute-start.4 = (bf16[640,128]{1,0:T(8,128)(2,1)S(1)}, bf16[640,128]{1,0:T(8,128)(2,1)S(1)}, u32[]{:S(2)}, u32[]{:S(2)}) collective-permute-start(bf16[640,128]{1,0:T(8,128)(2,1)S(1)} %get-tuple-element.41), channel_id=1, source_target_pairs={{0,24},{4,28},{8,0},{12,4},{16,8},{20,12},{24,16},{28,20},{32,56},... | collective-permute-start | bytes 491528 | tf_op jit(solution)/shard_map/ppermute | solution.py:210
  87.6 14.4 %collective-permute-start.5 = (bf16[640,128]{1,0:T(8,128)(2,1)S(1)}, bf16[640,128]{1,0:T(8,128)(2,1)S(1)}, u32[]{:S(2)}, u32[]{:S(2)}) collective-permute-start(bf16[640,128]{1,0:T(8,128)(2,1)S(1)} %shard_map.120.own_ref), channel_id=1, source_target_pairs={{0,8},{4,12},{8,16},{12,20},{16,24},{20,28},{24,0},{28,4},{32,40},... | collective-permute-start | bytes 491528 | tf_op jit(solution)/shard_map/ppermute | solution.py:210
  92.9 14.0 %collective-permute-start.6 = (bf16[640,128]{1,0:T(8,128)(2,1)S(1)}, bf16[640,128]{1,0:T(8,128)(2,1)S(1)}, u32[]{:S(2)}, u32[]{:S(2)}) collective-permute-start(bf16[640,128]{1,0:T(8,128)(2,1)S(1)} %shard_map.120.own_ref), channel_id=1, source_target_pairs={{0,24},{4,28},{8,0},{12,4},{16,8},{20,12},{24,16},{28,20},{32,56},... | collective-permute-start | bytes 491528 | tf_op jit(solution)/shard_map/ppermute | solution.py:210
  122.2 16.2 %collective-permute-start.7 = (bf16[2,640,128]{2,1,0:T(8,128)(2,1)S(1)}, bf16[2,640,128]{2,1,0:T(8,128)(2,1)S(1)}, u32[]{:S(2)}, u32[]{:S(2)}) collective-permute-start(bf16[2,640,128]{2,1,0:T(8,128)(2,1)S(1)} %get-tuple-element.46), channel_id=1, source_target_pairs={{0,4},{4,8},{8,12},{12,16},{16,20},{20,24},{24,28},{28,0},{32,36},... | collective-permute-start | bytes 983048 | tf_op jit(solution)/shard_map/ppermute | solution.py:210
  125.6 12.8 %collective-permute-start.8 = (bf16[2,640,128]{2,1,0:T(8,128)(2,1)S(1)}, bf16[2,640,128]{2,1,0:T(8,128)(2,1)S(1)}, u32[]{:S(2)}, u32[]{:S(2)}) collective-permute-start(bf16[2,640,128]{2,1,0:T(8,128)(2,1)S(1)} %get-tuple-element.47), channel_id=1, source_target_pairs={{0,28},{4,0},{8,4},{12,8},{16,12},{20,16},{24,20},{28,24},{32,60},... | collective-permute-start | bytes 983048 | tf_op jit(solution)/shard_map/ppermute | solution.py:210
  128.7 9.7 %collective-permute-start.9 = (bf16[640,128]{1,0:T(8,128)(2,1)S(1)}, bf16[640,128]{1,0:T(8,128)(2,1)S(1)}, u32[]{:S(2)}, u32[]{:S(2)}) collective-permute-start(bf16[640,128]{1,0:T(8,128)(2,1)S(1)} %get-tuple-element.48), channel_id=1, source_target_pairs={{0,8},{4,12},{8,16},{12,20},{16,24},{20,28},{24,0},{28,4},{32,56},... | collective-permute-start | bytes 491528 | tf_op jit(solution)/shard_map/ppermute | solution.py:210
  142.6 33.6 %all-to-all-start.2 = ((bf16[16,40,512]{2,1,0:T(8,128)(2,1)}), bf16[16,40,512]{2,1,0:T(8,128)(2,1)S(1)}, u32[]{:S(2)}, u32[]{:S(2)}) async-start(bf16[16,40,512]{2,1,0:T(8,128)(2,1)} %bitcast.26), calls=%async_computation.3 | async-start | bytes 1310720 | tf_op jit(solution)/shard_map/all_to_all | solution.py:220
  162.7 17.0 %copy-start.7 = (bf16[1,128,640]{2,1,0:T(8,128)(2,1)S(1)}, bf16[1,128,640]{2,1,0:T(8,128)(2,1)}, u32[]{:S(2)}) copy-start(bf16[1,128,640]{2,1,0:T(8,128)(2,1)} %copy-done.6) | copy-start | bytes 491524
  162.7 36.6 %copy-start.2 = (bf16[2,128,640]{2,1,0:T(8,128)(2,1)S(1)}, bf16[2,128,640]{2,1,0:T(8,128)(2,1)}, u32[]{:S(2)}) copy-start(bf16[2,128,640]{2,1,0:T(8,128)(2,1)} %copy-done.1) | copy-start | bytes 983044
  176.2 23.0 %all-to-all-start.3 = ((bf16[16,40,512]{2,1,0:T(8,128)(2,1)}), bf16[16,40,512]{2,1,0:T(8,128)(2,1)S(1)}, u32[]{:S(2)}, u32[]{:S(2)}) async-start(bf16[16,40,512]{2,1,0:T(8,128)(2,1)} %bitcast.56), calls=%async_computation.4 | async-start | bytes 1310720 | tf_op jit(solution)/shard_map/all_to_all | solution.py:220
  180.0 7.3 %collective-permute-start.10 = (bf16[1,128,512]{2,1,0:T(8,128)(2,1)S(1)}, bf16[1,128,512]{2,1,0:T(8,128)(2,1)S(1)}, u32[]{:S(2)}, u32[]{:S(2)}) collective-permute-start(bf16[1,128,512]{2,1,0:T(8,128)(2,1)S(1)} %bitcast.46), channel_id=1, source_target_pairs={{1,0},{2,1},{3,2},{5,4},{6,5},{7,6},{9,8},{10,9},{11,10},{13,12},{... | collective-permute-start | bytes 393224 | tf_op jit(solution)/shard_map/ppermute | solution.py:216
Sparse Core Ops, SparseCore 0:
  10.1 51.4 all-gather.2
  69.6 50.8 reduce-scatter.1
  122.5 40.0 all-gather.4

commit v6 on v5

--- a/solution.py
+++ b/solution.py
@@ -267,8 +267,8 @@
         low, high = rotated(own, 2), rotated(own, -2)
         two, one = shape((2,) + own.shape), shape(own.shape)
         ahead, behind, across = call(pack_kernel, (two, two, one), (core, own, low, high), scalars=True)
+        across = rotated(across, 2, True)
         ahead, behind, across, other = lax.optimization_barrier((ahead, behind, across, other))
-        across = rotated(across, 2, True)
         return (own, low, high, rotated(ahead, 1), rotated(behind, -1), across), other
 
     send_a, slope = call(

time: 209 us -> 210 us (level)
  waiting for transfers between devices: 92.8 us -> 94.9 us
    ppermute x10, waiting for transfers between devices: 28 us -> 36.1 us  [rotated(): return lax.ppermute(value, ('node', 'local'), pairs)]
    reduce_scatter x1, waiting for transfers between devices: 13.5 us -> 6.98 us  [body(): lax.psum_scatter(part_b.reshape(locals_, 2 * slots, units), 'local', scat...]
    all_gather x1, waiting for transfers between devices: 6.49 us -> 9.76 us  [body(): lax.all_gather(hidden, 'local', axis=0, tiled=True)]
    all_to_all x4, waiting for transfers between devices: 38.7 us -> 36.3 us  [exchange(): return lax.all_to_all(value, axis, split_axis=0, concat_axis=0, tiled=True)]
  transfers between devices with their start and end apart: 18 -> 18, of which waited for: 13 -> 15; matrix products, arithmetic and copies ran while one was open for 1% -> 1% of each run, Pallas kernels for 8% -> 8%
where the time goes in v6:
time: 210 us; the launch traced here: 209 us
  waiting for transfers between devices  94.9 us (45%)
  starting transfers between devices  70 us (33%)
  Pallas kernels  21.9 us (10%)
  between operations  14 us (7%)
  local copies, waits for them, and re-layouts  8.15 us (4%)
    ppermute x10, starting transfers between devices, rotated(): return lax.ppermute(value, ('node', 'local'), pairs)  37.2 us
    all_to_all x4, waiting for transfers between devices, exchange(): return lax.all_to_all(value, axis, split_axis=0, concat_axis=0, tiled=True)  36.3 us
    ppermute x10, waiting for transfers between devices, rotated(): return lax.ppermute(value, ('node', 'local'), pairs)  36.1 us
    all_to_all x4, starting transfers between devices, exchange(): return lax.all_to_all(value, axis, split_axis=0, concat_axis=0, tiled=True)  31.5 us
    pallas_call x14, Pallas kernels, call(): pl.pallas_call(kernel, out_shape=outs, scratch_shapes=scratch, compiler_p...  21.9 us
    all_gather x1, waiting for transfers between devices, body(): lax.all_gather(hidden, 'local', axis=0, tiled=True)  9.76 us
    unnamed x30, local copies, waits for them, and re-layouts  8.15 us
    reduce_scatter x1, waiting for transfers between devices, body(): lax.psum_scatter(part_b.reshape(locals_, 2 * slots, units), 'local', scat...  6.98 us
  transfers between devices with their start and end apart: 18, of which 15 were waited for; matrix products, arithmetic and copies ran while one was open for 1% of the time, Pallas kernels for 8%

profile of v6, /device:TPU:1, one launch (start us, length us, event | category | flops | bytes accessed | tf_op | source)
XLA Modules:
  0.0 209.0 jit_solution(14058005960481724809)
XLA Ops:
  7.2 0.0 all-gather.3.cloned.1.call-start
  7.2 2.5 %shard_map.116 = (bf16[640,512]{1,0:T(8,128)(2,1)}, bf16[2,640,128]{2,1,0:T(8,128)(2,1)}) custom-call(s32[4,128]{1,0:T(4,128)} %bitcast.47, f32[4,128]{1,0:T(4,128)} %bitcast.49, bf16[128,512]{1,0:T(8,128)(2,1)} %bitcast.61, bf16[2,128,640]{2,1,0:T(8,128)(2,1)} %bitcast.59), custom_call_target="tpu_custom_call" | custom-call | flops 83886080 | bytes 1445888 | tf_op jit(solution)/shard_map/pallas_call | solution.py:26
  9.7 0.0 all-gather.3.cloned.1.call-update
  9.7 10.3 %all-to-all-start = ((bf16[16,40,512]{2,1,0:T(8,128)(2,1)}), bf16[16,40,512]{2,1,0:T(8,128)(2,1)S(1)}, u32[]{:S(2)}, u32[]{:S(2)}) async-start(bf16[16,40,512]{2,1,0:T(8,128)(2,1)} %bitcast.58), calls=%async_computation | async-start | bytes 1310720 | tf_op jit(solution)/shard_map/all_to_all | solution.py:220
  20.0 0.0 copy-start.10
  20.0 0.0 copy-start.11
  20.0 0.0 copy-start.12
  20.1 0.0 copy-start.8
  20.1 2.2 %copy.15 = bf16[1,1,512,2,1024]{4,2,3,1,0:T(8,128)(2,1)S(1)} copy(bf16[1,1,512,2,1024]{4,3,2,1,0:T(2,128)(2,1)} %param.16) | data formatting | bytes 4194304 | tf_op args[6]
  22.3 0.0 copy-start.13
  22.4 0.3 shard_map.114.table_ref
  22.6 0.7 copy-done.6
  23.3 0.3 shard_map.115.table_ref
  23.6 0.7 copy-done.1
  24.3 1.3 shard_map.113
  25.6 14.4 %all-to-all-done = bf16[16,40,512]{2,1,0:T(8,128)(2,1)S(1)} async-done(((bf16[16,40,512]{2,1,0:T(8,128)(2,1)}), bf16[16,40,512]{2,1,0:T(8,128)(2,1)S(1)}, u32[]{:S(2)}, u32[]{:S(2)}) %all-to-all-start) | async-done | bytes 655392 | tf_op jit(solution)/shard_map/all_to_all | solution.py:220
  40.1 3.5 %all-to-all-start.1 = ((bf16[16,40,512]{2,1,0:T(8,128)(2,1)}), bf16[16,40,512]{2,1,0:T(8,128)(2,1)S(1)}, u32[]{:S(2)}, u32[]{:S(2)}) async-start(bf16[16,40,512]{2,1,0:T(8,128)(2,1)} %bitcast.20), calls=%async_computation.1 | async-start | bytes 1310720 | tf_op jit(solution)/shard_map/all_to_all | solution.py:220
  43.6 0.0 reduce-scatter.2.cloned.1.call-start
  43.6 0.0 copy-start.3
  43.7 1.2 copy-done.3
  44.9 1.1 copy-done.5
  46.0 2.1 shard_map.117
  48.1 2.3 %collective-permute-start = (bf16[2,640,128]{2,1,0:T(8,128)(2,1)}, bf16[2,640,128]{2,1,0:T(8,128)(2,1)}, u32[]{:S(2)}, u32[]{:S(2)}) collective-permute-start(bf16[2,640,128]{2,1,0:T(8,128)(2,1)} %get-tuple-element.31), channel_id=1, source_target_pairs={{0,4},{4,8},{8,12},{12,16},{16,20},{20,24},{24,28},{28,0},{32,36},... | collective-permute-start | bytes 983048 | tf_op jit(solution)/shard_map/ppermute | solution.py:210
  50.4 8.6 %collective-permute-start.1 = (bf16[2,640,128]{2,1,0:T(8,128)(2,1)}, bf16[2,640,128]{2,1,0:T(8,128)(2,1)}, u32[]{:S(2)}, u32[]{:S(2)}) collective-permute-start(bf16[2,640,128]{2,1,0:T(8,128)(2,1)} %get-tuple-element.32), channel_id=1, source_target_pairs={{0,28},{4,0},{8,4},{12,8},{16,12},{20,16},{24,20},{28,24},{32,60},... | collective-permute-start | bytes 983048 | tf_op jit(solution)/shard_map/ppermute | solution.py:210
  59.0 1.9 collective-permute-start.2
  60.9 2.2 %all-to-all-done.1 = bf16[16,40,512]{2,1,0:T(8,128)(2,1)S(1)} async-done(((bf16[16,40,512]{2,1,0:T(8,128)(2,1)}), bf16[16,40,512]{2,1,0:T(8,128)(2,1)S(1)}, u32[]{:S(2)}, u32[]{:S(2)}) %all-to-all-start.1) | async-done | bytes 655392 | tf_op jit(solution)/shard_map/all_to_all | solution.py:220
  63.1 2.4 %shard_map.118 = bf16[8,2,640,128]{3,2,1,0:T(8,128)(2,1)S(1)} custom-call(bf16[640,512]{1,0:T(8,128)(2,1)S(1)} %bitcast.41, bf16[2,512,1024]{2,1,0:T(8,128)(2,1)S(1)} %bitcast.36), custom_call_target="tpu_custom_call" | custom-call | flops 1342177280 | bytes 5373952 | tf_op jit(solution)/shard_map/pallas_call | solution.py:26
  65.5 1.5 copy-done
  67.0 2.4 %collective-permute-done.2.across_ref = bf16[640,128]{1,0:T(8,128)(2,1)S(1)} collective-permute-done((bf16[640,128]{1,0:T(8,128)(2,1)}, bf16[640,128]{1,0:T(8,128)(2,1)S(1)}, u32[]{:S(2)}, u32[]{:S(2)}) %collective-permute-start.2) | collective-permute-done | bytes 163872 | tf_op jit(solution)/shard_map/ppermute | solution.py:210
  69.4 0.0 all-gather.3.cloned.1.call-done
  69.4 0.0 reduce-scatter.2.cloned.1.call-update
  69.4 0.0 all-gather.5.cloned.1.call-start
  69.5 1.2 shard_map.119
  70.7 3.2 %collective-permute-start.3 = (bf16[640,128]{1,0:T(8,128)(2,1)S(1)}, bf16[640,128]{1,0:T(8,128)(2,1)S(1)}, u32[]{:S(2)}, u32[]{:S(2)}) collective-permute-start(bf16[640,128]{1,0:T(8,128)(2,1)S(1)} %get-tuple-element.40), channel_id=1, source_target_pairs={{0,8},{4,12},{8,16},{12,20},{16,24},{20,28},{24,0},{28,4},{32,40},... | collective-permute-start | bytes 491528 | tf_op jit(solution)/shard_map/ppermute | solution.py:210
  74.0 5.3 %collective-permute-start.4 = (bf16[640,128]{1,0:T(8,128)(2,1)S(1)}, bf16[640,128]{1,0:T(8,128)(2,1)S(1)}, u32[]{:S(2)}, u32[]{:S(2)}) collective-permute-start(bf16[640,128]{1,0:T(8,128)(2,1)S(1)} %get-tuple-element.41), channel_id=1, source_target_pairs={{0,24},{4,28},{8,0},{12,4},{16,8},{20,12},{24,16},{28,20},{32,56},... | collective-permute-start | bytes 491528 | tf_op jit(solution)/shard_map/ppermute | solution.py:210
  79.3 2.3 %collective-permute-done.3.refs_3_ = bf16[640,128]{1,0:T(8,128)(2,1)S(1)} collective-permute-done((bf16[640,128]{1,0:T(8,128)(2,1)S(1)}, bf16[640,128]{1,0:T(8,128)(2,1)S(1)}, u32[]{:S(2)}, u32[]{:S(2)}) %collective-permute-start.3) | collective-permute-done | bytes 163872 | tf_op jit(solution)/shard_map/ppermute | solution.py:210
  81.6 4.8 %collective-permute-done.4.refs_4_ = bf16[640,128]{1,0:T(8,128)(2,1)S(1)} collective-permute-done((bf16[640,128]{1,0:T(8,128)(2,1)S(1)}, bf16[640,128]{1,0:T(8,128)(2,1)S(1)}, u32[]{:S(2)}, u32[]{:S(2)}) %collective-permute-start.4) | collective-permute-done | bytes 163872 | tf_op jit(solution)/shard_map/ppermute | solution.py:210
  86.4 1.2 shard_map.120.own_ref
  87.6 5.3 %collective-permute-start.5 = (bf16[640,128]{1,0:T(8,128)(2,1)S(1)}, bf16[640,128]{1,0:T(8,128)(2,1)S(1)}, u32[]{:S(2)}, u32[]{:S(2)}) collective-permute-start(bf16[640,128]{1,0:T(8,128)(2,1)S(1)} %shard_map.120.own_ref), channel_id=1, source_target_pairs={{0,8},{4,12},{8,16},{12,20},{16,24},{20,28},{24,0},{28,4},{32,40},... | collective-permute-start | bytes 491528 | tf_op jit(solution)/shard_map/ppermute | solution.py:210
  92.9 2.1 %collective-permute-start.6 = (bf16[640,128]{1,0:T(8,128)(2,1)S(1)}, bf16[640,128]{1,0:T(8,128)(2,1)S(1)}, u32[]{:S(2)}, u32[]{:S(2)}) collective-permute-start(bf16[640,128]{1,0:T(8,128)(2,1)S(1)} %shard_map.120.own_ref), channel_id=1, source_target_pairs={{0,24},{4,28},{8,0},{12,4},{16,8},{20,12},{24,16},{28,20},{32,56},... | collective-permute-start | bytes 491528 | tf_op jit(solution)/shard_map/ppermute | solution.py:210
  95.0 7.0 %collective-permute-done.5.low_ref = bf16[640,128]{1,0:T(8,128)(2,1)S(1)} collective-permute-done((bf16[640,128]{1,0:T(8,128)(2,1)S(1)}, bf16[640,128]{1,0:T(8,128)(2,1)S(1)}, u32[]{:S(2)}, u32[]{:S(2)}) %collective-permute-start.5) | collective-permute-done | bytes 163872 | tf_op jit(solution)/shard_map/ppermute | solution.py:210
  102.0 4.9 %collective-permute-done.6.high_ref = bf16[640,128]{1,0:T(8,128)(2,1)S(1)} collective-permute-done((bf16[640,128]{1,0:T(8,128)(2,1)S(1)}, bf16[640,128]{1,0:T(8,128)(2,1)S(1)}, u32[]{:S(2)}, u32[]{:S(2)}) %collective-permute-start.6) | collective-permute-done | bytes 163872 | tf_op jit(solution)/shard_map/ppermute | solution.py:210
  106.9 0.1 shard_map.121
  107.0 1.9 collective-permute-start.7
  108.9 9.6 %collective-permute-done.7.across_ref = bf16[640,128]{1,0:T(8,128)(2,1)S(1)} collective-permute-done((bf16[640,128]{1,0:T(8,128)(2,1)S(1)}, bf16[640,128]{1,0:T(8,128)(2,1)S(1)}, u32[]{:S(2)}, u32[]{:S(2)}) %collective-permute-start.7) | collective-permute-done | bytes 163872 | tf_op jit(solution)/shard_map/ppermute | solution.py:210
  118.5 7.0 %reduce-scatter.2.cloned.1.call-done = bf16[1,1280,128]{2,1,0:T(8,128)(2,1)} async-done(((bf16[8,1280,128]{2,1,0:T(8,128)(2,1)}), bf16[1,1280,128]{2,1,0:T(8,128)(2,1)}) %reduce-scatter.2.cloned.1.call-update) | async-done | bytes 327696 | tf_op jit(solution)/shard_map/reduce_scatter | solution.py:307
  125.5 1.7 shard_map.123
  127.2 0.0 all-gather.5.cloned.1.call-update
  127.2 1.9 collective-permute-start.8
  129.1 4.6 %collective-permute-start.9 = (bf16[2,640,128]{2,1,0:T(8,128)(2,1)S(1)}, bf16[2,640,128]{2,1,0:T(8,128)(2,1)S(1)}, u32[]{:S(2)}, u32[]{:S(2)}) collective-permute-start(bf16[2,640,128]{2,1,0:T(8,128)(2,1)S(1)} %get-tuple-element.47), channel_id=1, source_target_pairs={{0,28},{4,0},{8,4},{12,8},{16,12},{20,16},{24,20},{28,24},{32,60},... | collective-permute-start | bytes 983048 | tf_op jit(solution)/shard_map/ppermute | solution.py:210
  133.7 4.2 %collective-permute-done.8.ahead_ref = bf16[2,640,128]{2,1,0:T(8,128)(2,1)S(1)} collective-permute-done((bf16[2,640,128]{2,1,0:T(8,128)(2,1)S(1)}, bf16[2,640,128]{2,1,0:T(8,128)(2,1)S(1)}, u32[]{:S(2)}, u32[]{:S(2)}) %collective-permute-start.8) | collective-permute-done | bytes 327712 | tf_op jit(solution)/shard_map/ppermute | solution.py:210
  138.0 0.9 collective-permute-done.9.behind_ref
  138.9 4.2 %shard_map.122 = bf16[640,512]{1,0:T(8,128)(2,1)} custom-call(s32[8]{0:T(128)S(1)} %and_select_fusion.place_ref, bf16[640,128]{1,0:T(8,128)(2,1)S(1)} %shard_map.120.own_ref, bf16[640,128]{1,0:T(8,128)(2,1)S(1)} %collective-permute-done.5.low_ref, bf16[640,128]{1,0:T(8,128)(2,1)S(1)} %collective-permute-done.6.high_ref, ...), custom_call_target="tpu_custom_call" | custom-call | flops 1342177280 | bytes 6684704 | tf_op jit(solution)/shard_map/pallas_call | solution.py:26
  143.1 12.6 %all-to-all-start.2 = ((bf16[16,40,512]{2,1,0:T(8,128)(2,1)}), bf16[16,40,512]{2,1,0:T(8,128)(2,1)S(1)}, u32[]{:S(2)}, u32[]{:S(2)}) async-start(bf16[16,40,512]{2,1,0:T(8,128)(2,1)} %bitcast.26), calls=%async_computation.3 | async-start | bytes 1310720 | tf_op jit(solution)/shard_map/all_to_all | solution.py:220
  155.6 9.8 %all-gather.5.cloned.1.call-done = bf16[5120,128]{1,0:T(8,128)(2,1)} async-done(((bf16[640,128]{1,0:T(8,128)(2,1)}), bf16[5120,128]{1,0:T(8,128)(2,1)}) %all-gather.5.cloned.1.call-update) | async-done | bytes 1310736 | tf_op jit(solution)/shard_map/all_gather | solution.py:321
  165.4 3.4 %shard_map.124 = bf16[640,512]{1,0:T(8,128)(2,1)} custom-call(bf16[8,640,128]{2,1,0:T(8,128)(2,1)} %bitcast.57, bf16[1024,512]{1,0:T(8,128)(2,1)} %bitcast.42), custom_call_target="tpu_custom_call" | custom-call | flops 671088640 | bytes 3014656 | tf_op jit(solution)/shard_map/pallas_call | solution.py:26
  168.8 6.9 %all-to-all-done.2 = bf16[16,40,512]{2,1,0:T(8,128)(2,1)S(1)} async-done(((bf16[16,40,512]{2,1,0:T(8,128)(2,1)}), bf16[16,40,512]{2,1,0:T(8,128)(2,1)S(1)}, u32[]{:S(2)}, u32[]{:S(2)}) %all-to-all-start.2) | async-done | bytes 655392 | tf_op jit(solution)/shard_map/all_to_all | solution.py:220
  175.7 5.1 %all-to-all-start.3 = ((bf16[16,40,512]{2,1,0:T(8,128)(2,1)}), bf16[16,40,512]{2,1,0:T(8,128)(2,1)S(1)}, u32[]{:S(2)}, u32[]{:S(2)}) async-start(bf16[16,40,512]{2,1,0:T(8,128)(2,1)} %bitcast.56), calls=%async_computation.4 | async-start | bytes 1310720 | tf_op jit(solution)/shard_map/all_to_all | solution.py:220
  180.8 0.3 shard_map.126
  181.1 1.3 collective-permute-start.10
  182.4 5.7 %collective-permute-done.10 = bf16[1,128,512]{2,1,0:T(8,128)(2,1)S(1)} collective-permute-done((bf16[1,128,512]{2,1,0:T(8,128)(2,1)S(1)}, bf16[1,128,512]{2,1,0:T(8,128)(2,1)S(1)}, u32[]{:S(2)}, u32[]{:S(2)}) %collective-permute-start.10) | collective-permute-done | bytes 131104 | tf_op jit(solution)/shard_map/ppermute | solution.py:216
  188.0 12.8 %all-to-all-done.3 = bf16[16,40,512]{2,1,0:T(8,128)(2,1)S(1)} async-done(((bf16[16,40,512]{2,1,0:T(8,128)(2,1)}), bf16[16,40,512]{2,1,0:T(8,128)(2,1)S(1)}, u32[]{:S(2)}, u32[]{:S(2)}) %all-to-all-start.3) | async-done | bytes 655392 | tf_op jit(solution)/shard_map/all_to_all | solution.py:220
  200.8 1.0 shard_map.125
  201.8 0.7 copy.17
  (20 shorter events, 0.0 us)
Async XLA Ops:
  7.2 62.3 %all-gather.3.cloned.1.call-start = ((), (), s32[]{:S(2)}) async-start(), calls=%async_computation.5 | async-start | bytes 2949120 | tf_op jit(solution)/shard_map/all_gather | solution.py:285
  9.7 30.3 %all-to-all-start = ((bf16[16,40,512]{2,1,0:T(8,128)(2,1)}), bf16[16,40,512]{2,1,0:T(8,128)(2,1)S(1)}, u32[]{:S(2)}, u32[]{:S(2)}) async-start(bf16[16,40,512]{2,1,0:T(8,128)(2,1)} %bitcast.58), calls=%async_computation | async-start | bytes 1310720 | tf_op jit(solution)/shard_map/all_to_all | solution.py:220
  20.0 2.3 %copy-start.9 = (s32[1,128,4]{1,2,0:T(4,128)S(1)}, s32[1,128,4]{1,2,0:T(4,128)}, u32[]{:S(2)}) copy-start(s32[1,128,4]{1,2,0:T(4,128)} %param.12) | copy-start | bytes 6148
  20.0 2.3 %copy-start.10 = (f32[1,128,4]{1,2,0:T(4,128)S(1)}, f32[1,128,4]{1,2,0:T(4,128)}, u32[]{:S(2)}) copy-start(f32[1,128,4]{1,2,0:T(4,128)} %param.14) | copy-start | bytes 6148
  20.0 3.3 %copy-start.11 = (s32[1,128,4]{1,2,0:T(4,128)S(1)}, s32[1,128,4]{1,2,0:T(4,128)}, u32[]{:S(2)}) copy-start(s32[1,128,4]{1,2,0:T(4,128)} %param.13) | copy-start | bytes 6148
  20.0 3.3 %copy-start.12 = (f32[1,128,4]{1,2,0:T(4,128)S(1)}, f32[1,128,4]{1,2,0:T(4,128)}, u32[]{:S(2)}) copy-start(f32[1,128,4]{1,2,0:T(4,128)} %param.15) | copy-start | bytes 6148
  20.1 4.3 %copy-start.8 = (bf16[1,128,512]{2,1,0:T(8,128)(2,1)S(1)}, bf16[1,128,512]{2,1,0:T(8,128)(2,1)}, u32[]{:S(2)}) copy-start(bf16[1,128,512]{2,1,0:T(8,128)(2,1)} %param.10) | copy-start | bytes 393220
  22.3 21.3 %copy-start.13 = (s32[8]{0:T(128)S(1)}, s32[8]{0:T(128)}, u32[]{:S(2)}) copy-start(s32[8]{0:T(128)} %constant.41.clone) | copy-start | bytes 100
  22.6 0.7 copy-start.6
  23.6 0.7 copy-start.1
  40.1 3.6 %copy-start.4 = (bf16[16,40,512]{2,1,0:T(8,128)(2,1)}, bf16[16,40,512]{2,1,0:T(8,128)(2,1)S(1)}, u32[]{:S(2)}) copy-start(bf16[16,40,512]{2,1,0:T(8,128)(2,1)S(1)} %all-to-all-done) | copy-start | bytes 1966084
  40.1 23.1 %all-to-all-start.1 = ((bf16[16,40,512]{2,1,0:T(8,128)(2,1)}), bf16[16,40,512]{2,1,0:T(8,128)(2,1)S(1)}, u32[]{:S(2)}, u32[]{:S(2)}) async-start(bf16[16,40,512]{2,1,0:T(8,128)(2,1)} %bitcast.20), calls=%async_computation.1 | async-start | bytes 1310720 | tf_op jit(solution)/shard_map/all_to_all | solution.py:220
  43.6 81.9 %reduce-scatter.2.cloned.1.call-start = ((), (), s32[]{:S(2)}) async-start(), calls=%async_computation.6 | async-start | bytes 2949120 | tf_op jit(solution)/shard_map/reduce_scatter | solution.py:307
  43.6 1.2 copy-start.3
  44.9 1.1 copy-start.5
  48.1 21.3 %collective-permute-start = (bf16[2,640,128]{2,1,0:T(8,128)(2,1)}, bf16[2,640,128]{2,1,0:T(8,128)(2,1)}, u32[]{:S(2)}, u32[]{:S(2)}) collective-permute-start(bf16[2,640,128]{2,1,0:T(8,128)(2,1)} %get-tuple-element.31), channel_id=1, source_target_pairs={{0,4},{4,8},{8,12},{12,16},{16,20},{20,24},{24,28},{28,0},{32,36},... | collective-permute-start | bytes 983048 | tf_op jit(solution)/shard_map/ppermute | solution.py:210
  50.4 19.0 %collective-permute-start.1 = (bf16[2,640,128]{2,1,0:T(8,128)(2,1)}, bf16[2,640,128]{2,1,0:T(8,128)(2,1)}, u32[]{:S(2)}, u32[]{:S(2)}) collective-permute-start(bf16[2,640,128]{2,1,0:T(8,128)(2,1)} %get-tuple-element.32), channel_id=1, source_target_pairs={{0,28},{4,0},{8,4},{12,8},{16,12},{20,16},{24,20},{28,24},{32,60},... | collective-permute-start | bytes 983048 | tf_op jit(solution)/shard_map/ppermute | solution.py:210
  59.0 10.4 %collective-permute-start.2 = (bf16[640,128]{1,0:T(8,128)(2,1)}, bf16[640,128]{1,0:T(8,128)(2,1)S(1)}, u32[]{:S(2)}, u32[]{:S(2)}) collective-permute-start(bf16[640,128]{1,0:T(8,128)(2,1)} %get-tuple-element.33), channel_id=1, source_target_pairs={{0,24},{4,28},{8,0},{12,4},{16,8},{20,12},{24,16},{28,20},{32,40},... | collective-permute-start | bytes 491528 | tf_op jit(solution)/shard_map/ppermute | solution.py:210
  65.5 1.5 copy-start
  69.4 96.0 %all-gather.5.cloned.1.call-start = ((), (), s32[]{:S(2)}) async-start(), calls=%async_computation.7 | async-start | bytes 1474560 | tf_op jit(solution)/shard_map/all_gather | solution.py:321
  70.7 10.9 %collective-permute-start.3 = (bf16[640,128]{1,0:T(8,128)(2,1)S(1)}, bf16[640,128]{1,0:T(8,128)(2,1)S(1)}, u32[]{:S(2)}, u32[]{:S(2)}) collective-permute-start(bf16[640,128]{1,0:T(8,128)(2,1)S(1)} %get-tuple-element.40), channel_id=1, source_target_pairs={{0,8},{4,12},{8,16},{12,20},{16,24},{20,28},{24,0},{28,4},{32,40},... | collective-permute-start | bytes 491528 | tf_op jit(solution)/shard_map/ppermute | solution.py:210
  74.0 12.4 %collective-permute-start.4 = (bf16[640,128]{1,0:T(8,128)(2,1)S(1)}, bf16[640,128]{1,0:T(8,128)(2,1)S(1)}, u32[]{:S(2)}, u32[]{:S(2)}) collective-permute-start(bf16[640,128]{1,0:T(8,128)(2,1)S(1)} %get-tuple-element.41), channel_id=1, source_target_pairs={{0,24},{4,28},{8,0},{12,4},{16,8},{20,12},{24,16},{28,20},{32,56},... | collective-permute-start | bytes 491528 | tf_op jit(solution)/shard_map/ppermute | solution.py:210
  87.6 14.4 %collective-permute-start.5 = (bf16[640,128]{1,0:T(8,128)(2,1)S(1)}, bf16[640,128]{1,0:T(8,128)(2,1)S(1)}, u32[]{:S(2)}, u32[]{:S(2)}) collective-permute-start(bf16[640,128]{1,0:T(8,128)(2,1)S(1)} %shard_map.120.own_ref), channel_id=1, source_target_pairs={{0,8},{4,12},{8,16},{12,20},{16,24},{20,28},{24,0},{28,4},{32,40},... | collective-permute-start | bytes 491528 | tf_op jit(solution)/shard_map/ppermute | solution.py:210
  92.9 14.0 %collective-permute-start.6 = (bf16[640,128]{1,0:T(8,128)(2,1)S(1)}, bf16[640,128]{1,0:T(8,128)(2,1)S(1)}, u32[]{:S(2)}, u32[]{:S(2)}) collective-permute-start(bf16[640,128]{1,0:T(8,128)(2,1)S(1)} %shard_map.120.own_ref), channel_id=1, source_target_pairs={{0,24},{4,28},{8,0},{12,4},{16,8},{20,12},{24,16},{28,20},{32,56},... | collective-permute-start | bytes 491528 | tf_op jit(solution)/shard_map/ppermute | solution.py:210
  107.0 11.5 %collective-permute-start.7 = (bf16[640,128]{1,0:T(8,128)(2,1)S(1)}, bf16[640,128]{1,0:T(8,128)(2,1)S(1)}, u32[]{:S(2)}, u32[]{:S(2)}) collective-permute-start(bf16[640,128]{1,0:T(8,128)(2,1)S(1)} %get-tuple-element.44), channel_id=1, source_target_pairs={{0,8},{4,12},{8,16},{12,20},{16,24},{20,28},{24,0},{28,4},{32,56},... | collective-permute-start | bytes 491528 | tf_op jit(solution)/shard_map/ppermute | solution.py:210
  127.2 10.8 %collective-permute-start.8 = (bf16[2,640,128]{2,1,0:T(8,128)(2,1)S(1)}, bf16[2,640,128]{2,1,0:T(8,128)(2,1)S(1)}, u32[]{:S(2)}, u32[]{:S(2)}) collective-permute-start(bf16[2,640,128]{2,1,0:T(8,128)(2,1)S(1)} %get-tuple-element.46), channel_id=1, source_target_pairs={{0,4},{4,8},{8,12},{12,16},{16,20},{20,24},{24,28},{28,0},{32,36},... | collective-permute-start | bytes 983048 | tf_op jit(solution)/shard_map/ppermute | solution.py:210
  129.1 9.7 %collective-permute-start.9 = (bf16[2,640,128]{2,1,0:T(8,128)(2,1)S(1)}, bf16[2,640,128]{2,1,0:T(8,128)(2,1)S(1)}, u32[]{:S(2)}, u32[]{:S(2)}) collective-permute-start(bf16[2,640,128]{2,1,0:T(8,128)(2,1)S(1)} %get-tuple-element.47), channel_id=1, source_target_pairs={{0,28},{4,0},{8,4},{12,8},{16,12},{20,16},{24,20},{28,24},{32,60},... | collective-permute-start | bytes 983048 | tf_op jit(solution)/shard_map/ppermute | solution.py:210
  143.1 32.6 %all-to-all-start.2 = ((bf16[16,40,512]{2,1,0:T(8,128)(2,1)}), bf16[16,40,512]{2,1,0:T(8,128)(2,1)S(1)}, u32[]{:S(2)}, u32[]{:S(2)}) async-start(bf16[16,40,512]{2,1,0:T(8,128)(2,1)} %bitcast.26), calls=%async_computation.3 | async-start | bytes 1310720 | tf_op jit(solution)/shard_map/all_to_all | solution.py:220
  165.4 15.4 %copy-start.7 = (bf16[1,128,640]{2,1,0:T(8,128)(2,1)S(1)}, bf16[1,128,640]{2,1,0:T(8,128)(2,1)}, u32[]{:S(2)}) copy-start(bf16[1,128,640]{2,1,0:T(8,128)(2,1)} %copy-done.6) | copy-start | bytes 491524
  165.4 35.4 %copy-start.2 = (bf16[2,128,640]{2,1,0:T(8,128)(2,1)S(1)}, bf16[2,128,640]{2,1,0:T(8,128)(2,1)}, u32[]{:S(2)}) copy-start(bf16[2,128,640]{2,1,0:T(8,128)(2,1)} %copy-done.1) | copy-start | bytes 983044
  175.7 25.1 %all-to-all-start.3 = ((bf16[16,40,512]{2,1,0:T(8,128)(2,1)}), bf16[16,40,512]{2,1,0:T(8,128)(2,1)S(1)}, u32[]{:S(2)}, u32[]{:S(2)}) async-start(bf16[16,40,512]{2,1,0:T(8,128)(2,1)} %bitcast.56), calls=%async_computation.4 | async-start | bytes 1310720 | tf_op jit(solution)/shard_map/all_to_all | solution.py:220
  181.1 7.0 %collective-permute-start.10 = (bf16[1,128,512]{2,1,0:T(8,128)(2,1)S(1)}, bf16[1,128,512]{2,1,0:T(8,128)(2,1)S(1)}, u32[]{:S(2)}, u32[]{:S(2)}) collective-permute-start(bf16[1,128,512]{2,1,0:T(8,128)(2,1)S(1)} %bitcast.46), channel_id=1, source_target_pairs={{1,0},{2,1},{3,2},{5,4},{6,5},{7,6},{9,8},{10,9},{11,10},{13,12},{... | collective-permute-start | bytes 393224 | tf_op jit(solution)/shard_map/ppermute | solution.py:216
Sparse Core Ops, SparseCore 0:
  10.1 51.4 all-gather.2
  69.6 55.8 reduce-scatter.1
  127.5 37.8 all-gather.4

commit v7 on v5

--- a/solution.py
+++ b/solution.py
@@ -257,7 +257,7 @@
     def partials(kernel, block, x, w):
         kinds = [shape(lead + block) for lead in ((2,), (2,), (), (3,))]
         flops = 2 * width * locals_ * functools.reduce(lambda a, b: a * b, block)
-        return call(kernel, kinds, (place, x, w), flops=flops, scalars=True)
+        return call(kernel, kinds, (place, x, w), flops=flops, scalars=True, limit=VMEM_WHOLE)
 
     def relay_sum(own, ahead, behind, across):
         kind = shape(across.shape)

time: 209 us -> 208 us (level)
    all_to_all x4, starting transfers between devices: 30.8 us -> 26.8 us  [exchange(): return lax.all_to_all(value, axis, split_axis=0, concat_axis=0, tiled=True)]
    reduce_scatter x1, waiting for transfers between devices: 13.5 us -> 10.5 us  [body(): lax.psum_scatter(part_b.reshape(locals_, 2 * slots, units), 'local', scat...]
    all_gather x1, waiting for transfers between devices: 6.49 us -> 8.69 us  [body(): lax.all_gather(hidden, 'local', axis=0, tiled=True)]
    ppermute x10, waiting for transfers between devices: 28 us -> 30.1 us  [rotated(): return lax.ppermute(value, ('node', 'local'), pairs)]
where the time goes in v7:
time: 208 us; the launch traced here: 206 us
  waiting for transfers between devices  93.7 us (45%)
  starting transfers between devices  68.6 us (33%)
  Pallas kernels  22.8 us (11%)
  between operations  14.1 us (7%)
  local copies, waits for them, and re-layouts  6.66 us (3%)
    ppermute x10, starting transfers between devices, rotated(): return lax.ppermute(value, ('node', 'local'), pairs)  40.4 us
    all_to_all x4, waiting for transfers between devices, exchange(): return lax.all_to_all(value, axis, split_axis=0, concat_axis=0, tiled=True)  37.2 us
    ppermute x10, waiting for transfers between devices, rotated(): return lax.ppermute(value, ('node', 'local'), pairs)  30.1 us
    all_to_all x4, starting transfers between devices, exchange(): return lax.all_to_all(value, axis, split_axis=0, concat_axis=0, tiled=True)  26.8 us
    pallas_call x14, Pallas kernels, call(): pl.pallas_call(kernel, out_shape=outs, scratch_shapes=scratch, compiler_p...  22.8 us
    reduce_scatter x1, waiting for transfers between devices, body(): lax.psum_scatter(part_b.reshape(locals_, 2 * slots, units), 'local', scat...  10.5 us
    all_gather x1, waiting for transfers between devices, body(): lax.all_gather(hidden, 'local', axis=0, tiled=True)  8.69 us
    ppermute x1, waiting for transfers between devices, shifted(): lax.ppermute(value, axis, [(source, source + steps) for source in range(f...  7.02 us
  transfers between devices with their start and end apart: 18, of which 13 were waited for; matrix products, arithmetic and copies ran while one was open for 1% of the time, Pallas kernels for 8%

profile of v7, /device:TPU:1, one launch (start us, length us, event | category | flops | bytes accessed | tf_op | source)
XLA Modules:
  0.0 206.3 jit_solution(18125624709100498416)
XLA Ops:
  7.2 0.0 all-gather.3.cloned.1.call-start
  7.2 2.5 %shard_map.116 = (bf16[640,512]{1,0:T(8,128)(2,1)}, bf16[2,640,128]{2,1,0:T(8,128)(2,1)}) custom-call(s32[4,128]{1,0:T(4,128)} %bitcast.44, f32[4,128]{1,0:T(4,128)} %bitcast.46, bf16[128,512]{1,0:T(8,128)(2,1)} %bitcast.61, bf16[2,128,640]{2,1,0:T(8,128)(2,1)} %bitcast.59), custom_call_target="tpu_custom_call" | custom-call | flops 83886080 | bytes 1445888 | tf_op jit(solution)/shard_map/pallas_call | solution.py:26
  9.7 0.0 all-gather.3.cloned.1.call-update
  9.7 10.3 %all-to-all-start = ((bf16[16,40,512]{2,1,0:T(8,128)(2,1)}), bf16[16,40,512]{2,1,0:T(8,128)(2,1)S(1)}, u32[]{:S(2)}, u32[]{:S(2)}) async-start(bf16[16,40,512]{2,1,0:T(8,128)(2,1)} %bitcast.58), calls=%async_computation | async-start | bytes 1310720 | tf_op jit(solution)/shard_map/all_to_all | solution.py:220
  20.0 0.0 copy-start.6
  20.0 0.0 copy-start.7
  20.0 0.0 copy-start.8
  20.0 0.0 copy-start.4
  20.1 2.2 %copy.15 = bf16[1,1,512,2,1024]{4,2,3,1,0:T(8,128)(2,1)S(1)} copy(bf16[1,1,512,2,1024]{4,3,2,1,0:T(2,128)(2,1)} %param.16) | data formatting | bytes 4194304 | tf_op args[6]
  22.3 0.0 copy-start.13
  22.3 0.3 shard_map.114.table_ref
  22.6 0.6 copy-done.2
  23.3 0.3 shard_map.115.table_ref
  23.6 1.3 shard_map.113
  24.9 15.2 %all-to-all-done = bf16[16,40,512]{2,1,0:T(8,128)(2,1)S(1)} async-done(((bf16[16,40,512]{2,1,0:T(8,128)(2,1)}), bf16[16,40,512]{2,1,0:T(8,128)(2,1)S(1)}, u32[]{:S(2)}, u32[]{:S(2)}) %all-to-all-start) | async-done | bytes 655392 | tf_op jit(solution)/shard_map/all_to_all | solution.py:220
  40.0 0.8 copy-done.12
  40.9 3.5 %all-to-all-start.1 = ((bf16[16,40,512]{2,1,0:T(8,128)(2,1)}), bf16[16,40,512]{2,1,0:T(8,128)(2,1)S(1)}, u32[]{:S(2)}, u32[]{:S(2)}) async-start(bf16[16,40,512]{2,1,0:T(8,128)(2,1)} %bitcast.20), calls=%async_computation.1 | async-start | bytes 1310720 | tf_op jit(solution)/shard_map/all_to_all | solution.py:220
  44.4 0.0 reduce-scatter.2.cloned.1.call-start
  44.4 0.5 and_select_fusion.place_ref
  45.0 3.2 %shard_map.117 = (bf16[2,640,128]{2,1,0:T(8,128)(2,1)}, bf16[2,640,128]{2,1,0:T(8,128)(2,1)}, bf16[640,128]{1,0:T(8,128)(2,1)}, bf16[3,640,128]{2,1,0:T(8,128)(2,1)}) custom-call(s32[8]{0:T(128)} %and_select_fusion.place_ref, bf16[640,512]{1,0:T(8,128)(2,1)} %bitcast.57, bf16[1024,512]{1,0:T(8,128)(2,1)} %bitcast.55), custom_call_target="tpu_custom_call" | custom-call | flops 671088640 | bytes 3014688 | tf_op jit(solution)/shard_map/pallas_call | solution.py:26
  48.1 2.3 %collective-permute-start = (bf16[2,640,128]{2,1,0:T(8,128)(2,1)}, bf16[2,640,128]{2,1,0:T(8,128)(2,1)S(1)}, u32[]{:S(2)}, u32[]{:S(2)}) collective-permute-start(bf16[2,640,128]{2,1,0:T(8,128)(2,1)} %get-tuple-element.31), channel_id=1, source_target_pairs={{0,4},{4,8},{8,12},{12,16},{16,20},{20,24},{24,28},{28,0},{32,36},... | collective-permute-start | bytes 983048 | tf_op jit(solution)/shard_map/ppermute | solution.py:210
  50.5 8.6 %collective-permute-start.1 = (bf16[2,640,128]{2,1,0:T(8,128)(2,1)}, bf16[2,640,128]{2,1,0:T(8,128)(2,1)}, u32[]{:S(2)}, u32[]{:S(2)}) collective-permute-start(bf16[2,640,128]{2,1,0:T(8,128)(2,1)} %get-tuple-element.32), channel_id=1, source_target_pairs={{0,28},{4,0},{8,4},{12,8},{16,12},{20,16},{24,20},{28,24},{32,60},... | collective-permute-start | bytes 983048 | tf_op jit(solution)/shard_map/ppermute | solution.py:210
  59.1 1.9 collective-permute-start.2
  61.0 2.9 %all-to-all-done.1 = bf16[16,40,512]{2,1,0:T(8,128)(2,1)S(1)} async-done(((bf16[16,40,512]{2,1,0:T(8,128)(2,1)}), bf16[16,40,512]{2,1,0:T(8,128)(2,1)S(1)}, u32[]{:S(2)}, u32[]{:S(2)}) %all-to-all-start.1) | async-done | bytes 655392 | tf_op jit(solution)/shard_map/all_to_all | solution.py:220
  63.9 2.4 %shard_map.118 = bf16[8,2,640,128]{3,2,1,0:T(8,128)(2,1)S(1)} custom-call(bf16[640,512]{1,0:T(8,128)(2,1)S(1)} %bitcast.41, bf16[2,512,1024]{2,1,0:T(8,128)(2,1)S(1)} %bitcast.36), custom_call_target="tpu_custom_call" | custom-call | flops 1342177280 | bytes 5373952 | tf_op jit(solution)/shard_map/pallas_call | solution.py:26
  66.3 1.5 copy-done
  67.8 1.7 collective-permute-done.2.across_ref
  69.5 0.0 collective-permute-done.ahead_ref.refs_1_
  69.5 0.0 collective-permute-done.1.behind_ref.refs_2_
  69.5 0.0 all-gather.3.cloned.1.call-done
  69.6 0.0 reduce-scatter.2.cloned.1.call-update
  69.6 0.0 copy-start.9
  69.6 0.0 all-gather.5.cloned.1.call-start
  69.7 1.2 shard_map.119
  70.8 3.3 %collective-permute-start.3 = (bf16[640,128]{1,0:T(8,128)(2,1)S(1)}, bf16[640,128]{1,0:T(8,128)(2,1)S(1)}, u32[]{:S(2)}, u32[]{:S(2)}) collective-permute-start(bf16[640,128]{1,0:T(8,128)(2,1)S(1)} %get-tuple-element.40), channel_id=1, source_target_pairs={{0,8},{4,12},{8,16},{12,20},{16,24},{20,28},{24,0},{28,4},{32,40},... | collective-permute-start | bytes 491528 | tf_op jit(solution)/shard_map/ppermute | solution.py:210
  74.1 6.8 %collective-permute-start.4 = (bf16[640,128]{1,0:T(8,128)(2,1)S(1)}, bf16[640,128]{1,0:T(8,128)(2,1)S(1)}, u32[]{:S(2)}, u32[]{:S(2)}) collective-permute-start(bf16[640,128]{1,0:T(8,128)(2,1)S(1)} %get-tuple-element.41), channel_id=1, source_target_pairs={{0,24},{4,28},{8,0},{12,4},{16,8},{20,12},{24,16},{28,20},{32,56},... | collective-permute-start | bytes 491528 | tf_op jit(solution)/shard_map/ppermute | solution.py:210
  80.9 6.3 %collective-permute-done.3.refs_3_ = bf16[640,128]{1,0:T(8,128)(2,1)S(1)} collective-permute-done((bf16[640,128]{1,0:T(8,128)(2,1)S(1)}, bf16[640,128]{1,0:T(8,128)(2,1)S(1)}, u32[]{:S(2)}, u32[]{:S(2)}) %collective-permute-start.3) | collective-permute-done | bytes 163872 | tf_op jit(solution)/shard_map/ppermute | solution.py:210
  87.2 3.5 %collective-permute-done.4.refs_4_ = bf16[640,128]{1,0:T(8,128)(2,1)S(1)} collective-permute-done((bf16[640,128]{1,0:T(8,128)(2,1)S(1)}, bf16[640,128]{1,0:T(8,128)(2,1)S(1)}, u32[]{:S(2)}, u32[]{:S(2)}) %collective-permute-start.4) | collective-permute-done | bytes 163872 | tf_op jit(solution)/shard_map/ppermute | solution.py:210
  90.7 1.1 shard_map.120.own_ref
  91.8 5.3 %collective-permute-start.5 = (bf16[640,128]{1,0:T(8,128)(2,1)S(1)}, bf16[640,128]{1,0:T(8,128)(2,1)S(1)}, u32[]{:S(2)}, u32[]{:S(2)}) collective-permute-start(bf16[640,128]{1,0:T(8,128)(2,1)S(1)} %shard_map.120.own_ref), channel_id=1, source_target_pairs={{0,8},{4,12},{8,16},{12,20},{16,24},{20,28},{24,0},{28,4},{32,40},... | collective-permute-start | bytes 491528 | tf_op jit(solution)/shard_map/ppermute | solution.py:210
  97.2 2.8 %collective-permute-start.6 = (bf16[640,128]{1,0:T(8,128)(2,1)S(1)}, bf16[640,128]{1,0:T(8,128)(2,1)S(1)}, u32[]{:S(2)}, u32[]{:S(2)}) collective-permute-start(bf16[640,128]{1,0:T(8,128)(2,1)S(1)} %shard_map.120.own_ref), channel_id=1, source_target_pairs={{0,24},{4,28},{8,0},{12,4},{16,8},{20,12},{24,16},{28,20},{32,56},... | collective-permute-start | bytes 491528 | tf_op jit(solution)/shard_map/ppermute | solution.py:210
  100.0 8.4 %collective-permute-done.5.low_ref = bf16[640,128]{1,0:T(8,128)(2,1)S(1)} collective-permute-done((bf16[640,128]{1,0:T(8,128)(2,1)S(1)}, bf16[640,128]{1,0:T(8,128)(2,1)S(1)}, u32[]{:S(2)}, u32[]{:S(2)}) %collective-permute-start.5) | collective-permute-done | bytes 163872 | tf_op jit(solution)/shard_map/ppermute | solution.py:210
  108.4 3.0 %collective-permute-done.6.high_ref = bf16[640,128]{1,0:T(8,128)(2,1)S(1)} collective-permute-done((bf16[640,128]{1,0:T(8,128)(2,1)S(1)}, bf16[640,128]{1,0:T(8,128)(2,1)S(1)}, u32[]{:S(2)}, u32[]{:S(2)}) %collective-permute-start.6) | collective-permute-done | bytes 163872 | tf_op jit(solution)/shard_map/ppermute | solution.py:210
  111.3 0.1 shard_map.121
  111.5 0.7 copy-done.10
  112.2 10.5 %reduce-scatter.2.cloned.1.call-done = bf16[1,1280,128]{2,1,0:T(8,128)(2,1)} async-done(((bf16[8,1280,128]{2,1,0:T(8,128)(2,1)}), bf16[1,1280,128]{2,1,0:T(8,128)(2,1)}) %reduce-scatter.2.cloned.1.call-update) | async-done | bytes 327696 | tf_op jit(solution)/shard_map/reduce_scatter | solution.py:307
  122.7 1.7 shard_map.123
  124.5 0.0 all-gather.5.cloned.1.call-update
  124.5 3.1 %collective-permute-start.7 = (bf16[2,640,128]{2,1,0:T(8,128)(2,1)}, bf16[2,640,128]{2,1,0:T(8,128)(2,1)S(1)}, u32[]{:S(2)}, u32[]{:S(2)}) collective-permute-start(bf16[2,640,128]{2,1,0:T(8,128)(2,1)} %copy-done.10), channel_id=1, source_target_pairs={{0,4},{4,8},{8,12},{12,16},{16,20},{20,24},{24,28},{28,0},{32,36},... | collective-permute-start | bytes 983048 | tf_op jit(solution)/shard_map/ppermute | solution.py:210
  127.6 3.4 %collective-permute-start.8 = (bf16[2,640,128]{2,1,0:T(8,128)(2,1)S(1)}, bf16[2,640,128]{2,1,0:T(8,128)(2,1)S(1)}, u32[]{:S(2)}, u32[]{:S(2)}) collective-permute-start(bf16[2,640,128]{2,1,0:T(8,128)(2,1)S(1)} %get-tuple-element.47), channel_id=1, source_target_pairs={{0,28},{4,0},{8,4},{12,8},{16,12},{20,16},{24,20},{28,24},{32,60},... | collective-permute-start | bytes 983048 | tf_op jit(solution)/shard_map/ppermute | solution.py:210
  131.0 2.8 %collective-permute-start.9 = (bf16[640,128]{1,0:T(8,128)(2,1)}, bf16[640,128]{1,0:T(8,128)(2,1)S(1)}, u32[]{:S(2)}, u32[]{:S(2)}) collective-permute-start(bf16[640,128]{1,0:T(8,128)(2,1)} %copy-done.11), channel_id=1, source_target_pairs={{0,8},{4,12},{8,16},{12,20},{16,24},{20,28},{24,0},{28,4},{32,56},... | collective-permute-start | bytes 491528 | tf_op jit(solution)/shard_map/ppermute | solution.py:210
  133.8 7.2 %collective-permute-done.9.across_ref = bf16[640,128]{1,0:T(8,128)(2,1)S(1)} collective-permute-done((bf16[640,128]{1,0:T(8,128)(2,1)}, bf16[640,128]{1,0:T(8,128)(2,1)S(1)}, u32[]{:S(2)}, u32[]{:S(2)}) %collective-permute-start.9) | collective-permute-done | bytes 163872 | tf_op jit(solution)/shard_map/ppermute | solution.py:210
  141.0 4.2 %shard_map.122 = bf16[640,512]{1,0:T(8,128)(2,1)} custom-call(s32[8]{0:T(128)S(1)} %copy-done.9, bf16[640,128]{1,0:T(8,128)(2,1)S(1)} %shard_map.120.own_ref, bf16[640,128]{1,0:T(8,128)(2,1)S(1)} %collective-permute-done.5.low_ref, bf16[640,128]{1,0:T(8,128)(2,1)S(1)} %collective-permute-done.6.high_ref, ...), custom_call_target="tpu_custom_call" | custom-call | flops 1342177280 | bytes 6684704 | tf_op jit(solution)/shard_map/pallas_call | solution.py:26
  145.2 9.6 %all-to-all-start.2 = ((bf16[16,40,512]{2,1,0:T(8,128)(2,1)}), bf16[16,40,512]{2,1,0:T(8,128)(2,1)S(1)}, u32[]{:S(2)}, u32[]{:S(2)}) async-start(bf16[16,40,512]{2,1,0:T(8,128)(2,1)} %bitcast.26), calls=%async_computation.3 | async-start | bytes 1310720 | tf_op jit(solution)/shard_map/all_to_all | solution.py:220
  154.8 8.7 %all-gather.5.cloned.1.call-done = bf16[5120,128]{1,0:T(8,128)(2,1)} async-done(((bf16[640,128]{1,0:T(8,128)(2,1)}), bf16[5120,128]{1,0:T(8,128)(2,1)}) %all-gather.5.cloned.1.call-update) | async-done | bytes 1310736 | tf_op jit(solution)/shard_map/all_gather | solution.py:321
  163.5 3.3 %shard_map.124 = bf16[640,512]{1,0:T(8,128)(2,1)} custom-call(bf16[8,640,128]{2,1,0:T(8,128)(2,1)} %bitcast.54, bf16[1024,512]{1,0:T(8,128)(2,1)} %bitcast.56), custom_call_target="tpu_custom_call" | custom-call | flops 671088640 | bytes 3014656 | tf_op jit(solution)/shard_map/pallas_call | solution.py:26
  166.8 8.0 %all-to-all-done.2 = bf16[16,40,512]{2,1,0:T(8,128)(2,1)S(1)} async-done(((bf16[16,40,512]{2,1,0:T(8,128)(2,1)}), bf16[16,40,512]{2,1,0:T(8,128)(2,1)S(1)}, u32[]{:S(2)}, u32[]{:S(2)}) %all-to-all-start.2) | async-done | bytes 655392 | tf_op jit(solution)/shard_map/all_to_all | solution.py:220
  174.8 3.5 %all-to-all-start.3 = ((bf16[16,40,512]{2,1,0:T(8,128)(2,1)}), bf16[16,40,512]{2,1,0:T(8,128)(2,1)S(1)}, u32[]{:S(2)}, u32[]{:S(2)}) async-start(bf16[16,40,512]{2,1,0:T(8,128)(2,1)} %bitcast.53), calls=%async_computation.4 | async-start | bytes 1310720 | tf_op jit(solution)/shard_map/all_to_all | solution.py:220
  178.3 0.3 shard_map.126
  178.6 1.3 collective-permute-start.10
  179.9 7.0 %collective-permute-done.10 = bf16[1,128,512]{2,1,0:T(8,128)(2,1)S(1)} collective-permute-done((bf16[1,128,512]{2,1,0:T(8,128)(2,1)S(1)}, bf16[1,128,512]{2,1,0:T(8,128)(2,1)S(1)}, u32[]{:S(2)}, u32[]{:S(2)}) %collective-permute-start.10) | collective-permute-done | bytes 131104 | tf_op jit(solution)/shard_map/ppermute | solution.py:216
  186.9 11.2 %all-to-all-done.3 = bf16[16,40,512]{2,1,0:T(8,128)(2,1)S(1)} async-done(((bf16[16,40,512]{2,1,0:T(8,128)(2,1)}), bf16[16,40,512]{2,1,0:T(8,128)(2,1)S(1)}, u32[]{:S(2)}, u32[]{:S(2)}) %all-to-all-start.3) | async-done | bytes 655392 | tf_op jit(solution)/shard_map/all_to_all | solution.py:220
  198.1 1.0 shard_map.125
  199.1 0.7 copy.17
  (20 shorter events, 0.0 us)
Async XLA Ops:
  7.2 62.4 %all-gather.3.cloned.1.call-start = ((), (), s32[]{:S(2)}) async-start(), calls=%async_computation.5 | async-start | bytes 2949120 | tf_op jit(solution)/shard_map/all_gather | solution.py:285
  9.7 30.3 %all-to-all-start = ((bf16[16,40,512]{2,1,0:T(8,128)(2,1)}), bf16[16,40,512]{2,1,0:T(8,128)(2,1)S(1)}, u32[]{:S(2)}, u32[]{:S(2)}) async-start(bf16[16,40,512]{2,1,0:T(8,128)(2,1)} %bitcast.58), calls=%async_computation | async-start | bytes 1310720 | tf_op jit(solution)/shard_map/all_to_all | solution.py:220
  20.0 2.3 %copy-start.5 = (s32[1,128,4]{1,2,0:T(4,128)S(1)}, s32[1,128,4]{1,2,0:T(4,128)}, u32[]{:S(2)}) copy-start(s32[1,128,4]{1,2,0:T(4,128)} %param.12) | copy-start | bytes 6148
  20.0 2.3 %copy-start.6 = (f32[1,128,4]{1,2,0:T(4,128)S(1)}, f32[1,128,4]{1,2,0:T(4,128)}, u32[]{:S(2)}) copy-start(f32[1,128,4]{1,2,0:T(4,128)} %param.14) | copy-start | bytes 6148
  20.0 3.2 %copy-start.7 = (s32[1,128,4]{1,2,0:T(4,128)S(1)}, s32[1,128,4]{1,2,0:T(4,128)}, u32[]{:S(2)}) copy-start(s32[1,128,4]{1,2,0:T(4,128)} %param.13) | copy-start | bytes 6148
  20.0 3.2 %copy-start.8 = (f32[1,128,4]{1,2,0:T(4,128)S(1)}, f32[1,128,4]{1,2,0:T(4,128)}, u32[]{:S(2)}) copy-start(f32[1,128,4]{1,2,0:T(4,128)} %param.15) | copy-start | bytes 6148
  20.0 3.5 %copy-start.4 = (bf16[1,128,512]{2,1,0:T(8,128)(2,1)S(1)}, bf16[1,128,512]{2,1,0:T(8,128)(2,1)}, u32[]{:S(2)}) copy-start(bf16[1,128,512]{2,1,0:T(8,128)(2,1)} %param.10) | copy-start | bytes 393220
  22.3 22.1 %copy-start.13 = (s32[8]{0:T(128)S(1)}, s32[8]{0:T(128)}, u32[]{:S(2)}) copy-start(s32[8]{0:T(128)} %constant.41.clone) | copy-start | bytes 100
  22.6 0.7 copy-start.2
  40.0 0.8 copy-start.12
  40.9 23.1 %all-to-all-start.1 = ((bf16[16,40,512]{2,1,0:T(8,128)(2,1)}), bf16[16,40,512]{2,1,0:T(8,128)(2,1)S(1)}, u32[]{:S(2)}, u32[]{:S(2)}) async-start(bf16[16,40,512]{2,1,0:T(8,128)(2,1)} %bitcast.20), calls=%async_computation.1 | async-start | bytes 1310720 | tf_op jit(solution)/shard_map/all_to_all | solution.py:220
  44.4 78.3 %reduce-scatter.2.cloned.1.call-start = ((), (), s32[]{:S(2)}) async-start(), calls=%async_computation.6 | async-start | bytes 2949120 | tf_op jit(solution)/shard_map/reduce_scatter | solution.py:307
  48.1 21.4 %collective-permute-start = (bf16[2,640,128]{2,1,0:T(8,128)(2,1)}, bf16[2,640,128]{2,1,0:T(8,128)(2,1)S(1)}, u32[]{:S(2)}, u32[]{:S(2)}) collective-permute-start(bf16[2,640,128]{2,1,0:T(8,128)(2,1)} %get-tuple-element.31), channel_id=1, source_target_pairs={{0,4},{4,8},{8,12},{12,16},{16,20},{20,24},{24,28},{28,0},{32,36},... | collective-permute-start | bytes 983048 | tf_op jit(solution)/shard_map/ppermute | solution.py:210
  50.5 19.1 %collective-permute-start.1 = (bf16[2,640,128]{2,1,0:T(8,128)(2,1)}, bf16[2,640,128]{2,1,0:T(8,128)(2,1)}, u32[]{:S(2)}, u32[]{:S(2)}) collective-permute-start(bf16[2,640,128]{2,1,0:T(8,128)(2,1)} %get-tuple-element.32), channel_id=1, source_target_pairs={{0,28},{4,0},{8,4},{12,8},{16,12},{20,16},{24,20},{28,24},{32,60},... | collective-permute-start | bytes 983048 | tf_op jit(solution)/shard_map/ppermute | solution.py:210
  59.1 10.4 %collective-permute-start.2 = (bf16[640,128]{1,0:T(8,128)(2,1)}, bf16[640,128]{1,0:T(8,128)(2,1)}, u32[]{:S(2)}, u32[]{:S(2)}) collective-permute-start(bf16[640,128]{1,0:T(8,128)(2,1)} %get-tuple-element.33), channel_id=1, source_target_pairs={{0,24},{4,28},{8,0},{12,4},{16,8},{20,12},{24,16},{28,20},{32,40},... | collective-permute-start | bytes 491528 | tf_op jit(solution)/shard_map/ppermute | solution.py:210
  66.3 1.5 copy-start
  67.8 1.8 copy-start.1
  69.6 71.4 %copy-start.9 = (s32[8]{0:T(128)S(1)}, s32[8]{0:T(128)}, u32[]{:S(2)}) copy-start(s32[8]{0:T(128)} %and_select_fusion.place_ref) | copy-start | bytes 100
  69.6 93.9 %all-gather.5.cloned.1.call-start = ((), (), s32[]{:S(2)}) async-start(), calls=%async_computation.7 | async-start | bytes 1474560 | tf_op jit(solution)/shard_map/all_gather | solution.py:321
  70.8 16.4 %collective-permute-start.3 = (bf16[640,128]{1,0:T(8,128)(2,1)S(1)}, bf16[640,128]{1,0:T(8,128)(2,1)S(1)}, u32[]{:S(2)}, u32[]{:S(2)}) collective-permute-start(bf16[640,128]{1,0:T(8,128)(2,1)S(1)} %get-tuple-element.40), channel_id=1, source_target_pairs={{0,8},{4,12},{8,16},{12,20},{16,24},{20,28},{24,0},{28,4},{32,40},... | collective-permute-start | bytes 491528 | tf_op jit(solution)/shard_map/ppermute | solution.py:210
  74.1 16.6 %collective-permute-start.4 = (bf16[640,128]{1,0:T(8,128)(2,1)S(1)}, bf16[640,128]{1,0:T(8,128)(2,1)S(1)}, u32[]{:S(2)}, u32[]{:S(2)}) collective-permute-start(bf16[640,128]{1,0:T(8,128)(2,1)S(1)} %get-tuple-element.41), channel_id=1, source_target_pairs={{0,24},{4,28},{8,0},{12,4},{16,8},{20,12},{24,16},{28,20},{32,56},... | collective-permute-start | bytes 491528 | tf_op jit(solution)/shard_map/ppermute | solution.py:210
  91.8 16.5 %collective-permute-start.5 = (bf16[640,128]{1,0:T(8,128)(2,1)S(1)}, bf16[640,128]{1,0:T(8,128)(2,1)S(1)}, u32[]{:S(2)}, u32[]{:S(2)}) collective-permute-start(bf16[640,128]{1,0:T(8,128)(2,1)S(1)} %shard_map.120.own_ref), channel_id=1, source_target_pairs={{0,8},{4,12},{8,16},{12,20},{16,24},{20,28},{24,0},{28,4},{32,40},... | collective-permute-start | bytes 491528 | tf_op jit(solution)/shard_map/ppermute | solution.py:210
  97.2 14.2 %collective-permute-start.6 = (bf16[640,128]{1,0:T(8,128)(2,1)S(1)}, bf16[640,128]{1,0:T(8,128)(2,1)S(1)}, u32[]{:S(2)}, u32[]{:S(2)}) collective-permute-start(bf16[640,128]{1,0:T(8,128)(2,1)S(1)} %shard_map.120.own_ref), channel_id=1, source_target_pairs={{0,24},{4,28},{8,0},{12,4},{16,8},{20,12},{24,16},{28,20},{32,56},... | collective-permute-start | bytes 491528 | tf_op jit(solution)/shard_map/ppermute | solution.py:210
  111.5 0.7 copy-start.10
  112.2 15.4 %copy-start.11 = (bf16[640,128]{1,0:T(8,128)(2,1)}, bf16[640,128]{1,0:T(8,128)(2,1)S(1)}, u32[]{:S(2)}) copy-start(bf16[640,128]{1,0:T(8,128)(2,1)S(1)} %get-tuple-element.48) | copy-start | bytes 491524
  124.5 16.5 %collective-permute-start.7 = (bf16[2,640,128]{2,1,0:T(8,128)(2,1)}, bf16[2,640,128]{2,1,0:T(8,128)(2,1)S(1)}, u32[]{:S(2)}, u32[]{:S(2)}) collective-permute-start(bf16[2,640,128]{2,1,0:T(8,128)(2,1)} %copy-done.10), channel_id=1, source_target_pairs={{0,4},{4,8},{8,12},{12,16},{16,20},{20,24},{24,28},{28,0},{32,36},... | collective-permute-start | bytes 983048 | tf_op jit(solution)/shard_map/ppermute | solution.py:210
  127.6 13.5 %collective-permute-start.8 = (bf16[2,640,128]{2,1,0:T(8,128)(2,1)S(1)}, bf16[2,640,128]{2,1,0:T(8,128)(2,1)S(1)}, u32[]{:S(2)}, u32[]{:S(2)}) collective-permute-start(bf16[2,640,128]{2,1,0:T(8,128)(2,1)S(1)} %get-tuple-element.47), channel_id=1, source_target_pairs={{0,28},{4,0},{8,4},{12,8},{16,12},{20,16},{24,20},{28,24},{32,60},... | collective-permute-start | bytes 983048 | tf_op jit(solution)/shard_map/ppermute | solution.py:210
  131.0 10.0 %collective-permute-start.9 = (bf16[640,128]{1,0:T(8,128)(2,1)}, bf16[640,128]{1,0:T(8,128)(2,1)S(1)}, u32[]{:S(2)}, u32[]{:S(2)}) collective-permute-start(bf16[640,128]{1,0:T(8,128)(2,1)} %copy-done.11), channel_id=1, source_target_pairs={{0,8},{4,12},{8,16},{12,20},{16,24},{20,28},{24,0},{28,4},{32,56},... | collective-permute-start | bytes 491528 | tf_op jit(solution)/shard_map/ppermute | solution.py:210
  145.2 29.6 %all-to-all-start.2 = ((bf16[16,40,512]{2,1,0:T(8,128)(2,1)}), bf16[16,40,512]{2,1,0:T(8,128)(2,1)S(1)}, u32[]{:S(2)}, u32[]{:S(2)}) async-start(bf16[16,40,512]{2,1,0:T(8,128)(2,1)} %bitcast.26), calls=%async_computation.3 | async-start | bytes 1310720 | tf_op jit(solution)/shard_map/all_to_all | solution.py:220
  163.5 14.8 %copy-start.3 = (bf16[1,128,640]{2,1,0:T(8,128)(2,1)S(1)}, bf16[1,128,640]{2,1,0:T(8,128)(2,1)}, u32[]{:S(2)}) copy-start(bf16[1,128,640]{2,1,0:T(8,128)(2,1)} %copy-done.2) | copy-start | bytes 491524
  174.8 23.3 %all-to-all-start.3 = ((bf16[16,40,512]{2,1,0:T(8,128)(2,1)}), bf16[16,40,512]{2,1,0:T(8,128)(2,1)S(1)}, u32[]{:S(2)}, u32[]{:S(2)}) async-start(bf16[16,40,512]{2,1,0:T(8,128)(2,1)} %bitcast.53), calls=%async_computation.4 | async-start | bytes 1310720 | tf_op jit(solution)/shard_map/all_to_all | solution.py:220
  178.6 8.3 %collective-permute-start.10 = (bf16[1,128,512]{2,1,0:T(8,128)(2,1)S(1)}, bf16[1,128,512]{2,1,0:T(8,128)(2,1)S(1)}, u32[]{:S(2)}, u32[]{:S(2)}) collective-permute-start(bf16[1,128,512]{2,1,0:T(8,128)(2,1)S(1)} %bitcast.43), channel_id=1, source_target_pairs={{1,0},{2,1},{3,2},{5,4},{6,5},{7,6},{9,8},{10,9},{11,10},{13,12},{... | collective-permute-start | bytes 393224 | tf_op jit(solution)/shard_map/ppermute | solution.py:216
Sparse Core Ops, SparseCore 0:
  10.1 51.3 all-gather.2
  69.7 52.9 reduce-scatter.1
  124.8 38.6 all-gather.4
